TPU v7x, 32 devices: a whole 2x2x4 slice. The times are simulated.
32 devices in a mesh: dp: 4 (over y, x), heads: 4 (over z), side: 2 (over core).
Axes of the slice: x: 2, y: 2, z: 4, core: 2. Of those that a mesh axis runs over, the one named last changes fastest.
Arguments:
- queries: bfloat16 [96, 2, 4096], P('dp', None, ('heads', 'side')), may hold values from -6 to 6
- new_keys: bfloat16 [96, 2, 4096], P('dp', None, ('heads', 'side')), may hold values from -6 to 6
- new_values: bfloat16 [96, 2, 4096], P('dp', None, ('heads', 'side')), may hold values from -6 to 6
- head_states: bfloat16 [96, 32, 128, 128], P('dp', ('heads', 'side')), may hold values from -6 to 6
- slopes: float32 [32], P(('heads', 'side')), may hold values from 0.004 to 0.9
- head_gain: float32 [4096], P(('heads', 'side')), may hold values from 0.5 to 1.5
- out_weight: bfloat16 [4096, 3072], P(('heads', 'side')), may hold values from -0.125 to 0.125
- residual: bfloat16 [96, 2, 3072], P('dp', None, ('heads', 'side')), may hold values from -10 to 10
- norm_gain: float32 [3072], replicated, may hold values from 0.5 to 1.5
- expert_ids: int32 [96, 2, 2], P('dp'), may hold values from 0 to 3, all different within a row; in each aligned block of 48 rows (0 to 47, 48 to 95, ..., all dimensions but the last counted through in order) at most 36 rows name the same one
- expert_gates: float32 [96, 2, 2], P('dp'), may hold values from 0.2 to 1
- w_gate: bfloat16 [4, 4, 768, 4608], P('dp', None, 'side', 'heads'), may hold values from -0.109375 to 0.109375
- w_up: bfloat16 [4, 4, 768, 4608], P('dp', None, 'side', 'heads'), may hold values from -0.109375 to 0.109375
- w_down: bfloat16 [4, 4608, 4, 768], P('dp', 'heads', None, 'side'), may hold values from -0.125 to 0.125
Outputs:
- state_out: bfloat16 [96, 32, 128, 128], P('dp', ('heads', 'side'))
- resid_out: bfloat16 [96, 2, 3072], P('dp', None, ('heads', 'side'))
- moe_out: bfloat16 [96, 2, 3072], P('dp', None, ('heads', 'side'))
Inputs may be any that keep to these rules, and one draw needn't show every extreme that they name: `expert_ids`: among the 48 tokens of one dp index a token's 2 experts differ, no expert is chosen by more than 36 of them, and some expert is chosen by exactly 36.
All inputs are finite; a program needn't handle non-finite values.
Results may differ from a plain program's by a relative error of at most 0.025.
Values may be sent and summed in bfloat16 or wider, within the bound.
No kernel may reach another device: no remote copies, remote signals or barrier semaphores. Data moves between devices by JAX's collectives and lax.ppermute only.
A program may use at most 64 MiB of HBM per device.

v0:
```python
import jax
import jax.numpy as jnp
from jax import lax
from jax.sharding import PartitionSpec as P


def local(
    queries,
    new_keys,
    new_values,
    head_states,
    slopes,
    head_gain,
    out_weight,
    residual,
    norm_gain,
    expert_ids,
    expert_gates,
    w_gate,
    w_up,
    w_down,
):
    requests_dev, step_count, inner_width = queries.shape
    local_heads = slopes.shape[0]
    head_size = inner_width // local_heads
    query_rows = queries.astype(jnp.float32).reshape(
        requests_dev, step_count, local_heads, head_size
    )
    key_rows = new_keys.astype(jnp.float32).reshape(
        requests_dev, step_count, local_heads, head_size
    )
    value_rows = new_values.astype(jnp.float32).reshape(
        requests_dev, step_count, local_heads, head_size
    )
    decays = jnp.exp(-slopes)[None, :, None, None]
    current = head_states.astype(jnp.float32)
    outputs = []
    for step in range(step_count):
        current = decays * current + key_rows[:, step, :, :, None] * value_rows[:, step, :, None, :]
        outputs.append(
            jnp.einsum(
                "rhi,rhij->rhj", query_rows[:, step], current, precision=lax.Precision.HIGHEST
            )
        )
    state_out = current.astype(jnp.bfloat16)
    head_output = jnp.stack(outputs, 1)
    scaled = head_output * lax.rsqrt(jnp.mean(head_output * head_output, -1, keepdims=True) + 1e-06)
    tokens_dev = requests_dev * step_count
    normed = (
        (scaled * head_gain.reshape(local_heads, head_size))
        .astype(jnp.bfloat16)
        .reshape(tokens_dev, inner_width)
    )
    partial_out = jnp.dot(normed, out_weight, preferred_element_type=jnp.float32)
    attention = lax.psum_scatter(partial_out, ("heads", "side"), scatter_dimension=1, tiled=True)
    width = norm_gain.shape[0]
    piece_width = attention.shape[1]
    resid_new = (residual.reshape(tokens_dev, piece_width).astype(jnp.float32) + attention).astype(
        jnp.bfloat16
    )
    stream = resid_new.astype(jnp.float32)
    sum_squares = lax.psum(jnp.sum(stream * stream, 1), ("heads", "side"))
    gain_piece = lax.dynamic_slice_in_dim(
        norm_gain, lax.axis_index(("heads", "side")) * piece_width, piece_width
    )
    mixed_in = (stream * lax.rsqrt(sum_squares / width + 1e-06)[:, None] * gain_piece).astype(
        jnp.bfloat16
    )
    groups = lax.axis_size("dp")
    heads_count = lax.axis_size("heads")
    choices_each = expert_ids.shape[2]
    capacity = max(2, 3 * choices_each * tokens_dev // (2 * groups))
    flat_ids = expert_ids.reshape(-1)
    onehot_table = (flat_ids[:, None] == jnp.arange(groups, dtype=jnp.int32)[None, :]).astype(
        jnp.int32
    )
    earlier = jnp.cumsum(onehot_table, 0) - onehot_table
    slot_index = jnp.sum(earlier * onehot_table, 1)
    target = flat_ids * capacity + slot_index
    source_row = jnp.arange(tokens_dev * choices_each, dtype=jnp.int32) // choices_each
    gate_flat = w_gate[0].reshape(-1, w_gate.shape[3])
    up_flat = w_up[0].reshape(-1, w_up.shape[3])
    down_flat = w_down[0].reshape(w_down.shape[1], -1)
    holder = jnp.zeros((groups * capacity, mixed_in.shape[1]), mixed_in.dtype)
    arrived = lax.all_to_all(
        holder.at[target].set(mixed_in[source_row]).reshape(groups, capacity, mixed_in.shape[1]),
        "dp",
        split_axis=0,
        concat_axis=0,
        tiled=True,
    )
    piece = lax.all_gather(arrived, "heads", axis=2, tiled=True)
    flat_piece = piece.reshape(-1, piece.shape[2])
    gate_part = jnp.dot(flat_piece, gate_flat, preferred_element_type=jnp.float32)
    up_part = jnp.dot(flat_piece, up_flat, preferred_element_type=jnp.float32)
    gate_val, up_val = (
        lax.psum(gate_part.astype(jnp.bfloat16), "side").astype(jnp.float32),
        lax.psum(up_part.astype(jnp.bfloat16), "side").astype(jnp.float32),
    )
    activation = (jax.nn.silu(gate_val) * up_val).astype(jnp.bfloat16)
    down_part = jnp.dot(activation, down_flat, preferred_element_type=jnp.float32).reshape(
        groups, capacity, heads_count, piece_width
    )
    reduced = lax.psum_scatter(
        down_part.astype(jnp.bfloat16), "heads", scatter_dimension=2, tiled=True
    )
    returned = lax.all_to_all(reduced, "dp", split_axis=0, concat_axis=0, tiled=True)
    picked = returned.reshape(groups * capacity, piece_width)[target].astype(jnp.float32)
    weighted = picked * expert_gates.reshape(-1)[:, None]
    moe_out = jnp.sum(weighted.reshape(tokens_dev, choices_each, piece_width), 1).astype(
        jnp.bfloat16
    )
    return (
        state_out,
        resid_new.reshape(requests_dev, step_count, piece_width),
        moe_out.reshape(requests_dev, step_count, piece_width),
    )


def solution(mesh):
    return jax.shard_map(
        local,
        mesh=mesh,
        in_specs=(
            P("dp", None, ("heads", "side")),
            P("dp", None, ("heads", "side")),
            P("dp", None, ("heads", "side")),
            P("dp", ("heads", "side"), None, None),
            P(("heads", "side")),
            P(("heads", "side")),
            P(("heads", "side"), None),
            P("dp", None, ("heads", "side")),
            P(),
            P("dp", None, None),
            P("dp", None, None),
            P("dp", None, "side", "heads"),
            P("dp", None, "side", "heads"),
            P("dp", "heads", None, "side"),
        ),
        out_specs=(
            P("dp", ("heads", "side"), None, None),
            P("dp", None, ("heads", "side")),
            P("dp", None, ("heads", "side")),
        ),
        check_vma=False,
    )
```

profile of v0, /device:TPU:0, one launch (start us, length us, event | category | flops | bytes accessed | tf_op | source)
XLA Modules:
  0.0 209.7 jit_solution(11162556744923903305)
XLA Ops:
  7.2 1.6 reshape.157
  8.8 1.5 reshape.159
  14.2 5.6 %fusion = f32[24,4,1,128]{3,2,1,0:T(1,128)S(1)} fusion(bf16[24,4,128,128]{3,2,1,0:T(8,128)(2,1)} %param.17, f32[24,4,128]{2,1,0:T(4,128)S(1)} %get-tuple-element.9, f32[24,4,128]{2,1,0:T(4,128)S(1)} %get-tuple-element.14, f32[4]{0:T(128)S(1)} %negate_exponential_fusion, bf16[24,4,128,1]{2,1,0,3:T(4,128)(2,1)S(1)} %get-tuple-element.11), kind=kOutput, calls=%fused_computation.5 | convolution fusion | flops 25165824 | bytes 3317776 | tf_op jit(solution)/shard_map/rhi,rhij->rhj/dot_general | solution.py:41
  19.8 5.6 %fusion.1 = f32[24,4,1,128]{3,2,1,0:T(1,128)S(1)} fusion(bf16[24,4,128,128]{3,2,1,0:T(8,128)(2,1)S(1)} %copy-done.3, f32[24,4,128]{2,1,0:T(4,128)S(1)} %get-tuple-element.10, f32[24,4,128]{2,1,0:T(4,128)S(1)} %get-tuple-element.13, f32[24,4,128]{2,1,0:T(4,128)S(1)} %get-tuple-element.9, f32[24,4,128]{2,1,0:T(4,128)S(1)} %get-tuple-element.14, ...), kind=kOutput, calls=%fused_computation.6 | convolution fusion | flops 29884416 | bytes 3416080 | tf_op jit(solution)/shard_map/rhi,rhij->rhj/dot_general | solution.py:41
  29.3 3.4 %fusion.25 = f32[48,3072]{1,0:T(8,128)} fusion(bf16[512,3072]{1,0:T(8,128)(2,1)} %param.20, f32[6,8,4,128]{3,2,1,0:T(4,128)S(1)} %bitcast.71, f32[512]{0:T(512)S(1)} %copy-done.11), kind=kOutput, calls=%fused_computation.42 | convolution fusion | flops 151044096 | bytes 3835904 | tf_op jit(solution)/shard_map/dot_general | solution.py:54
  36.5 1.5 reduce_window_sum.11
  42.5 24.3 %reduce-scatter.2.cloned.1.call-done = f32[48,384]{1,0:T(8,128)} async-done(((f32[48,3072]{1,0:T(8,128)}), f32[48,384]{1,0:T(8,128)}) %reduce-scatter.2.cloned.1.call-update) | async-done | bytes 73744 | tf_op jit(solution)/shard_map/reduce_scatter | solution.py:55
  66.8 1.6 fusion.18
  68.4 14.4 %psum.21 = f32[48]{0:T(128)} all-reduce(f32[48]{0:T(128)S(1)} %get-tuple-element.5), channel_id=1, replica_groups=mesh['dp'=4,'heads'=4,'side'=2] {'heads','side'}, use_global_device_ids=true, to_apply=%region_5.6 | all-reduce | flops 48 | bytes 384 | tf_op jit(solution)/shard_map/psum | solution.py:62
  83.5 1.5 fusion.20
  85.0 2.8 %scatter_custom_fusion = bf16[144,384]{1,0:T(8,128)(2,1)} fusion(s32[96]{0:T(128)S(1)} %fusion.32, bf16[48,384]{1,0:T(8,128)(2,1)} %fusion.20, s32[1024]{0:T(1024)S(1)} %pad_clamp_fusion.1, bf16[]{:T(256)} %constant.43.clone.1), kind=kCustom, calls=%fused_computation.37 | custom fusion | bytes 111104 | tf_op jit(solution)/shard_map/scatter | solution.py:86
  87.8 1.6 reshape.153
  89.4 8.5 %all_to_all.10 = bf16[4,36,384]{2,1,0:T(8,128)(2,1)S(1)} all-to-all(bf16[4,36,384]{2,1,0:T(8,128)(2,1)} %reshape.153), channel_id=1, replica_groups=mesh['dp'=4,'heads'=4,'side'=2] {'dp'}, dimensions={0} | all-to-all | bytes 221184 | tf_op jit(solution)/shard_map/all_to_all | solution.py:85
  97.9 15.7 %all_gather.3 = bf16[4,36,1536]{2,1,0:T(8,128)(2,1)} all-gather(bf16[4,36,384]{2,1,0:T(8,128)(2,1)S(1)} %all_to_all.10), channel_id=1, replica_groups=mesh['dp'=4,'heads'=4,'side'=2] {'heads'}, dimensions={2}, use_global_device_ids=true | all-gather | bytes 552960 | tf_op jit(solution)/shard_map/all_gather | solution.py:92
  113.6 1.9 reshape.154
  115.5 2.6 %convolution_convert_fusion = bf16[144,1152]{1,0:T(8,128)(2,1)} fusion(bf16[144,1536]{1,0:T(8,128)(2,1)} %reshape.154, bf16[1536,1152]{1,0:T(8,128)(2,1)S(1)} %bitcast.66), kind=kOutput, calls=%fused_computation.16 | convolution fusion | flops 509773824 | bytes 4313088 | tf_op jit(solution)/shard_map/dot_general | solution.py:95
  118.1 1.5 convolution_convert_fusion.1
  119.7 4.4 %copy.94 = bf16[144,8,4,384]{3,1,2,0:T(8,128)(2,1)} copy(bf16[144,8,4,384]{3,2,1,0:T(4,128)(2,1)} %bitcast.69) | data formatting | bytes 7077888
  124.2 5.8 %copy.77 = bf16[1536,1152]{1,0:T(8,128)(2,1)} copy(bf16[1536,1152]{0,1:T(8,128)(2,1)} %bitcast.67) | data formatting | bytes 7077888 | tf_op jit(solution)/shard_map/dot_general | solution.py:101
  131.3 4.9 %all-reduce.7.cloned.1.call-done = (bf16[144,1152]{1,0:T(8,128)(2,1)}, bf16[144,1152]{1,0:T(8,128)(2,1)}) async-done(((bf16[144,1152]{1,0:T(8,128)(2,1)}, bf16[144,1152]{1,0:T(8,128)(2,1)}), (bf16[144,1152]{1,0:T(8,128)(2,1)}, bf16[144,1152]{1,0:T(8,128)(2,1)})) %all-reduce.7.cloned.1.call-update) | async-done | bytes 663568 | tf_op jit(solution)/shard_map/psum | solution.py:98
  136.2 2.0 fusion.15
  138.2 1.8 reshape.190
  140.0 3.5 %convolution_convert_fusion.2 = bf16[4,36,4,384]{3,1,2,0:T(8,128)(2,1)S(1)} fusion(bf16[4,384,1152,1]{2,1,0,3:T(8,128)(2,1)} %bitcast.70, bf16[4,36,1152,1]{2,1,0,3:T(8,128)(2,1)} %reshape.190), kind=kOutput, calls=%fused_computation.18 | convolution fusion | flops 509829120 | bytes 4313088 | tf_op jit(solution)/shard_map/dot_general | solution.py:101
  144.5 7.8 %fusion.2 = bf16[24,4,128,128]{3,2,1,0:T(8,128)(2,1)} fusion(bf16[24,4,128,128]{3,2,1,0:T(8,128)(2,1)} %param.17, f32[24,4,128]{2,1,0:T(4,128)} %copy-done.5, f32[24,4,128]{2,1,0:T(4,128)} %copy-done.6, f32[24,4,128]{2,1,0:T(4,128)} %copy-done.4, f32[24,4,128]{2,1,0:T(4,128)} %copy-done.7, f32[4]{0:T(128)S(1)} %copy-done.14), kind=kLoop, calls=%fused_computation.7 | loop fusion | flops 12582912 | bytes 6488080 | tf_op jit(solution)/shard_map/convert_element_type | solution.py:45
  152.4 30.9 %all-reduce.5.cloned.1.call-done = bf16[4,36,4,384]{3,0,1,2:T(4,128)(2,1)} async-done(((bf16[4,36,4,384]{3,0,1,2:T(4,128)(2,1)}), bf16[4,36,4,384]{3,0,1,2:T(4,128)(2,1)}) %all-reduce.5.cloned.1.call-update) | async-done | bytes 442384
  183.2 1.6 constant_dynamic-slice_fusion
  185.5 3.9 %all-to-all-start.1 = ((bf16[4,36,1,384]{3,1,2,0:T(8,128)(2,1)}), bf16[4,36,1,384]{3,1,2,0:T(8,128)(2,1)}, u32[]{:S(2)}, u32[]{:S(2)}) async-start(bf16[4,36,1,384]{3,1,2,0:T(8,128)(2,1)} %copy.79), calls=%async_computation.2 | async-start | bytes 245760 | tf_op jit(solution)/shard_map/all_to_all | solution.py:107
  190.8 3.6 %all-to-all-done.1 = bf16[4,36,1,384]{3,1,2,0:T(8,128)(2,1)} async-done(((bf16[4,36,1,384]{3,1,2,0:T(8,128)(2,1)}), bf16[4,36,1,384]{3,1,2,0:T(8,128)(2,1)}, u32[]{:S(2)}, u32[]{:S(2)}) %all-to-all-start.1) | async-done | bytes 110624 | tf_op jit(solution)/shard_map/all_to_all | solution.py:107
  194.5 1.6 reshape.155
  196.0 2.3 %gather_fusion = bf16[96,384]{1,0:T(8,128)(2,1)} fusion(bf16[144,384]{1,0:T(8,128)(2,1)} %reshape.155, s32[1024]{0:T(1024)S(1)} %pad_clamp_fusion), kind=kCustom, calls=%fused_computation.1 | custom fusion | bytes 147840 | tf_op jit(solution)/shard_map/gather | solution.py:108
  198.4 1.6 reshape.161
  200.0 1.8 multiply_reduce_fusion
  (67 shorter events, 22.4 us)
Async XLA Ops:
  7.2 108.3 %copy-start = (bf16[1,4,384,1152]{3,2,1,0:T(8,128)(2,1)S(1)}, bf16[1,4,384,1152]{3,2,1,0:T(8,128)(2,1)}, u32[]{:S(2)}) copy-start(bf16[1,4,384,1152]{3,2,1,0:T(8,128)(2,1)} %param.26) | copy-start | bytes 10616836
  7.2 59.6 %reduce-scatter.2.cloned.1.call-start = ((), (), s32[]{:S(2)}) async-start(), calls=%async_computation.3 | async-start | bytes 663552 | tf_op jit(solution)/shard_map/reduce_scatter | solution.py:55
  11.0 8.8 %copy-start.13 = (f32[4]{0:T(128)}, f32[4]{0:T(128)S(1)}, u32[]{:S(2)}) copy-start(f32[4]{0:T(128)S(1)} %negate_exponential_fusion) | copy-start | bytes 52
  14.1 5.6 %copy-start.4 = (f32[24,4,128]{2,1,0:T(4,128)}, f32[24,4,128]{2,1,0:T(4,128)S(1)}, u32[]{:S(2)}) copy-start(f32[24,4,128]{2,1,0:T(4,128)S(1)} %get-tuple-element.9) | copy-start | bytes 147460
  14.1 5.6 %copy-start.5 = (f32[24,4,128]{2,1,0:T(4,128)}, f32[24,4,128]{2,1,0:T(4,128)S(1)}, u32[]{:S(2)}) copy-start(f32[24,4,128]{2,1,0:T(4,128)S(1)} %get-tuple-element.10) | copy-start | bytes 147460
  14.1 5.6 %copy-start.6 = (f32[24,4,128]{2,1,0:T(4,128)}, f32[24,4,128]{2,1,0:T(4,128)S(1)}, u32[]{:S(2)}) copy-start(f32[24,4,128]{2,1,0:T(4,128)S(1)} %get-tuple-element.13) | copy-start | bytes 147460
  14.1 5.6 %copy-start.7 = (f32[24,4,128]{2,1,0:T(4,128)}, f32[24,4,128]{2,1,0:T(4,128)S(1)}, u32[]{:S(2)}) copy-start(f32[24,4,128]{2,1,0:T(4,128)S(1)} %get-tuple-element.14) | copy-start | bytes 147460
  14.2 5.6 %copy-start.3 = (bf16[24,4,128,128]{3,2,1,0:T(8,128)(2,1)S(1)}, bf16[24,4,128,128]{3,2,1,0:T(8,128)(2,1)}, u32[]{:S(2)}) copy-start(bf16[24,4,128,128]{3,2,1,0:T(8,128)(2,1)} %param.17) | copy-start | bytes 9437188
  19.7 5.7 %copy-start.8 = (f32[24,4,1,128]{3,2,1,0:T(1,128)}, f32[24,4,1,128]{3,2,1,0:T(1,128)S(1)}, u32[]{:S(2)}) copy-start(f32[24,4,1,128]{3,2,1,0:T(1,128)S(1)} %fusion) | copy-start | bytes 147460
  19.8 9.5 %copy-start.11 = (f32[512]{0:T(512)S(1)}, f32[512]{0:T(512)}, u32[]{:S(2)}) copy-start(f32[512]{0:T(512)} %param.19) | copy-start | bytes 6148
  25.5 0.6 copy-start.9
  25.5 8.7 %copy-start.10 = (s32[24,2,2]{0,2,1:T(2,128)S(1)}, s32[24,2,2]{0,2,1:T(2,128)}, u32[]{:S(2)}) copy-start(s32[24,2,2]{0,2,1:T(2,128)} %param.23) | copy-start | bytes 1156
  32.7 103.4 %all-reduce.7.cloned.1.call-start = ((), (), s32[]{:S(2)}) async-start(), calls=%async_computation.5 | async-start | bytes 1327104 | tf_op jit(solution)/shard_map/psum | solution.py:98
  115.5 2.6 %copy-start.1 = (bf16[144,1536]{1,0:T(8,128)(2,1)S(1)}, bf16[144,1536]{1,0:T(8,128)(2,1)}, u32[]{:S(2)}) copy-start(bf16[144,1536]{1,0:T(8,128)(2,1)} %reshape.154) | copy-start | bytes 1327108
  115.5 2.6 %copy-start.2 = (bf16[1,4,384,1152]{3,2,1,0:T(8,128)(2,1)S(1)}, bf16[1,4,384,1152]{3,2,1,0:T(8,128)(2,1)}, u32[]{:S(2)}) copy-start(bf16[1,4,384,1152]{3,2,1,0:T(8,128)(2,1)} %param.25) | copy-start | bytes 10616836
  119.6 63.6 %all-reduce.5.cloned.1.call-start = ((), (), s32[]{:S(2)}) async-start(), calls=%async_computation.4 | async-start | bytes 884736
  124.2 5.8 %copy-start.12 = (f32[24,2,2]{0,2,1:T(2,128)S(1)}, f32[24,2,2]{0,2,1:T(2,128)}, u32[]{:S(2)}) copy-start(f32[24,2,2]{0,2,1:T(2,128)} %param.24) | copy-start | bytes 1156
  124.2 6.5 %copy-start.15 = (u32[32]{0:T(128)S(1)}, u32[32]{0:T(128)}, u32[]{:S(2)}) copy-start(u32[32]{0:T(128)} %constant.64) | copy-start | bytes 388
  140.0 4.6 %copy-start.14 = (f32[4]{0:T(128)S(1)}, f32[4]{0:T(128)}, u32[]{:S(2)}) copy-start(f32[4]{0:T(128)} %copy-done.13) | copy-start | bytes 52
  185.5 9.0 %all-to-all-start.1 = ((bf16[4,36,1,384]{3,1,2,0:T(8,128)(2,1)}), bf16[4,36,1,384]{3,1,2,0:T(8,128)(2,1)}, u32[]{:S(2)}, u32[]{:S(2)}) async-start(bf16[4,36,1,384]{3,1,2,0:T(8,128)(2,1)} %copy.79), calls=%async_computation.2 | async-start | bytes 245760 | tf_op jit(solution)/shard_map/all_to_all | solution.py:107
Sparse Core Ops, SparseCore 0:
  32.9 33.8 reduce-scatter.1
  119.8 16.3 all-reduce.6
  144.6 38.5 all-reduce.4
where the time goes:
time: 212 us; the launch traced here: 210 us
  waiting for transfers between devices  63.7 us (30%)
  local copies, waits for them, and re-layouts  45.4 us (21%)
  blocking collectives  38.6 us (18%)
  matrix products  22.2 us (10%)
  other arithmetic  21.6 us (10%)
  between operations  14 us (7%)
  starting transfers between devices  4.05 us (2%)
    unnamed x4, waiting for transfers between devices  30.9 us
    reduce_scatter x1, waiting for transfers between devices, local(): lax.psum_scatter(partial_out, ('heads', 'side'), scatter_dimension=1, til...  24.3 us
    all_gather x1, blocking collectives, local(): piece = lax.all_gather(arrived, 'heads', axis=2, tiled=True)  15.7 us
    psum x1, blocking collectives, local(): sum_squares = lax.psum(jnp.sum(stream * stream, 1), ('heads', 'side'))  14.4 us
    dot_general x2, matrix products, local(): jnp.einsum('rhi,rhij->rhj', query_rows[:, step], current, precision=lax.P...  11.2 us
    all_to_all x1, blocking collectives, local(): lax.all_to_all(holder.at[target].set(mixed_in[source_row]).reshape(groups...  8.55 us
    unnamed x36, local copies, waits for them, and re-layouts  7.99 us
    convert_element_type x1, other arithmetic, local(): state_out = current.astype(jnp.bfloat16)  7.83 us
  transfers between devices with their start and end apart: 4, of which 4 were waited for; matrix products, arithmetic and copies ran while one was open for 15% of the time, Pallas kernels for 0%

commit v1 on v0

v1 whole, which is shorter than its diff:
```python
import functools

import jax
import jax.numpy as jnp
from jax import lax
from jax.experimental import pallas as pl
from jax.experimental.pallas import tpu as pltpu
from jax.sharding import PartitionSpec as P

BF = jnp.bfloat16
F32 = jnp.float32
VMEM_LIMIT = 48 * 1024 * 1024


def params():
    return pltpu.CompilerParams(vmem_limit_bytes=VMEM_LIMIT)


def struct(shape, dtype):
    return jax.ShapeDtypeStruct(shape, dtype)


def whole_vmem(count):
    return [pl.BlockSpec(memory_space=pltpu.VMEM)] * count


def cost(flops, size):
    return pl.CostEstimate(flops=flops, bytes_accessed=size, transcendentals=0)


def dot(a, b):
    return jnp.dot(a, b, preferred_element_type=F32)


def attention_kernel(
    slope_ref, q_ref, k_ref, v_ref, s_ref, gain_ref, w_hbm,
    so_ref, mine_ref, other_ref, normed, w_vmem, w_sem,
):
    step, steps = pl.program_id(0), pl.num_programs(0)
    copy = pltpu.make_async_copy(w_hbm, w_vmem, w_sem)

    @pl.when(step == 0)
    def _():
        copy.start()

    requests, tokens, width = q_ref.shape
    heads, size = s_ref.shape[1], s_ref.shape[2]
    rows = requests * tokens
    row = lax.broadcasted_iota(jnp.int32, (rows, size), 0)
    second = row % tokens == 1
    owner = row // tokens
    parts = []
    for h in range(heads):
        at = slice(h * size, (h + 1) * size)
        q16 = q_ref[:, :, at].reshape(rows, size)
        k16 = k_ref[:, :, at].reshape(rows, size)
        q, k = q16.astype(F32), k16.astype(F32)
        v = v_ref[:, :, at].reshape(rows, size).astype(F32)
        decay = jnp.exp(jnp.full((rows, size), -slope_ref[h], F32))
        read = jnp.zeros((rows, size), F32)
        for r in range(requests):
            read = jnp.where(owner == r, dot(q16, s_ref[r, h]), read)
        k_before = pltpu.roll(k, 1, 0)
        v_before = pltpu.roll(v, 1, 0)
        same = jnp.sum(q * k, -1, keepdims=True)
        cross = jnp.sum(q * k_before, -1, keepdims=True)
        out = jnp.where(second, decay * decay, decay) * read + same * v
        out = out + jnp.where(second, decay * cross * v_before, 0.0)
        out = out * lax.rsqrt(jnp.mean(out * out, -1, keepdims=True) + 1e-06)
        parts.append((out * gain_ref[:, at]).astype(BF))
        weighted = jnp.where(second, v, decay * v)
        spread = jnp.concatenate(
            [jnp.where(owner == r, weighted, 0.0).astype(BF) for r in range(requests)], 1
        )
        update = lax.dot_general(
            k16, spread, (((0,), (0,)), ((), ())), preferred_element_type=F32
        )
        keep = jnp.exp(jnp.full((size, size), -2.0 * slope_ref[h], F32))
        for r in range(requests):
            so_ref[r, h] = (
                keep * s_ref[r, h].astype(F32) + update[:, r * size : (r + 1) * size]
            ).astype(BF)
    block = jnp.concatenate(parts, 1) if heads > 1 else parts[0]
    normed[pl.ds(pl.multiple_of(step * rows, rows), rows), :] = block

    @pl.when(step == steps - 1)
    def _():
        copy.wait()
        side = lax.axis_index("side")
        groups, _, piece = mine_ref.shape
        for a in range(groups):
            both = dot(normed[...], w_vmem[:, 2 * a * piece : 2 * (a + 1) * piece])
            low, high = both[:, :piece], both[:, piece:]
            mine_ref[a] = jnp.where(side == 0, low, high)
            other_ref[a] = jnp.where(side == 0, high, low).astype(BF)


def attention(slopes, queries, new_keys, new_values, head_states, gain, out_weight, groups):
    requests, tokens, width = queries.shape
    heads, size = head_states.shape[1:3]
    block = 8 if requests % 8 == 0 else requests
    piece = out_weight.shape[1] // (2 * groups)
    rows = requests * tokens
    vec = pl.BlockSpec((block, tokens, width), lambda i: (i, 0, 0))
    state = pl.BlockSpec((block, heads, size, size), lambda i: (i, 0, 0, 0))
    fixed = pl.BlockSpec((groups, rows, piece), lambda i: (0, 0, 0))
    return pl.pallas_call(
        attention_kernel,
        grid=(requests // block,),
        in_specs=[
            pl.BlockSpec(memory_space=pltpu.SMEM),
            vec, vec, vec, state,
            pl.BlockSpec((1, width), lambda i: (0, 0)),
            pl.BlockSpec(memory_space=pl.ANY),
        ],
        out_specs=[state, fixed, fixed],
        out_shape=[
            struct(head_states.shape, BF),
            struct((groups, rows, piece), F32),
            struct((groups, rows, piece), BF),
        ],
        scratch_shapes=[
            pltpu.VMEM((rows, width), BF),
            pltpu.VMEM(out_weight.shape, BF),
            pltpu.SemaphoreType.DMA,
        ],
        compiler_params=params(),
        name="attention",
    )(slopes, queries, new_keys, new_values, head_states, gain, out_weight)


def split_kernel(mine_ref, recv_ref, own_ref, *send_refs):
    me = lax.axis_index("heads")
    own_ref[...] = mine_ref[me].astype(F32) + recv_ref[me].astype(F32)
    for k, send_ref in enumerate(send_refs, 1):
        at = me ^ k
        send_ref[...] = (mine_ref[at].astype(F32) + recv_ref[at].astype(F32)).astype(BF)


def split(mine, recv):
    groups, rows, piece = mine.shape
    return pl.pallas_call(
        split_kernel,
        in_specs=whole_vmem(2),
        out_specs=whole_vmem(groups),
        out_shape=[struct((rows, piece), F32)] + [struct((rows, piece), BF)] * (groups - 1),
        compiler_params=params(),
        name="split_sum",
    )(mine, recv)


def residual_kernel(residual_ref, own_ref, *refs):
    recv_refs, (resid_ref, flat_ref) = refs[:-2], refs[-2:]
    total = own_ref[...]
    for recv_ref in recv_refs:
        total = total + recv_ref[...].astype(F32)
    total = residual_ref[...].astype(F32).reshape(total.shape) + total
    rounded = total.astype(BF)
    flat_ref[...] = rounded
    resid_ref[...] = rounded.reshape(resid_ref.shape)


def add_residual(residual, own, recvs):
    return pl.pallas_call(
        residual_kernel,
        in_specs=whole_vmem(2 + len(recvs)),
        out_specs=whole_vmem(2),
        out_shape=[struct(residual.shape, BF), struct(own.shape, BF)],
        compiler_params=params(),
        name="add_residual",
    )(residual, own, *recvs)


def gate_up_kernel(gain_ref, wg_ref, wu_ref, *refs):
    x_refs, (out_ref, placed) = refs[:-2], refs[-2:]
    me, side = lax.axis_index("heads"), lax.axis_index("side")
    groups, rows, piece = x_refs[0].shape
    hidden = wg_ref.shape[3]
    total = rows * len(x_refs)
    squares = jnp.zeros((total, 1), F32)
    for k in range(groups):
        at = me ^ k
        x = jnp.concatenate([x_ref[k] for x_ref in x_refs], 0).astype(F32)
        squares = squares + jnp.sum(x * x, -1, keepdims=True)
        placed[at] = (x * gain_ref[pl.ds(at * 2 + side, 1), :]).astype(BF)
    lhs = jnp.concatenate([placed[a] for a in range(groups)], 1)
    wide = 384 if hidden % 384 == 0 else hidden
    for n in range(0, hidden, wide):
        rhs = wg_ref[0, :, :, n : n + wide].reshape(groups * piece, wide)
        out_ref[:, n : n + wide] = dot(lhs, rhs).astype(BF)
    for n in range(0, hidden, wide):
        rhs = wu_ref[0, :, :, n : n + wide].reshape(groups * piece, wide)
        out_ref[:, hidden + n : hidden + n + wide] = dot(lhs, rhs).astype(BF)
    coarse = squares.astype(BF)
    fine = (squares - coarse.astype(F32)).astype(BF)
    lane = lax.broadcasted_iota(jnp.int32, (total, 128), 1)
    extra = jnp.where(lane == 0, coarse.astype(F32), jnp.where(lane == 1, fine.astype(F32), 0.0))
    out_ref[:, 2 * hidden :] = extra.astype(BF)


def gate_up(gain, w_gate, w_up, xs):
    groups, rows, piece = xs[0].shape
    hidden = w_gate.shape[3]
    total = rows * len(xs)
    return pl.pallas_call(
        gate_up_kernel,
        in_specs=whole_vmem(3 + len(xs)),
        out_specs=pl.BlockSpec(memory_space=pltpu.VMEM),
        out_shape=struct((total, 2 * hidden + 128), BF),
        scratch_shapes=[pltpu.VMEM((groups, total, piece), BF)],
        compiler_params=params(),
        name="gate_up",
    )(gain, w_gate, w_up, *xs)


def regroup_kernel(w_ref, out_ref):
    count = w_ref.shape[1]
    step = 64 if count % 64 == 0 else 32

    def one(i, carry):
        at = pl.ds(pl.multiple_of(i * step, step), step)
        out_ref[:, at, :] = w_ref[0, at].swapaxes(0, 1)
        return carry

    lax.fori_loop(0, count // step, one, 0)


def regroup(w_down):
    _, hidden, groups, piece = w_down.shape
    return pl.pallas_call(
        regroup_kernel,
        in_specs=whole_vmem(1),
        out_specs=pl.BlockSpec(memory_space=pltpu.VMEM),
        out_shape=struct((groups, hidden, piece), BF),
        compiler_params=params(),
        name="regroup_down",
    )(w_down)


def down_kernel(width, part_ref, recv_ref, w_ref, *out_refs):
    groups, rows, piece = out_refs[0].shape
    hidden = w_ref.shape[1]
    extra = part_ref[:, 2 * hidden :].astype(F32) + recv_ref[:, 2 * hidden :].astype(F32)
    squares = extra[:, 0:1] + extra[:, 1:2]
    scale = lax.rsqrt(squares / width + 1e-06)
    gate = (part_ref[:, :hidden].astype(F32) + recv_ref[:, :hidden].astype(F32)) * scale
    up = (
        part_ref[:, hidden : 2 * hidden].astype(F32) + recv_ref[:, hidden : 2 * hidden].astype(F32)
    ) * scale
    act = (gate / (1.0 + jnp.exp(-gate)) * up).astype(BF)
    for a in range(groups):
        out = dot(act, w_ref[a]).astype(BF)
        for d, out_ref in enumerate(out_refs):
            out_ref[a] = out[d * rows : (d + 1) * rows]


def down(width, part, recv, weights, count):
    groups, hidden, piece = weights.shape
    rows = part.shape[0] // count
    return pl.pallas_call(
        functools.partial(down_kernel, width),
        in_specs=whole_vmem(3),
        out_specs=whole_vmem(count),
        out_shape=[struct((groups, rows, piece), BF)] * count,
        compiler_params=params(),
        name="down",
    )(part, recv, weights)


def combine_kernel(count, ids_ref, gates_ref, *refs):
    y_refs, out_refs = refs[:count], refs[count:]
    here, me = lax.axis_index("dp"), lax.axis_index("heads")
    groups, rows, piece = y_refs[0].shape
    tokens, choices, requests = ids_ref.shape
    row = lax.broadcasted_iota(jnp.int32, (rows, requests), 0)
    lane = lax.broadcasted_iota(jnp.int32, (rows, requests), 1)
    mine = [(row // tokens == lane) & (row % tokens == s) for s in range(tokens)]
    weights = []
    for d in range(count):
        weight = jnp.zeros((rows, requests), F32)
        for s in range(tokens):
            for c in range(choices):
                gate = jnp.where(
                    ids_ref[s, c : c + 1, :] == (here ^ d), gates_ref[s, c : c + 1, :], 0.0
                )
                weight = weight + jnp.where(mine[s], gate, 0.0)
        weights.append(jnp.sum(weight, -1, keepdims=True))
    for k, out_ref in enumerate(out_refs):
        at = me ^ k
        total = jnp.zeros((rows, piece), F32)
        for weight, y_ref in zip(weights, y_refs):
            total = total + weight * y_ref[at].astype(F32)
        out_ref[...] = total.astype(out_ref.dtype)


def combine(ids, gates, ys):
    groups, rows, piece = ys[0].shape
    return pl.pallas_call(
        functools.partial(combine_kernel, len(ys)),
        in_specs=whole_vmem(2 + len(ys)),
        out_specs=whole_vmem(groups),
        out_shape=[struct((rows, piece), F32)] + [struct((rows, piece), BF)] * (groups - 1),
        compiler_params=params(),
        name="combine",
    )(ids, gates, *ys)


def finish_kernel(own_ref, *refs):
    recv_refs, out_ref = refs[:-1], refs[-1]
    total = own_ref[...]
    for recv_ref in recv_refs:
        total = total + recv_ref[...].astype(F32)
    out_ref[...] = total.astype(BF).reshape(out_ref.shape)


def finish(own, recvs, shape):
    return pl.pallas_call(
        finish_kernel,
        in_specs=whole_vmem(1 + len(recvs)),
        out_specs=pl.BlockSpec(memory_space=pltpu.VMEM),
        out_shape=struct(shape, BF),
        compiler_params=params(),
        name="finish",
    )(own, *recvs)


def swap(x, axis, k):
    size = lax.axis_size(axis)
    return lax.ppermute(x, axis, [(i, i ^ k) for i in range(size)])


def local(
    queries, new_keys, new_values, head_states, slopes, head_gain, out_weight, residual,
    norm_gain, expert_ids, expert_gates, w_gate, w_up, w_down,
):
    groups, count = lax.axis_size("heads"), lax.axis_size("dp")
    width = norm_gain.shape[0]
    piece = residual.shape[2]
    state_out, mine, other = attention(
        slopes, queries, new_keys, new_values, head_states,
        head_gain.reshape(1, -1), out_weight, groups,
    )
    own, *sends = split(mine, swap(other, "side", 1))
    recvs = [swap(x, "heads", k) for k, x in enumerate(sends, 1)]
    resid_out, flat = add_residual(residual, own, recvs)
    gathered = jnp.stack([flat] + [swap(flat, "heads", k) for k in range(1, groups)])
    xs = [gathered] + [swap(gathered, "dp", k) for k in range(1, count)]
    part = gate_up(norm_gain.reshape(-1, piece), w_gate, w_up, xs)
    weights = regroup(w_down)
    own, *sends = down(width, part, swap(part, "side", 1), weights, count)
    ys = [own] + [swap(x, "dp", k) for k, x in enumerate(sends, 1)]
    own, *sends = combine(
        jnp.transpose(expert_ids, (1, 2, 0)), jnp.transpose(expert_gates, (1, 2, 0)), ys
    )
    recvs = [swap(x, "heads", k) for k, x in enumerate(sends, 1)]
    return state_out, resid_out, finish(own, recvs, residual.shape)


def solution(mesh):
    return jax.shard_map(
        local,
        mesh=mesh,
        in_specs=(
            P("dp", None, ("heads", "side")),
            P("dp", None, ("heads", "side")),
            P("dp", None, ("heads", "side")),
            P("dp", ("heads", "side"), None, None),
            P(("heads", "side")),
            P(("heads", "side")),
            P(("heads", "side"), None),
            P("dp", None, ("heads", "side")),
            P(),
            P("dp", None, None),
            P("dp", None, None),
            P("dp", None, "side", "heads"),
            P("dp", None, "side", "heads"),
            P("dp", "heads", None, "side"),
        ),
        out_specs=(
            P("dp", ("heads", "side"), None, None),
            P("dp", None, ("heads", "side")),
            P("dp", None, ("heads", "side")),
        ),
        check_vma=False,
    )
```

time: 212 us -> 70 us (0.33)
  waiting for transfers between devices: 63.7 us -> 24 us
  local copies, waits for them, and re-layouts: 45.4 us -> 6.34 us
  blocking collectives: 38.6 us -> 0 us
  matrix products: 22.2 us -> 0 us
  other arithmetic: 21.6 us -> 0.7 us
  starting transfers between devices: 4.05 us -> 22.1 us
  Pallas kernels: 0 us -> 15.7 us
  between operations: 14 us -> 0.73 us
    unnamed x4 -> x0, waiting for transfers between devices: 30.9 us -> none
    reduce_scatter x1 -> x0, waiting for transfers between devices: 24.3 us -> none  [local(): lax.psum_scatter(partial_out, ('heads', 'side'), scatter_dimension=1, til...]
    ppermute x0 -> x17, waiting for transfers between devices: none -> 24 us  [swap(): return lax.ppermute(x, axis, [(i, i ^ k) for i in range(size)])]
    dot_general x6 -> x0, matrix products: 22.2 us -> none  [the longest x2 11.2 us: local(): jnp.einsum('rhi,rhij->rhj', query_rows[:, step], current, precision=lax.P...]
    ppermute x0 -> x17, starting transfers between devices: none -> 22.1 us  [swap(): return lax.ppermute(x, axis, [(i, i ^ k) for i in range(size)])]
    all_gather x1 -> x0, blocking collectives: 15.7 us -> none  [local(): piece = lax.all_gather(arrived, 'heads', axis=2, tiled=True)]
    pallas_call x0 -> x8, Pallas kernels: none -> 15.7 us  [the longest x1 5.36 us: attention(): pl.pallas_call(attention_kernel, grid=(requests // block,), in_specs=[pl....]
    psum x1 -> x0, blocking collectives: 14.4 us -> none  [local(): sum_squares = lax.psum(jnp.sum(stream * stream, 1), ('heads', 'side'))]
  transfers between devices with their start and end apart: 4 -> 17, of which waited for: 4 -> 13; matrix products, arithmetic and copies ran while one was open for 15% -> 1% of each run, Pallas kernels for 0% -> 4%
where the time goes in v1:
time: 70 us; the launch traced here: 69.6 us
  waiting for transfers between devices  24 us (34%)
  starting transfers between devices  22.1 us (32%)
  Pallas kernels  15.7 us (22%)
  local copies, waits for them, and re-layouts  6.34 us (9%)
  between operations  0.73 us (1%)
    ppermute x17, waiting for transfers between devices, swap(): return lax.ppermute(x, axis, [(i, i ^ k) for i in range(size)])  24 us
    ppermute x17, starting transfers between devices, swap(): return lax.ppermute(x, axis, [(i, i ^ k) for i in range(size)])  22.1 us
    unnamed x20, local copies, waits for them, and re-layouts  5.63 us
    pallas_call x1, Pallas kernels, attention(): pl.pallas_call(attention_kernel, grid=(requests // block,), in_specs=[pl....  5.36 us
    pallas_call x1, Pallas kernels, gate_up(): pl.pallas_call(gate_up_kernel, in_specs=whole_vmem(3 + len(xs)), out_spec...  4.34 us
    pallas_call x1, Pallas kernels, regroup(): pl.pallas_call(regroup_kernel, in_specs=whole_vmem(1), out_specs=pl.Block...  2.92 us
    pallas_call x1, Pallas kernels, down(): pl.pallas_call(functools.partial(down_kernel, width), in_specs=whole_vmem...  1.47 us
  transfers between devices with their start and end apart: 17, of which 13 were waited for; matrix products, arithmetic and copies ran while one was open for 1% of the time, Pallas kernels for 4%

profile of v1, /device:TPU:0, one launch (start us, length us, event | category | flops | bytes accessed | tf_op | source)
XLA Modules:
  0.0 69.6 jit_solution(17158219427463860458)
XLA Ops:
  0.6 1.9 %copy-done.1 = bf16[24,4,128,128]{3,2,1,0:T(8,128)(2,1)S(1)} copy-done((bf16[24,4,128,128]{3,2,1,0:T(8,128)(2,1)S(1)}, bf16[24,4,128,128]{3,2,1,0:T(8,128)(2,1)}, u32[]{:S(2)}) %copy-start.1) | copy-done | bytes 3145752
  2.5 0.8 %copy-done.2 = bf16[24,2,512]{2,1,0:T(2,128)(2,1)S(1)} copy-done((bf16[24,2,512]{2,1,0:T(2,128)(2,1)S(1)}, bf16[24,2,512]{2,1,0:T(2,128)(2,1)}, u32[]{:S(2)}) %copy-start.2) | copy-done | bytes 49176
  3.3 0.8 %copy-done.3 = bf16[24,2,512]{2,1,0:T(2,128)(2,1)S(1)} copy-done((bf16[24,2,512]{2,1,0:T(2,128)(2,1)S(1)}, bf16[24,2,512]{2,1,0:T(2,128)(2,1)}, u32[]{:S(2)}) %copy-start.3) | copy-done | bytes 49176
  4.1 0.8 %copy-done.4 = bf16[24,2,512]{2,1,0:T(2,128)(2,1)S(1)} copy-done((bf16[24,2,512]{2,1,0:T(2,128)(2,1)S(1)}, bf16[24,2,512]{2,1,0:T(2,128)(2,1)}, u32[]{:S(2)}) %copy-start.4) | copy-done | bytes 49176
  4.9 0.7 copy-done.6
  6.3 5.4 %attention.1 = (bf16[24,4,128,128]{3,2,1,0:T(8,128)(2,1)}, f32[4,48,384]{2,1,0:T(8,128)S(1)}, bf16[4,48,384]{2,1,0:T(8,128)(2,1)S(1)}) custom-call(f32[4]{0:T(128)S(1)} %copy-done.9, bf16[24,2,512]{2,1,0:T(2,128)(2,1)S(1)} %copy-done.2, bf16[24,2,512]{2,1,0:T(2,128)(2,1)S(1)} %copy-done.3, bf16[24,2,512]{2,1,0:T(2,128)(2,1)S(1)} %copy-done.4, ...), custom_call_target="tpu_custom_call" | custom-call | tf_op jit(solution)/shard_map/attention/pallas_call | solution.py:107
  12.1 1.0 %collective-permute-done.recv_ref = bf16[4,48,384]{2,1,0:T(8,128)(2,1)S(1)} collective-permute-done((bf16[4,48,384]{2,1,0:T(8,128)(2,1)S(1)}, bf16[4,48,384]{2,1,0:T(8,128)(2,1)S(1)}, u32[]{:S(2)}, u32[]{:S(2)}) %collective-permute-start) | collective-permute-done | bytes 147488 | tf_op jit(solution)/shard_map/ppermute | solution.py:329
  13.2 3.0 %collective-permute-start.1 = (bf16[48,384]{1,0:T(8,128)(2,1)S(1)}, bf16[48,384]{1,0:T(8,128)(2,1)S(1)}, u32[]{:S(2)}, u32[]{:S(2)}) collective-permute-start(bf16[48,384]{1,0:T(8,128)(2,1)S(1)} %get-tuple-element.24), channel_id=1, source_target_pairs={{0,2},{2,0},{4,6},{6,4},{1,3},{3,1},{5,7},{7,5},{8,10},{10,8},{12,... | collective-permute-start | bytes 110600 | tf_op jit(solution)/shard_map/ppermute | solution.py:329
  16.2 2.6 %collective-permute-start.2 = (bf16[48,384]{1,0:T(8,128)(2,1)S(1)}, bf16[48,384]{1,0:T(8,128)(2,1)S(1)}, u32[]{:S(2)}, u32[]{:S(2)}) collective-permute-start(bf16[48,384]{1,0:T(8,128)(2,1)S(1)} %get-tuple-element.25), channel_id=1, source_target_pairs={{0,4},{2,6},{4,0},{6,2},{1,5},{3,7},{5,1},{7,3},{8,12},{10,14},{12... | collective-permute-start | bytes 110600 | tf_op jit(solution)/shard_map/ppermute | solution.py:329
  18.8 3.0 %collective-permute-done.2.refs_1_ = bf16[48,384]{1,0:T(8,128)(2,1)S(1)} collective-permute-done((bf16[48,384]{1,0:T(8,128)(2,1)S(1)}, bf16[48,384]{1,0:T(8,128)(2,1)S(1)}, u32[]{:S(2)}, u32[]{:S(2)}) %collective-permute-start.2) | collective-permute-done | bytes 36896 | tf_op jit(solution)/shard_map/ppermute | solution.py:329
  21.8 2.8 %collective-permute-done.3.refs_2_ = bf16[48,384]{1,0:T(8,128)(2,1)S(1)} collective-permute-done((bf16[48,384]{1,0:T(8,128)(2,1)S(1)}, bf16[48,384]{1,0:T(8,128)(2,1)S(1)}, u32[]{:S(2)}, u32[]{:S(2)}) %collective-permute-start.3) | collective-permute-done | bytes 36896 | tf_op jit(solution)/shard_map/ppermute | solution.py:329
  25.7 3.9 %collective-permute-start.4 = (bf16[48,384]{1,0:T(8,128)(2,1)S(1)}, bf16[48,384]{1,0:T(8,128)(2,1)S(1)}, u32[]{:S(2)}, u32[]{:S(2)}) collective-permute-start(bf16[48,384]{1,0:T(8,128)(2,1)S(1)} %get-tuple-element.28), channel_id=1, source_target_pairs={{0,2},{2,0},{4,6},{6,4},{1,3},{3,1},{5,7},{7,5},{8,10},{10,8},{12,... | collective-permute-start | bytes 110600 | tf_op jit(solution)/shard_map/ppermute | solution.py:329
  29.6 1.4 %collective-permute-done.6 = bf16[48,384]{1,0:T(8,128)(2,1)S(1)} collective-permute-done((bf16[48,384]{1,0:T(8,128)(2,1)S(1)}, bf16[48,384]{1,0:T(8,128)(2,1)S(1)}, u32[]{:S(2)}, u32[]{:S(2)}) %collective-permute-start.6) | collective-permute-done | bytes 36896 | tf_op jit(solution)/shard_map/ppermute | solution.py:329
  31.5 0.7 %pad_maximum_fusion.refs_0_ = bf16[4,48,384]{2,1,0:T(8,128)(2,1)} fusion(bf16[1,48,384]{2,1,0:T(8,128)(2,1)S(1)} %bitcast.11, bf16[1,48,384]{2,1,0:T(8,128)(2,1)S(1)} %bitcast.12, bf16[1,48,384]{2,1,0:T(8,128)(2,1)S(1)} %bitcast.13, bf16[1,48,384]{2,1,0:T(8,128)(2,1)S(1)} %bitcast.7), kind=kLoop, calls=%fused_computation | loop fusion | flops 221184 | bytes 294912 | tf_op jit(solution)/shard_map/stack | solution.py:346
  32.2 2.4 %collective-permute-start.9 = (bf16[4,48,384]{2,1,0:T(8,128)(2,1)}, bf16[4,48,384]{2,1,0:T(8,128)(2,1)}, u32[]{:S(2)}, u32[]{:S(2)}) collective-permute-start(bf16[4,48,384]{2,1,0:T(8,128)(2,1)} %pad_maximum_fusion.refs_0_), channel_id=1, source_target_pairs={{0,24},{8,16},{16,8},{24,0},{1,25},{9,17},{17,9},{25,1},{2,26},{10... | collective-permute-start | bytes 442376 | tf_op jit(solution)/shard_map/ppermute | solution.py:329
  35.7 0.7 %reshape.13.gain_ref = f32[8,384]{1,0:T(8,128)S(1)} reshape(f32[3072]{0:T(1024)} %param.22) | data formatting | bytes 24576 | tf_op jit(solution)/shard_map/reshape | solution.py:348
  36.4 2.3 %collective-permute-done.9.refs_3_ = bf16[4,48,384]{2,1,0:T(8,128)(2,1)} collective-permute-done((bf16[4,48,384]{2,1,0:T(8,128)(2,1)}, bf16[4,48,384]{2,1,0:T(8,128)(2,1)}, u32[]{:S(2)}, u32[]{:S(2)}) %collective-permute-start.9) | collective-permute-done | bytes 147488 | tf_op jit(solution)/shard_map/ppermute | solution.py:329
  38.8 1.6 %collective-permute-done.8.refs_2_ = bf16[4,48,384]{2,1,0:T(8,128)(2,1)} collective-permute-done((bf16[4,48,384]{2,1,0:T(8,128)(2,1)}, bf16[4,48,384]{2,1,0:T(8,128)(2,1)}, u32[]{:S(2)}, u32[]{:S(2)}) %collective-permute-start.8) | collective-permute-done | bytes 147488 | tf_op jit(solution)/shard_map/ppermute | solution.py:329
  40.7 4.3 %gate_up.1.part_ref = bf16[192,2432]{1,0:T(8,128)(2,1)S(1)} custom-call(f32[8,384]{1,0:T(8,128)S(1)} %reshape.13.gain_ref, bf16[1,4,384,1152]{3,2,1,0:T(8,128)(2,1)S(1)} %copy-done, bf16[1,4,384,1152]{3,2,1,0:T(8,128)(2,1)} %wu_ref.1, bf16[4,48,384]{2,1,0:T(8,128)(2,1)} %pad_maximum_fusion.refs_0_, bf16[4,48,384]{2,1,0:T(8,128)(2,1)} %collective-permute-done.7.refs_1_, ...), custom_call_target="tpu_custom_call" | custom-call | tf_op jit(solution)/shard_map/gate_up/pallas_call | solution.py:205
  45.1 2.9 %regroup_down.1.w_ref = bf16[4,1152,384]{2,1,0:T(8,128)(2,1)S(1)} custom-call(bf16[1,1152,4,384]{3,2,1,0:T(4,128)(2,1)} %w_ref.1), custom_call_target="tpu_custom_call" | custom-call | tf_op jit(solution)/shard_map/regroup_down/pallas_call | solution.py:230
  48.0 1.5 %down.1 = (bf16[4,48,384]{2,1,0:T(8,128)(2,1)S(1)}, bf16[4,48,384]{2,1,0:T(8,128)(2,1)S(1)}, bf16[4,48,384]{2,1,0:T(8,128)(2,1)S(1)}, bf16[4,48,384]{2,1,0:T(8,128)(2,1)S(1)}) custom-call(bf16[192,2432]{1,0:T(8,128)(2,1)S(1)} %gate_up.1.part_ref, bf16[192,2432]{1,0:T(8,128)(2,1)S(1)} %collective-permute-done.10.recv_ref, ...), custom_call_target="tpu_custom_call" | custom-call | tf_op jit(solution)/shard_map/down/pallas_call | solution.py:260
  49.5 1.2 %collective-permute-start.11 = (bf16[4,48,384]{2,1,0:T(8,128)(2,1)S(1)}, bf16[4,48,384]{2,1,0:T(8,128)(2,1)S(1)}, u32[]{:S(2)}, u32[]{:S(2)}) collective-permute-start(bf16[4,48,384]{2,1,0:T(8,128)(2,1)S(1)} %get-tuple-element.30), channel_id=1, source_target_pairs={{0,8},{8,0},{16,24},{24,16},{1,9},{9,1},{17,25},{25,17},{2,10},{10... | collective-permute-start | bytes 442376 | tf_op jit(solution)/shard_map/ppermute | solution.py:329
  50.7 1.0 %collective-permute-start.12 = (bf16[4,48,384]{2,1,0:T(8,128)(2,1)S(1)}, bf16[4,48,384]{2,1,0:T(8,128)(2,1)S(1)}, u32[]{:S(2)}, u32[]{:S(2)}) collective-permute-start(bf16[4,48,384]{2,1,0:T(8,128)(2,1)S(1)} %get-tuple-element.31), channel_id=1, source_target_pairs={{0,16},{8,24},{16,0},{24,8},{1,17},{9,25},{17,1},{25,9},{2,18},{10... | collective-permute-start | bytes 442376 | tf_op jit(solution)/shard_map/ppermute | solution.py:329
  51.7 1.4 %collective-permute-start.13 = (bf16[4,48,384]{2,1,0:T(8,128)(2,1)S(1)}, bf16[4,48,384]{2,1,0:T(8,128)(2,1)S(1)}, u32[]{:S(2)}, u32[]{:S(2)}) collective-permute-start(bf16[4,48,384]{2,1,0:T(8,128)(2,1)S(1)} %get-tuple-element.32), channel_id=1, source_target_pairs={{0,24},{8,16},{16,8},{24,0},{1,25},{9,17},{17,9},{25,1},{2,26},{10... | collective-permute-start | bytes 442376 | tf_op jit(solution)/shard_map/ppermute | solution.py:329
  53.1 3.2 %collective-permute-done.11.refs_1_ = bf16[4,48,384]{2,1,0:T(8,128)(2,1)S(1)} collective-permute-done((bf16[4,48,384]{2,1,0:T(8,128)(2,1)S(1)}, bf16[4,48,384]{2,1,0:T(8,128)(2,1)S(1)}, u32[]{:S(2)}, u32[]{:S(2)}) %collective-permute-start.11) | collective-permute-done | bytes 147488 | tf_op jit(solution)/shard_map/ppermute | solution.py:329
  56.2 2.2 %collective-permute-done.12.refs_2_ = bf16[4,48,384]{2,1,0:T(8,128)(2,1)S(1)} collective-permute-done((bf16[4,48,384]{2,1,0:T(8,128)(2,1)S(1)}, bf16[4,48,384]{2,1,0:T(8,128)(2,1)S(1)}, u32[]{:S(2)}, u32[]{:S(2)}) %collective-permute-start.12) | collective-permute-done | bytes 147488 | tf_op jit(solution)/shard_map/ppermute | solution.py:329
  58.4 1.6 %collective-permute-done.13.refs_3_ = bf16[4,48,384]{2,1,0:T(8,128)(2,1)S(1)} collective-permute-done((bf16[4,48,384]{2,1,0:T(8,128)(2,1)S(1)}, bf16[4,48,384]{2,1,0:T(8,128)(2,1)S(1)}, u32[]{:S(2)}, u32[]{:S(2)}) %collective-permute-start.13) | collective-permute-done | bytes 147488 | tf_op jit(solution)/shard_map/ppermute | solution.py:329
  60.2 2.1 %collective-permute-start.14 = (bf16[48,384]{1,0:T(8,128)(2,1)S(1)}, bf16[48,384]{1,0:T(8,128)(2,1)S(1)}, u32[]{:S(2)}, u32[]{:S(2)}) collective-permute-start(bf16[48,384]{1,0:T(8,128)(2,1)S(1)} %get-tuple-element.34), channel_id=1, source_target_pairs={{0,2},{2,0},{4,6},{6,4},{1,3},{3,1},{5,7},{7,5},{8,10},{10,8},{12,... | collective-permute-start | bytes 110600 | tf_op jit(solution)/shard_map/ppermute | solution.py:329
  62.3 0.9 %collective-permute-start.15 = (bf16[48,384]{1,0:T(8,128)(2,1)S(1)}, bf16[48,384]{1,0:T(8,128)(2,1)S(1)}, u32[]{:S(2)}, u32[]{:S(2)}) collective-permute-start(bf16[48,384]{1,0:T(8,128)(2,1)S(1)} %get-tuple-element.35), channel_id=1, source_target_pairs={{0,4},{2,6},{4,0},{6,2},{1,5},{3,7},{5,1},{7,3},{8,12},{10,14},{12... | collective-permute-start | bytes 110600 | tf_op jit(solution)/shard_map/ppermute | solution.py:329
  63.2 1.5 %collective-permute-start.16 = (bf16[48,384]{1,0:T(8,128)(2,1)S(1)}, bf16[48,384]{1,0:T(8,128)(2,1)S(1)}, u32[]{:S(2)}, u32[]{:S(2)}) collective-permute-start(bf16[48,384]{1,0:T(8,128)(2,1)S(1)} %get-tuple-element.36), channel_id=1, source_target_pairs={{0,6},{2,4},{4,2},{6,0},{1,7},{3,5},{5,3},{7,1},{8,14},{10,12},{12... | collective-permute-start | bytes 110600 | tf_op jit(solution)/shard_map/ppermute | solution.py:329
  64.7 2.8 %collective-permute-done.15.refs_1_ = bf16[48,384]{1,0:T(8,128)(2,1)S(1)} collective-permute-done((bf16[48,384]{1,0:T(8,128)(2,1)S(1)}, bf16[48,384]{1,0:T(8,128)(2,1)S(1)}, u32[]{:S(2)}, u32[]{:S(2)}) %collective-permute-start.15) | collective-permute-done | bytes 36896 | tf_op jit(solution)/shard_map/ppermute | solution.py:329
  67.5 1.4 %collective-permute-done.16.refs_2_ = bf16[48,384]{1,0:T(8,128)(2,1)S(1)} collective-permute-done((bf16[48,384]{1,0:T(8,128)(2,1)S(1)}, bf16[48,384]{1,0:T(8,128)(2,1)S(1)}, u32[]{:S(2)}, u32[]{:S(2)}) %collective-permute-start.16) | collective-permute-done | bytes 36896 | tf_op jit(solution)/shard_map/ppermute | solution.py:329
  (32 shorter events, 5.2 us)
Async XLA Ops:
  0.6 1.9 %copy-start.1 = (bf16[24,4,128,128]{3,2,1,0:T(8,128)(2,1)S(1)}, bf16[24,4,128,128]{3,2,1,0:T(8,128)(2,1)}, u32[]{:S(2)}) copy-start(bf16[24,4,128,128]{3,2,1,0:T(8,128)(2,1)} %s_ref.1) | copy-start | bytes 9437188
  2.5 0.8 %copy-start.2 = (bf16[24,2,512]{2,1,0:T(2,128)(2,1)S(1)}, bf16[24,2,512]{2,1,0:T(2,128)(2,1)}, u32[]{:S(2)}) copy-start(bf16[24,2,512]{2,1,0:T(2,128)(2,1)} %q_ref.1) | copy-start | bytes 147460
  3.3 0.8 %copy-start.3 = (bf16[24,2,512]{2,1,0:T(2,128)(2,1)S(1)}, bf16[24,2,512]{2,1,0:T(2,128)(2,1)}, u32[]{:S(2)}) copy-start(bf16[24,2,512]{2,1,0:T(2,128)(2,1)} %k_ref.1) | copy-start | bytes 147460
  4.1 0.8 %copy-start.4 = (bf16[24,2,512]{2,1,0:T(2,128)(2,1)S(1)}, bf16[24,2,512]{2,1,0:T(2,128)(2,1)}, u32[]{:S(2)}) copy-start(bf16[24,2,512]{2,1,0:T(2,128)(2,1)} %v_ref.1) | copy-start | bytes 147460
  4.9 0.7 copy-start.6
  5.6 0.7 copy-start.9
  6.3 18.3 %copy-start.5 = (bf16[24,2,384]{2,1,0:T(2,128)(2,1)S(1)}, bf16[24,2,384]{2,1,0:T(2,128)(2,1)}, u32[]{:S(2)}) copy-start(bf16[24,2,384]{2,1,0:T(2,128)(2,1)} %residual_ref.1) | copy-start | bytes 110596
  6.3 34.4 %copy-start = (bf16[1,4,384,1152]{3,2,1,0:T(8,128)(2,1)S(1)}, bf16[1,4,384,1152]{3,2,1,0:T(8,128)(2,1)}, u32[]{:S(2)}) copy-start(bf16[1,4,384,1152]{3,2,1,0:T(8,128)(2,1)} %wg_ref.1) | copy-start | bytes 10616836
  11.6 1.5 %collective-permute-start = (bf16[4,48,384]{2,1,0:T(8,128)(2,1)S(1)}, bf16[4,48,384]{2,1,0:T(8,128)(2,1)S(1)}, u32[]{:S(2)}, u32[]{:S(2)}) collective-permute-start(bf16[4,48,384]{2,1,0:T(8,128)(2,1)S(1)} %get-tuple-element.22), channel_id=1, source_target_pairs={{0,1},{1,0},{2,3},{3,2},{4,5},{5,4},{6,7},{7,6},{8,9},{9,8},{10,11... | collective-permute-start | bytes 442376 | tf_op jit(solution)/shard_map/ppermute | solution.py:329
  13.2 5.6 %collective-permute-start.1 = (bf16[48,384]{1,0:T(8,128)(2,1)S(1)}, bf16[48,384]{1,0:T(8,128)(2,1)S(1)}, u32[]{:S(2)}, u32[]{:S(2)}) collective-permute-start(bf16[48,384]{1,0:T(8,128)(2,1)S(1)} %get-tuple-element.24), channel_id=1, source_target_pairs={{0,2},{2,0},{4,6},{6,4},{1,3},{3,1},{5,7},{7,5},{8,10},{10,8},{12,... | collective-permute-start | bytes 110600 | tf_op jit(solution)/shard_map/ppermute | solution.py:329
  16.2 5.6 %collective-permute-start.2 = (bf16[48,384]{1,0:T(8,128)(2,1)S(1)}, bf16[48,384]{1,0:T(8,128)(2,1)S(1)}, u32[]{:S(2)}, u32[]{:S(2)}) collective-permute-start(bf16[48,384]{1,0:T(8,128)(2,1)S(1)} %get-tuple-element.25), channel_id=1, source_target_pairs={{0,4},{2,6},{4,0},{6,2},{1,5},{3,7},{5,1},{7,3},{8,12},{10,14},{12... | collective-permute-start | bytes 110600 | tf_op jit(solution)/shard_map/ppermute | solution.py:329
  18.8 5.8 %collective-permute-start.3 = (bf16[48,384]{1,0:T(8,128)(2,1)S(1)}, bf16[48,384]{1,0:T(8,128)(2,1)S(1)}, u32[]{:S(2)}, u32[]{:S(2)}) collective-permute-start(bf16[48,384]{1,0:T(8,128)(2,1)S(1)} %get-tuple-element.26), channel_id=1, source_target_pairs={{0,6},{2,4},{4,2},{6,0},{1,7},{3,5},{5,3},{7,1},{8,14},{10,12},{12... | collective-permute-start | bytes 110600 | tf_op jit(solution)/shard_map/ppermute | solution.py:329
  25.2 5.8 %collective-permute-start.6 = (bf16[48,384]{1,0:T(8,128)(2,1)S(1)}, bf16[48,384]{1,0:T(8,128)(2,1)S(1)}, u32[]{:S(2)}, u32[]{:S(2)}) collective-permute-start(bf16[48,384]{1,0:T(8,128)(2,1)S(1)} %get-tuple-element.28), channel_id=1, source_target_pairs={{0,6},{2,4},{4,2},{6,0},{1,7},{3,5},{5,3},{7,1},{8,14},{10,12},{12... | collective-permute-start | bytes 110600 | tf_op jit(solution)/shard_map/ppermute | solution.py:329
  25.7 5.3 %collective-permute-start.5 = (bf16[48,384]{1,0:T(8,128)(2,1)S(1)}, bf16[48,384]{1,0:T(8,128)(2,1)S(1)}, u32[]{:S(2)}, u32[]{:S(2)}) collective-permute-start(bf16[48,384]{1,0:T(8,128)(2,1)S(1)} %get-tuple-element.28), channel_id=1, source_target_pairs={{0,4},{2,6},{4,0},{6,2},{1,5},{3,7},{5,1},{7,3},{8,12},{10,14},{12... | collective-permute-start | bytes 110600 | tf_op jit(solution)/shard_map/ppermute | solution.py:329
  25.7 5.8 %collective-permute-start.4 = (bf16[48,384]{1,0:T(8,128)(2,1)S(1)}, bf16[48,384]{1,0:T(8,128)(2,1)S(1)}, u32[]{:S(2)}, u32[]{:S(2)}) collective-permute-start(bf16[48,384]{1,0:T(8,128)(2,1)S(1)} %get-tuple-element.28), channel_id=1, source_target_pairs={{0,2},{2,0},{4,6},{6,4},{1,3},{3,1},{5,7},{7,5},{8,10},{10,8},{12,... | collective-permute-start | bytes 110600 | tf_op jit(solution)/shard_map/ppermute | solution.py:329
  32.2 6.5 %collective-permute-start.9 = (bf16[4,48,384]{2,1,0:T(8,128)(2,1)}, bf16[4,48,384]{2,1,0:T(8,128)(2,1)}, u32[]{:S(2)}, u32[]{:S(2)}) collective-permute-start(bf16[4,48,384]{2,1,0:T(8,128)(2,1)} %pad_maximum_fusion.refs_0_), channel_id=1, source_target_pairs={{0,24},{8,16},{16,8},{24,0},{1,25},{9,17},{17,9},{25,1},{2,26},{10... | collective-permute-start | bytes 442376 | tf_op jit(solution)/shard_map/ppermute | solution.py:329
  34.7 5.7 %collective-permute-start.8 = (bf16[4,48,384]{2,1,0:T(8,128)(2,1)}, bf16[4,48,384]{2,1,0:T(8,128)(2,1)}, u32[]{:S(2)}, u32[]{:S(2)}) collective-permute-start(bf16[4,48,384]{2,1,0:T(8,128)(2,1)} %pad_maximum_fusion.refs_0_), channel_id=1, source_target_pairs={{0,16},{8,24},{16,0},{24,8},{1,17},{9,25},{17,1},{25,9},{2,18},{10... | collective-permute-start | bytes 442376 | tf_op jit(solution)/shard_map/ppermute | solution.py:329
  35.2 5.5 %collective-permute-start.7 = (bf16[4,48,384]{2,1,0:T(8,128)(2,1)}, bf16[4,48,384]{2,1,0:T(8,128)(2,1)}, u32[]{:S(2)}, u32[]{:S(2)}) collective-permute-start(bf16[4,48,384]{2,1,0:T(8,128)(2,1)} %pad_maximum_fusion.refs_0_), channel_id=1, source_target_pairs={{0,8},{8,0},{16,24},{24,16},{1,9},{9,1},{17,25},{25,17},{2,10},{10... | collective-permute-start | bytes 442376 | tf_op jit(solution)/shard_map/ppermute | solution.py:329
  45.0 3.0 %collective-permute-start.10 = (bf16[192,2432]{1,0:T(8,128)(2,1)S(1)}, bf16[192,2432]{1,0:T(8,128)(2,1)S(1)}, u32[]{:S(2)}, u32[]{:S(2)}) collective-permute-start(bf16[192,2432]{1,0:T(8,128)(2,1)S(1)} %gate_up.1.part_ref), channel_id=1, source_target_pairs={{0,1},{1,0},{2,3},{3,2},{4,5},{5,4},{6,7},{7,6},{8,9},{9,8},{10,11... | collective-permute-start | bytes 2801672 | tf_op jit(solution)/shard_map/ppermute | solution.py:329
  48.0 11.9 %copy-start.7 = (s32[24,2,2]{0,2,1:T(2,128)S(1)}, s32[24,2,2]{0,2,1:T(2,128)}, u32[]{:S(2)}) copy-start(s32[24,2,2]{0,2,1:T(2,128)} %param.23) | copy-start | bytes 1156
  48.0 11.9 %copy-start.8 = (f32[24,2,2]{0,2,1:T(2,128)S(1)}, f32[24,2,2]{0,2,1:T(2,128)}, u32[]{:S(2)}) copy-start(f32[24,2,2]{0,2,1:T(2,128)} %param.24) | copy-start | bytes 1156
  49.5 6.7 %collective-permute-start.11 = (bf16[4,48,384]{2,1,0:T(8,128)(2,1)S(1)}, bf16[4,48,384]{2,1,0:T(8,128)(2,1)S(1)}, u32[]{:S(2)}, u32[]{:S(2)}) collective-permute-start(bf16[4,48,384]{2,1,0:T(8,128)(2,1)S(1)} %get-tuple-element.30), channel_id=1, source_target_pairs={{0,8},{8,0},{16,24},{24,16},{1,9},{9,1},{17,25},{25,17},{2,10},{10... | collective-permute-start | bytes 442376 | tf_op jit(solution)/shard_map/ppermute | solution.py:329
  50.7 7.7 %collective-permute-start.12 = (bf16[4,48,384]{2,1,0:T(8,128)(2,1)S(1)}, bf16[4,48,384]{2,1,0:T(8,128)(2,1)S(1)}, u32[]{:S(2)}, u32[]{:S(2)}) collective-permute-start(bf16[4,48,384]{2,1,0:T(8,128)(2,1)S(1)} %get-tuple-element.31), channel_id=1, source_target_pairs={{0,16},{8,24},{16,0},{24,8},{1,17},{9,25},{17,1},{25,9},{2,18},{10... | collective-permute-start | bytes 442376 | tf_op jit(solution)/shard_map/ppermute | solution.py:329
  51.7 8.2 %collective-permute-start.13 = (bf16[4,48,384]{2,1,0:T(8,128)(2,1)S(1)}, bf16[4,48,384]{2,1,0:T(8,128)(2,1)S(1)}, u32[]{:S(2)}, u32[]{:S(2)}) collective-permute-start(bf16[4,48,384]{2,1,0:T(8,128)(2,1)S(1)} %get-tuple-element.32), channel_id=1, source_target_pairs={{0,24},{8,16},{16,8},{24,0},{1,25},{9,17},{17,9},{25,1},{2,26},{10... | collective-permute-start | bytes 442376 | tf_op jit(solution)/shard_map/ppermute | solution.py:329
  60.2 4.5 %collective-permute-start.14 = (bf16[48,384]{1,0:T(8,128)(2,1)S(1)}, bf16[48,384]{1,0:T(8,128)(2,1)S(1)}, u32[]{:S(2)}, u32[]{:S(2)}) collective-permute-start(bf16[48,384]{1,0:T(8,128)(2,1)S(1)} %get-tuple-element.34), channel_id=1, source_target_pairs={{0,2},{2,0},{4,6},{6,4},{1,3},{3,1},{5,7},{7,5},{8,10},{10,8},{12,... | collective-permute-start | bytes 110600 | tf_op jit(solution)/shard_map/ppermute | solution.py:329
  62.3 5.2 %collective-permute-start.15 = (bf16[48,384]{1,0:T(8,128)(2,1)S(1)}, bf16[48,384]{1,0:T(8,128)(2,1)S(1)}, u32[]{:S(2)}, u32[]{:S(2)}) collective-permute-start(bf16[48,384]{1,0:T(8,128)(2,1)S(1)} %get-tuple-element.35), channel_id=1, source_target_pairs={{0,4},{2,6},{4,0},{6,2},{1,5},{3,7},{5,1},{7,3},{8,12},{10,14},{12... | collective-permute-start | bytes 110600 | tf_op jit(solution)/shard_map/ppermute | solution.py:329
  63.2 5.8 %collective-permute-start.16 = (bf16[48,384]{1,0:T(8,128)(2,1)S(1)}, bf16[48,384]{1,0:T(8,128)(2,1)S(1)}, u32[]{:S(2)}, u32[]{:S(2)}) collective-permute-start(bf16[48,384]{1,0:T(8,128)(2,1)S(1)} %get-tuple-element.36), channel_id=1, source_target_pairs={{0,6},{2,4},{4,2},{6,0},{1,7},{3,5},{5,3},{7,1},{8,14},{10,12},{12... | collective-permute-start | bytes 110600 | tf_op jit(solution)/shard_map/ppermute | solution.py:329

commit v2 on v1

v2 whole, which is shorter than its diff:
```python
import functools

import jax
import jax.numpy as jnp
from jax import lax
from jax.experimental import pallas as pl
from jax.experimental.pallas import tpu as pltpu
from jax.sharding import PartitionSpec as P

BF = jnp.bfloat16
F32 = jnp.float32
VMEM_LIMIT = 20 * 1024 * 1024
BIG_LIMIT = 58 * 1024 * 1024


def params(limit=VMEM_LIMIT):
    return pltpu.CompilerParams(vmem_limit_bytes=limit)


def struct(shape, dtype):
    return jax.ShapeDtypeStruct(shape, dtype)


def whole_vmem(count):
    return [pl.BlockSpec(memory_space=pltpu.VMEM)] * count


def cost(flops, size):
    return pl.CostEstimate(flops=flops, bytes_accessed=size, transcendentals=0)


def dot(a, b):
    return jnp.dot(a, b, preferred_element_type=F32)


def attention_kernel(
    slope_hbm, q_hbm, k_hbm, v_hbm, s_hbm, gain_hbm, w_hbm, mine_ref, other_ref,
    slope, q_all, k_all, v_all, states, gain, weight, small_sem, state_sem, weight_sem,
):
    small = [
        pltpu.make_async_copy(source, target, small_sem.at[i])
        for i, (source, target) in enumerate(
            ((q_hbm, q_all), (k_hbm, k_all), (v_hbm, v_all), (gain_hbm, gain), (slope_hbm, slope))
        )
    ]
    requests, tokens, _ = q_all.shape
    heads, size = states.shape[1], states.shape[2]
    block = 8 if requests % 8 == 0 else requests
    blocks = requests // block
    loads = [
        pltpu.make_async_copy(
            s_hbm.at[pl.ds(i * block, block)], states.at[pl.ds(i * block, block)], state_sem.at[i]
        )
        for i in range(blocks)
    ]
    weight_load = pltpu.make_async_copy(w_hbm, weight, weight_sem)
    for copy in small + loads + [weight_load]:
        copy.start()
    for copy in small:
        copy.wait()
    rows = block * tokens
    row = lax.broadcasted_iota(jnp.int32, (rows, size), 0)
    second = row % tokens == 1
    owner = row // tokens
    normed = []
    for i in range(blocks):
        loads[i].wait()
        parts = []
        for h in range(heads):
            at = slice(h * size, (h + 1) * size)
            here = slice(i * block, (i + 1) * block)
            q16 = q_all[here, :, at].reshape(rows, size)
            q = q16.astype(F32)
            k = k_all[here, :, at].reshape(rows, size).astype(F32)
            v = v_all[here, :, at].reshape(rows, size).astype(F32)
            decay = jnp.exp(jnp.full((rows, size), -slope[h], F32))
            read = jnp.zeros((rows, size), F32)
            for r in range(block):
                read = jnp.where(owner == r, dot(q16, states[i * block + r, h]), read)
            k_before = pltpu.roll(k, 1, 0)
            v_before = pltpu.roll(v, 1, 0)
            same = jnp.sum(q * k, -1, keepdims=True)
            cross = jnp.sum(q * k_before, -1, keepdims=True)
            out = jnp.where(second, decay * decay, decay) * read + same * v
            out = out + jnp.where(second, decay * cross * v_before, 0.0)
            out = out * lax.rsqrt(jnp.mean(out * out, -1, keepdims=True) + 1e-06)
            parts.append((out * gain[:, at]).astype(BF))
        normed.append(jnp.concatenate(parts, 1) if heads > 1 else parts[0])
    normed = jnp.concatenate(normed, 0) if blocks > 1 else normed[0]
    weight_load.wait()
    side = lax.axis_index("side")
    groups, _, piece = mine_ref.shape
    for a in range(groups):
        both = dot(normed, weight[:, 2 * a * piece : 2 * (a + 1) * piece])
        low, high = both[:, :piece], both[:, piece:]
        mine_ref[a] = jnp.where(side == 0, low, high)
        other_ref[a] = jnp.where(side == 0, high, low).astype(BF)


def attention(slopes, queries, new_keys, new_values, head_states, gain, out_weight, groups):
    requests, tokens, width = queries.shape
    piece = out_weight.shape[1] // (2 * groups)
    rows = requests * tokens
    vec = pltpu.VMEM(queries.shape, BF)
    return pl.pallas_call(
        attention_kernel,
        in_specs=[pl.BlockSpec(memory_space=pltpu.HBM)] * 7,
        out_specs=whole_vmem(2),
        out_shape=[struct((groups, rows, piece), F32), struct((groups, rows, piece), BF)],
        scratch_shapes=[
            pltpu.SMEM(slopes.shape, F32), vec, vec, vec,
            pltpu.VMEM(head_states.shape, BF),
            pltpu.VMEM(gain.shape, F32),
            pltpu.VMEM(out_weight.shape, BF),
            pltpu.SemaphoreType.DMA((5,)),
            pltpu.SemaphoreType.DMA((requests,)),
            pltpu.SemaphoreType.DMA,
        ],
        compiler_params=params(BIG_LIMIT),
        name="attention",
    )(slopes, queries, new_keys, new_values, head_states, gain, out_weight)


def state_kernel(slope_ref, k_ref, v_ref, s_ref, after_ref, so_ref, done_ref):
    del after_ref
    done_ref[...] = jnp.zeros_like(done_ref)
    requests, tokens, _ = k_ref.shape
    heads, size = s_ref.shape[1], s_ref.shape[2]
    rows = requests * tokens
    row = lax.broadcasted_iota(jnp.int32, (rows, size), 0)
    second = row % tokens == 1
    owner = row // tokens
    for h in range(heads):
        at = slice(h * size, (h + 1) * size)
        k16 = k_ref[:, :, at].reshape(rows, size)
        v = v_ref[:, :, at].reshape(rows, size).astype(F32)
        decay = jnp.exp(jnp.full((rows, size), -slope_ref[h], F32))
        weighted = jnp.where(second, v, decay * v)
        spread = jnp.concatenate(
            [jnp.where(owner == r, weighted, 0.0).astype(BF) for r in range(requests)], 1
        )
        update = lax.dot_general(
            k16, spread, (((0,), (0,)), ((), ())), preferred_element_type=F32
        )
        keep = jnp.exp(jnp.full((size, size), -2.0 * slope_ref[h], F32))
        for r in range(requests):
            so_ref[r, h] = (
                keep * s_ref[r, h].astype(F32) + update[:, r * size : (r + 1) * size]
            ).astype(BF)


def new_state(slopes, new_keys, new_values, head_states, after):
    requests, tokens, width = new_keys.shape
    heads, size = head_states.shape[1:3]
    block = 8 if requests % 8 == 0 else requests
    vec = pl.BlockSpec((block, tokens, width), lambda i: (i, 0, 0))
    state = pl.BlockSpec((block, heads, size, size), lambda i: (i, 0, 0, 0))
    return pl.pallas_call(
        state_kernel,
        grid=(requests // block,),
        in_specs=[
            pl.BlockSpec(memory_space=pltpu.SMEM), vec, vec, state,
            pl.BlockSpec(memory_space=pl.ANY),
        ],
        out_specs=[state, pl.BlockSpec((8, 128), lambda i: (0, 0))],
        out_shape=[struct(head_states.shape, BF), struct((8, 128), F32)],
        compiler_params=params(),
        cost_estimate=cost(10**8, 8 * 10**6),
        name="new_state",
    )(slopes, new_keys, new_values, head_states, after)


def hold_kernel(x_ref, out_ref):
    out_ref[...] = x_ref[...]


def hold(x):
    return pl.pallas_call(
        hold_kernel,
        in_specs=whole_vmem(1),
        out_specs=pl.BlockSpec(memory_space=pltpu.VMEM),
        out_shape=struct(x.shape, x.dtype),
        compiler_params=params(),
        cost_estimate=cost(10**5, 10**6),
        name="hold",
    )(x)


def split_kernel(mine_ref, recv_ref, own_ref, *send_refs):
    me = lax.axis_index("heads")
    own_ref[...] = mine_ref[me].astype(F32) + recv_ref[me].astype(F32)
    for k, send_ref in zip(range(len(send_refs), 0, -1), send_refs):
        at = me ^ k
        send_ref[...] = (mine_ref[at].astype(F32) + recv_ref[at].astype(F32)).astype(BF)


def split(mine, recv):
    groups, rows, piece = mine.shape
    return pl.pallas_call(
        split_kernel,
        in_specs=whole_vmem(2),
        out_specs=whole_vmem(groups),
        out_shape=[struct((rows, piece), F32)] + [struct((rows, piece), BF)] * (groups - 1),
        compiler_params=params(),
        name="split_sum",
    )(mine, recv)


def residual_kernel(residual_ref, after_ref, own_ref, *refs):
    del after_ref
    recv_refs, flat_ref = refs[:-1], refs[-1]
    total = own_ref[...]
    for recv_ref in recv_refs:
        total = total + recv_ref[...].astype(F32)
    total = residual_ref[...].astype(F32).reshape(total.shape) + total
    flat_ref[...] = total.astype(BF)


def add_residual(residual, after, own, recvs):
    return pl.pallas_call(
        residual_kernel,
        in_specs=[whole_vmem(1)[0], pl.BlockSpec(memory_space=pl.ANY)] + whole_vmem(1 + len(recvs)),
        out_specs=pl.BlockSpec(memory_space=pltpu.VMEM),
        out_shape=struct(own.shape, BF),
        compiler_params=params(),
        name="add_residual",
    )(residual, after, own, *recvs)


def reshape_kernel(flat_ref, out_ref):
    out_ref[...] = flat_ref[...].reshape(out_ref.shape)


def by_request(flat, shape):
    return pl.pallas_call(
        reshape_kernel,
        in_specs=whole_vmem(1),
        out_specs=pl.BlockSpec(memory_space=pltpu.VMEM),
        out_shape=struct(shape, BF),
        compiler_params=params(),
        cost_estimate=cost(10**5, 10**6),
        name="by_request",
    )(flat)


def route_kernel(capacity, ids_ref, gates_ref, after_ref, pick_ref, high_ref, low_ref):
    del after_ref
    here = lax.axis_index("dp")
    tokens, choices, requests = ids_ref.shape
    rows, total = pick_ref.shape
    row = lax.broadcasted_iota(jnp.int32, (rows, requests), 0)
    lane = lax.broadcasted_iota(jnp.int32, (rows, requests), 1)
    mine = [(row // tokens == lane) & (row % tokens == s) for s in range(tokens)]
    ids, gates = [], []
    for c in range(choices):
        number, gate = jnp.zeros((rows, requests), jnp.int32), jnp.zeros((rows, requests), F32)
        for s in range(tokens):
            number = number + jnp.where(mine[s], ids_ref[s, c : c + 1, :], 0)
            gate = gate + jnp.where(mine[s], gates_ref[s, c : c + 1, :], 0.0)
        ids.append(jnp.sum(number.astype(F32), -1, keepdims=True).astype(jnp.int32))
        gates.append(jnp.sum(gate, -1, keepdims=True))
    column = lax.broadcasted_iota(jnp.int32, (rows, total), 1)
    expert = here ^ (column // capacity)
    chosen, weight = jnp.zeros((rows, total), F32), jnp.zeros((rows, total), F32)
    for c in range(choices):
        named = ids[c] == expert
        chosen = jnp.where(named, 1.0, chosen)
        weight = jnp.where(named, gates[c], weight)
    earlier = lax.broadcasted_iota(jnp.int32, (rows, rows), 1) < lax.broadcasted_iota(
        jnp.int32, (rows, rows), 0
    )
    place = dot(jnp.where(earlier, 1.0, 0.0).astype(BF), chosen.astype(BF))
    hit = (chosen > 0.5) & (place.astype(jnp.int32) == column % capacity)
    pick_ref[...] = jnp.where(hit, 1.0, 0.0).astype(BF)
    weight = jnp.where(hit, weight, 0.0)
    high = weight.astype(BF)
    high_ref[...] = high
    low_ref[...] = (weight - high.astype(F32)).astype(BF)


def route(ids, gates, after, capacity, count):
    rows = ids.shape[0] * ids.shape[2]
    return pl.pallas_call(
        functools.partial(route_kernel, capacity),
        in_specs=whole_vmem(2) + [pl.BlockSpec(memory_space=pl.ANY)],
        out_specs=whole_vmem(3),
        out_shape=[struct((rows, count * capacity), BF)] * 3,
        compiler_params=params(),
        cost_estimate=cost(10**5, 10**6),
        name="route",
    )(ids, gates, after)


def dispatch_kernel(count, pick_ref, *refs):
    x_refs, out_refs = refs[:-count], refs[-count:]
    capacity = out_refs[0].shape[0] // len(x_refs)
    picked = [
        lax.dot_general(
            pick_ref[...], x_ref[...], (((0,), (0,)), ((), ())), preferred_element_type=F32
        )
        for x_ref in x_refs
    ]
    for k, out_ref in zip((0, *range(count - 1, 0, -1)), out_refs):
        rows = [x[k * capacity : (k + 1) * capacity] for x in picked]
        out_ref[...] = jnp.concatenate(rows, 0).astype(BF)


def dispatch(pick, xs, count):
    piece = xs[0].shape[1]
    rows = len(xs) * pick.shape[1] // count
    return pl.pallas_call(
        functools.partial(dispatch_kernel, count),
        in_specs=whole_vmem(1 + len(xs)),
        out_specs=whole_vmem(count),
        out_shape=[struct((rows, piece), BF)] * count,
        compiler_params=params(),
        name="dispatch",
    )(pick, *xs)


def gate_up_kernel(gain_ref, wg_ref, wu_ref, after_ref, *refs):
    del after_ref
    x_refs, (out_ref, placed) = refs[:-2], refs[-2:]
    me, side = lax.axis_index("heads"), lax.axis_index("side")
    groups, total, piece = placed.shape
    hidden = wg_ref.shape[3]
    capacity = total // len(x_refs)
    squares = jnp.zeros((total, 1), F32)
    xs = [x_ref[...].astype(F32) for x_ref in x_refs]
    for k in range(groups):
        at = me ^ k
        x = jnp.concatenate([x[k * capacity : (k + 1) * capacity] for x in xs], 0)
        squares = squares + jnp.sum(x * x, -1, keepdims=True)
        placed[at] = (x * gain_ref[pl.ds(at * 2 + side, 1), :]).astype(BF)
    lhs = jnp.concatenate([placed[a] for a in range(groups)], 1)
    wide = 384 if hidden % 384 == 0 else hidden
    for n in range(0, hidden, wide):
        rhs = wg_ref[0, :, :, n : n + wide].reshape(groups * piece, wide)
        out_ref[:, n : n + wide] = dot(lhs, rhs).astype(BF)
    for n in range(0, hidden, wide):
        rhs = wu_ref[0, :, :, n : n + wide].reshape(groups * piece, wide)
        out_ref[:, hidden + n : hidden + n + wide] = dot(lhs, rhs).astype(BF)
    coarse = squares.astype(BF)
    fine = (squares - coarse.astype(F32)).astype(BF)
    lane = lax.broadcasted_iota(jnp.int32, (total, 128), 1)
    extra = jnp.where(lane == 0, coarse.astype(F32), jnp.where(lane == 1, fine.astype(F32), 0.0))
    out_ref[:, 2 * hidden :] = extra.astype(BF)


def gate_up(gain, w_gate, w_up, after, xs):
    _, groups, piece, hidden = w_gate.shape
    total = xs[0].shape[0] // groups * len(xs)
    return pl.pallas_call(
        gate_up_kernel,
        in_specs=whole_vmem(3) + [pl.BlockSpec(memory_space=pl.ANY)] + whole_vmem(len(xs)),
        out_specs=pl.BlockSpec(memory_space=pltpu.VMEM),
        out_shape=struct((total, 2 * hidden + 128), BF),
        scratch_shapes=[pltpu.VMEM((groups, total, piece), BF)],
        compiler_params=params(),
        name="gate_up",
    )(gain, w_gate, w_up, after, *xs)


def regroup_kernel(w_ref, after_ref, out_ref):
    del after_ref
    count = w_ref.shape[1]
    step = 64 if count % 64 == 0 else 32

    def one(i, carry):
        at = pl.ds(pl.multiple_of(i * step, step), step)
        out_ref[:, at, :] = w_ref[0, at].swapaxes(0, 1)
        return carry

    lax.fori_loop(0, count // step, one, 0)


def regroup(w_down, after):
    _, hidden, groups, piece = w_down.shape
    return pl.pallas_call(
        regroup_kernel,
        in_specs=[whole_vmem(1)[0], pl.BlockSpec(memory_space=pl.ANY)],
        out_specs=pl.BlockSpec(memory_space=pltpu.VMEM),
        out_shape=struct((groups, hidden, piece), BF),
        compiler_params=params(),
        cost_estimate=cost(10**8, 7 * 10**6),
        name="regroup_down",
    )(w_down, after)


def down_kernel(width, part_ref, recv_ref, w_ref, *out_refs):
    groups, hidden, piece = w_ref.shape
    capacity = part_ref.shape[0] // len(out_refs)
    extra = part_ref[:, 2 * hidden :].astype(F32) + recv_ref[:, 2 * hidden :].astype(F32)
    squares = extra[:, 0:1] + extra[:, 1:2]
    scale = lax.rsqrt(squares / width + 1e-06)
    gate = (part_ref[:, :hidden].astype(F32) + recv_ref[:, :hidden].astype(F32)) * scale
    up = (
        part_ref[:, hidden : 2 * hidden].astype(F32) + recv_ref[:, hidden : 2 * hidden].astype(F32)
    ) * scale
    act = (gate / (1.0 + jnp.exp(-gate)) * up).astype(BF)
    outs = [dot(act, w_ref[a]) for a in range(groups)]
    for d, out_ref in zip((0, *range(len(out_refs) - 1, 0, -1)), out_refs):
        rows = [out[d * capacity : (d + 1) * capacity] for out in outs]
        out_ref[...] = jnp.concatenate(rows, 0).astype(BF)


def down(width, part, recv, weights, count):
    groups, hidden, piece = weights.shape
    rows = part.shape[0] // count * groups
    return pl.pallas_call(
        functools.partial(down_kernel, width),
        in_specs=whole_vmem(3),
        out_specs=whole_vmem(count),
        out_shape=[struct((rows, piece), BF)] * count,
        compiler_params=params(),
        name="down",
    )(part, recv, weights)


def combine_kernel(count, high_ref, low_ref, *refs):
    y_refs, out_refs, total = refs[:count], refs[count:-1], refs[-1]
    me = lax.axis_index("heads")
    groups = total.shape[0]
    capacity = y_refs[0].shape[0] // groups
    ys = [y_ref[...].astype(F32) for y_ref in y_refs]
    for a in range(groups):
        y = jnp.concatenate([y[a * capacity : (a + 1) * capacity] for y in ys], 0).astype(BF)
        total[a] = dot(high_ref[...], y) + dot(low_ref[...], y)
    for k, out_ref in zip((0, *range(groups - 1, 0, -1)), out_refs):
        out_ref[...] = total[me ^ k].astype(out_ref.dtype)


def combine(high, low, ys, groups):
    rows, piece = high.shape[0], ys[0].shape[1]
    return pl.pallas_call(
        functools.partial(combine_kernel, len(ys)),
        in_specs=whole_vmem(2 + len(ys)),
        out_specs=whole_vmem(groups),
        out_shape=[struct((rows, piece), F32)] + [struct((rows, piece), BF)] * (groups - 1),
        scratch_shapes=[pltpu.VMEM((groups, rows, piece), F32)],
        compiler_params=params(),
        name="combine",
    )(high, low, *ys)


def finish_kernel(own_ref, *refs):
    recv_refs, out_ref = refs[:-1], refs[-1]
    total = own_ref[...]
    for recv_ref in recv_refs:
        total = total + recv_ref[...].astype(F32)
    out_ref[...] = total.astype(BF).reshape(out_ref.shape)


def finish(own, recvs, shape):
    return pl.pallas_call(
        finish_kernel,
        in_specs=whole_vmem(1 + len(recvs)),
        out_specs=pl.BlockSpec(memory_space=pltpu.VMEM),
        out_shape=struct(shape, BF),
        compiler_params=params(),
        name="finish",
    )(own, *recvs)


def swap(x, axis, k):
    size = lax.axis_size(axis)
    return lax.ppermute(x, axis, [(i, i ^ k) for i in range(size)])


def swaps(sends, axis):
    return [swap(x, axis, k) for k, x in zip(range(len(sends), 0, -1), sends)]


def local(
    queries, new_keys, new_values, head_states, slopes, head_gain, out_weight, residual,
    norm_gain, expert_ids, expert_gates, w_gate, w_up, w_down,
):
    groups, count = lax.axis_size("heads"), lax.axis_size("dp")
    width = norm_gain.shape[0]
    piece = residual.shape[2]
    mine, other = attention(
        slopes, queries, new_keys, new_values, head_states,
        head_gain.reshape(1, -1), out_weight, groups,
    )
    own, *sends = split(hold(mine), swap(other, "side", 1))
    recvs = swaps(sends, "heads")
    state_out, done = new_state(slopes, new_keys, new_values, head_states, own)
    flat = add_residual(residual, done, own, recvs)
    resid_out = by_request(flat, residual.shape)
    capacity = max(2, 3 * expert_ids.shape[2] * flat.shape[0] // (2 * count))
    pick, high, low = route(
        jnp.transpose(expert_ids, (1, 2, 0)), jnp.transpose(expert_gates, (1, 2, 0)), done,
        capacity, count,
    )
    gathered = [flat] + swaps([flat] * (groups - 1), "heads")[::-1]
    own, *sends = dispatch(pick, gathered, count)
    xs = [own] + swaps(sends, "dp")[::-1]
    weights = regroup(w_down, own)
    part = gate_up(norm_gain.reshape(-1, piece), w_gate, w_up, weights, xs)
    own, *sends = down(width, part, swap(part, "side", 1), weights, count)
    ys = [own] + swaps(sends, "dp")[::-1]
    own, *sends = combine(high, low, ys, groups)
    return state_out, resid_out, finish(own, swaps(sends, "heads"), residual.shape)


def solution(mesh):
    return jax.shard_map(
        local,
        mesh=mesh,
        in_specs=(
            P("dp", None, ("heads", "side")),
            P("dp", None, ("heads", "side")),
            P("dp", None, ("heads", "side")),
            P("dp", ("heads", "side"), None, None),
            P(("heads", "side")),
            P(("heads", "side")),
            P(("heads", "side"), None),
            P("dp", None, ("heads", "side")),
            P(),
            P("dp", None, None),
            P("dp", None, None),
            P("dp", None, "side", "heads"),
            P("dp", None, "side", "heads"),
            P("dp", "heads", None, "side"),
        ),
        out_specs=(
            P("dp", ("heads", "side"), None, None),
            P("dp", None, ("heads", "side")),
            P("dp", None, ("heads", "side")),
        ),
        check_vma=False,
    )
```

time: 70 us -> 56 us (0.80)
  waiting for transfers between devices: 24 us -> 15.4 us
  local copies, waits for them, and re-layouts: 6.34 us -> 3.01 us
  Pallas kernels: 15.7 us -> 14.4 us
    ppermute x17, waiting for transfers between devices: 24 us -> 15.4 us  [swap(): return lax.ppermute(x, axis, [(i, i ^ k) for i in range(size)])]
    unnamed x20 -> x24, local copies, waits for them, and re-layouts: 5.63 us -> 3 us
    pallas_call x4 -> x9, Pallas kernels: 13.3 us -> 12.1 us  [the longest x1 4.75 us: attention(): pl.pallas_call(attention_kernel, in_specs=[pl.BlockSpec(memory_space=pltp...]
    reshape x1, local copies, waits for them, and re-layouts: 0.71 us -> 0.01 us  [local(): part = gate_up(norm_gain.reshape(-1, piece), w_gate, w_up, weights, xs)]
  transfers between devices with their start and end apart: 17 -> 17, of which waited for: 13 -> 13; matrix products, arithmetic and copies ran while one was open for 1% -> 0% of each run, Pallas kernels for 4% -> 9%
where the time goes in v2:
time: 56 us; the launch traced here: 55.9 us
  starting transfers between devices  22.3 us (40%)
  waiting for transfers between devices  15.4 us (28%)
  Pallas kernels  14.4 us (26%)
  local copies, waits for them, and re-layouts  3.01 us (5%)
  between operations  0.79 us (1%)
    ppermute x17, starting transfers between devices, swap(): return lax.ppermute(x, axis, [(i, i ^ k) for i in range(size)])  22.3 us
    ppermute x17, waiting for transfers between devices, swap(): return lax.ppermute(x, axis, [(i, i ^ k) for i in range(size)])  15.4 us
    pallas_call x1, Pallas kernels, attention(): pl.pallas_call(attention_kernel, in_specs=[pl.BlockSpec(memory_space=pltp...  4.75 us
    pallas_call x1, Pallas kernels, new_state(): pl.pallas_call(state_kernel, grid=(requests // block,), in_specs=[pl.Bloc...  3.44 us
    unnamed x24, local copies, waits for them, and re-layouts  3 us
    pallas_call x1, Pallas kernels, gate_up(): pl.pallas_call(gate_up_kernel, in_specs=whole_vmem(3) + [pl.BlockSpec(mem...  1.75 us
    pallas_call x1, Pallas kernels, down(): pl.pallas_call(functools.partial(down_kernel, width), in_specs=whole_vmem...  1.24 us
  transfers between devices with their start and end apart: 17, of which 13 were waited for; matrix products, arithmetic and copies ran while one was open for 0% of the time, Pallas kernels for 9%

profile of v2, /device:TPU:0, one launch (start us, length us, event | category | flops | bytes accessed | tf_op | source)
XLA Modules:
  0.0 55.9 jit_solution(8467269174566344428)
XLA Ops:
  0.7 4.7 %attention.1 = (f32[4,48,384]{2,1,0:T(8,128)}, bf16[4,48,384]{2,1,0:T(8,128)(2,1)}) custom-call(f32[4]{0:T(128)} %slope_ref.1, bf16[24,2,512]{2,1,0:T(2,128)(2,1)} %q_hbm.1, bf16[24,2,512]{2,1,0:T(2,128)(2,1)} %k_ref.1, bf16[24,2,512]{2,1,0:T(2,128)(2,1)} %v_ref.1, bf16[24,4,128,128]{3,2,1,0:T(8,128)(2,1)} %s_ref.1, f32[1,512]{1,0:T(1,128)} %bitcast.5, ...), custom_call_target="tpu_custom_call" | custom-call | tf_op jit(solution)/shard_map/attention/pallas_call | solution.py:105
  5.5 0.5 collective-permute-start
  6.0 1.0 %copy-done.4 = f32[4,48,384]{2,1,0:T(8,128)S(1)} copy-done((f32[4,48,384]{2,1,0:T(8,128)S(1)}, f32[4,48,384]{2,1,0:T(8,128)}, u32[]{:S(2)}) %copy-start.4) | copy-done | bytes 294936
  7.2 5.0 %collective-permute-start.1 = (bf16[48,384]{1,0:T(8,128)(2,1)S(1)}, bf16[48,384]{1,0:T(8,128)(2,1)S(1)}, u32[]{:S(2)}, u32[]{:S(2)}) collective-permute-start(bf16[48,384]{1,0:T(8,128)(2,1)S(1)} %get-tuple-element.31), channel_id=1, source_target_pairs={{0,6},{2,4},{4,2},{6,0},{1,7},{3,5},{5,3},{7,1},{8,14},{10,12},{12... | collective-permute-start | bytes 110600 | tf_op jit(solution)/shard_map/ppermute | solution.py:467
  12.3 0.6 %collective-permute-start.3 = (bf16[48,384]{1,0:T(8,128)(2,1)S(1)}, bf16[48,384]{1,0:T(8,128)(2,1)S(1)}, u32[]{:S(2)}, u32[]{:S(2)}) collective-permute-start(bf16[48,384]{1,0:T(8,128)(2,1)S(1)} %get-tuple-element.33), channel_id=1, source_target_pairs={{0,2},{2,0},{4,6},{6,4},{1,3},{3,1},{5,7},{7,5},{8,10},{10,8},{12,... | collective-permute-start | bytes 110600 | tf_op jit(solution)/shard_map/ppermute | solution.py:467
  12.9 3.4 %new_state.1 = (bf16[24,4,128,128]{3,2,1,0:T(8,128)(2,1)}, f32[8,128]{1,0:T(8,128)S(1)}) custom-call(f32[4]{0:T(128)S(1)} %copy-done.10, bf16[24,2,512]{2,1,0:T(2,128)(2,1)S(1)} %copy-done.5, bf16[24,2,512]{2,1,0:T(2,128)(2,1)S(1)} %copy-done.6, bf16[24,4,128,128]{3,2,1,0:T(8,128)(2,1)S(1)} %copy-done, f32[48,384]{1,0:T(8,128)S(1)} %get-tuple-element.28.after_ref.own_ref), custom_call_target="tpu_custom_call" | custom-call | flops 100000000 | bytes 8000000 | tf_op jit(solution)/shard_map/new_state/pallas_call | solution.py:158
  16.4 0.8 %collective-permute-done.2.refs_1_ = bf16[48,384]{1,0:T(8,128)(2,1)S(1)} collective-permute-done((bf16[48,384]{1,0:T(8,128)(2,1)S(1)}, bf16[48,384]{1,0:T(8,128)(2,1)S(1)}, u32[]{:S(2)}, u32[]{:S(2)}) %collective-permute-start.2) | collective-permute-done | bytes 36896 | tf_op jit(solution)/shard_map/ppermute | solution.py:467
  17.2 3.1 %collective-permute-start.6 = (bf16[48,384]{1,0:T(8,128)(2,1)S(1)}, bf16[48,384]{1,0:T(8,128)(2,1)S(1)}, u32[]{:S(2)}, u32[]{:S(2)}) collective-permute-start(bf16[48,384]{1,0:T(8,128)(2,1)S(1)} %add_residual.1.flat_ref.refs_0_), channel_id=1, source_target_pairs={{0,6},{2,4},{4,2},{6,0},{1,7},{3,5},{5,3},{7,1},{8,14},{10,12},{12... | collective-permute-start | bytes 110600 | tf_op jit(solution)/shard_map/ppermute | solution.py:467
  20.3 1.4 %collective-permute-start.4 = (bf16[48,384]{1,0:T(8,128)(2,1)S(1)}, bf16[48,384]{1,0:T(8,128)(2,1)S(1)}, u32[]{:S(2)}, u32[]{:S(2)}) collective-permute-start(bf16[48,384]{1,0:T(8,128)(2,1)S(1)} %add_residual.1.flat_ref.refs_0_), channel_id=1, source_target_pairs={{0,2},{2,0},{4,6},{6,4},{1,3},{3,1},{5,7},{7,5},{8,10},{10,8},{12,... | collective-permute-start | bytes 110600 | tf_op jit(solution)/shard_map/ppermute | solution.py:467
  21.9 1.1 %collective-permute-done.6.refs_3_ = bf16[48,384]{1,0:T(8,128)(2,1)S(1)} collective-permute-done((bf16[48,384]{1,0:T(8,128)(2,1)S(1)}, bf16[48,384]{1,0:T(8,128)(2,1)S(1)}, u32[]{:S(2)}, u32[]{:S(2)}) %collective-permute-start.6) | collective-permute-done | bytes 36896 | tf_op jit(solution)/shard_map/ppermute | solution.py:467
  23.0 2.1 %collective-permute-done.5.refs_2_ = bf16[48,384]{1,0:T(8,128)(2,1)S(1)} collective-permute-done((bf16[48,384]{1,0:T(8,128)(2,1)S(1)}, bf16[48,384]{1,0:T(8,128)(2,1)S(1)}, u32[]{:S(2)}, u32[]{:S(2)}) %collective-permute-start.5) | collective-permute-done | bytes 36896 | tf_op jit(solution)/shard_map/ppermute | solution.py:467
  25.5 1.6 %collective-permute-start.7 = (bf16[144,384]{1,0:T(8,128)(2,1)S(1)}, bf16[144,384]{1,0:T(8,128)(2,1)S(1)}, u32[]{:S(2)}, u32[]{:S(2)}) collective-permute-start(bf16[144,384]{1,0:T(8,128)(2,1)S(1)} %get-tuple-element.38), channel_id=1, source_target_pairs={{0,8},{8,0},{16,24},{24,16},{1,9},{9,1},{17,25},{25,17},{2,10},{10... | collective-permute-start | bytes 331784 | tf_op jit(solution)/shard_map/ppermute | solution.py:467
  27.0 1.5 %collective-permute-start.8 = (bf16[144,384]{1,0:T(8,128)(2,1)S(1)}, bf16[144,384]{1,0:T(8,128)(2,1)S(1)}, u32[]{:S(2)}, u32[]{:S(2)}) collective-permute-start(bf16[144,384]{1,0:T(8,128)(2,1)S(1)} %get-tuple-element.39), channel_id=1, source_target_pairs={{0,16},{8,24},{16,0},{24,8},{1,17},{9,25},{17,1},{25,9},{2,18},{10... | collective-permute-start | bytes 331784 | tf_op jit(solution)/shard_map/ppermute | solution.py:467
  28.5 0.5 collective-permute-start.9
  29.0 2.0 %copy-done.3 = bf16[1,1152,4,384]{3,2,1,0:T(4,128)(2,1)S(1)} copy-done((bf16[1,1152,4,384]{3,2,1,0:T(4,128)(2,1)S(1)}, bf16[1,1152,4,384]{3,2,1,0:T(4,128)(2,1)}, u32[]{:S(2)}) %copy-start.3) | copy-done | bytes 3538968
  31.0 0.9 %regroup_down.1.after_ref.w_ref = bf16[4,1152,384]{2,1,0:T(8,128)(2,1)S(1)} custom-call(bf16[1,1152,4,384]{3,2,1,0:T(4,128)(2,1)S(1)} %copy-done.3, bf16[144,384]{1,0:T(8,128)(2,1)S(1)} %get-tuple-element.37.after_ref.refs_0_), custom_call_target="tpu_custom_call" | custom-call | flops 100000000 | bytes 7000000 | tf_op jit(solution)/shard_map/regroup_down/pallas_call | solution.py:379
  32.3 1.9 %collective-permute-done.9.refs_3_ = bf16[144,384]{1,0:T(8,128)(2,1)S(1)} collective-permute-done((bf16[144,384]{1,0:T(8,128)(2,1)S(1)}, bf16[144,384]{1,0:T(8,128)(2,1)S(1)}, u32[]{:S(2)}, u32[]{:S(2)}) %collective-permute-start.9) | collective-permute-done | bytes 110624 | tf_op jit(solution)/shard_map/ppermute | solution.py:467
  34.2 1.8 %gate_up.1.part_ref = bf16[144,2432]{1,0:T(8,128)(2,1)S(1)} custom-call(f32[8,384]{1,0:T(8,128)S(1)} %reshape.13.gain_ref, bf16[1,4,384,1152]{3,2,1,0:T(8,128)(2,1)S(1)} %copy-done.1, bf16[1,4,384,1152]{3,2,1,0:T(8,128)(2,1)S(1)} %copy-done.2, bf16[4,1152,384]{2,1,0:T(8,128)(2,1)S(1)} %regroup_down.1.after_ref.w_ref, ...), custom_call_target="tpu_custom_call" | custom-call | tf_op jit(solution)/shard_map/gate_up/pallas_call | solution.py:353
  36.0 2.1 %collective-permute-done.10.recv_ref = bf16[144,2432]{1,0:T(8,128)(2,1)S(1)} collective-permute-done((bf16[144,2432]{1,0:T(8,128)(2,1)S(1)}, bf16[144,2432]{1,0:T(8,128)(2,1)S(1)}, u32[]{:S(2)}, u32[]{:S(2)}) %collective-permute-start.10) | collective-permute-done | bytes 700448 | tf_op jit(solution)/shard_map/ppermute | solution.py:467
  38.2 1.2 %down.1 = (bf16[144,384]{1,0:T(8,128)(2,1)S(1)}, bf16[144,384]{1,0:T(8,128)(2,1)S(1)}, bf16[144,384]{1,0:T(8,128)(2,1)S(1)}, bf16[144,384]{1,0:T(8,128)(2,1)S(1)}) custom-call(bf16[144,2432]{1,0:T(8,128)(2,1)S(1)} %gate_up.1.part_ref, bf16[144,2432]{1,0:T(8,128)(2,1)S(1)} %collective-permute-done.10.recv_ref, ...), custom_call_target="tpu_custom_call" | custom-call | tf_op jit(solution)/shard_map/down/pallas_call | solution.py:410
  39.4 1.5 %collective-permute-start.11 = (bf16[144,384]{1,0:T(8,128)(2,1)S(1)}, bf16[144,384]{1,0:T(8,128)(2,1)S(1)}, u32[]{:S(2)}, u32[]{:S(2)}) collective-permute-start(bf16[144,384]{1,0:T(8,128)(2,1)S(1)} %get-tuple-element.42), channel_id=1, source_target_pairs={{0,8},{8,0},{16,24},{24,16},{1,9},{9,1},{17,25},{25,17},{2,10},{10... | collective-permute-start | bytes 331784 | tf_op jit(solution)/shard_map/ppermute | solution.py:467
  40.9 1.5 %collective-permute-start.12 = (bf16[144,384]{1,0:T(8,128)(2,1)S(1)}, bf16[144,384]{1,0:T(8,128)(2,1)S(1)}, u32[]{:S(2)}, u32[]{:S(2)}) collective-permute-start(bf16[144,384]{1,0:T(8,128)(2,1)S(1)} %get-tuple-element.43), channel_id=1, source_target_pairs={{0,16},{8,24},{16,0},{24,8},{1,17},{9,25},{17,1},{25,9},{2,18},{10... | collective-permute-start | bytes 331784 | tf_op jit(solution)/shard_map/ppermute | solution.py:467
  42.4 0.6 %collective-permute-start.13 = (bf16[144,384]{1,0:T(8,128)(2,1)S(1)}, bf16[144,384]{1,0:T(8,128)(2,1)S(1)}, u32[]{:S(2)}, u32[]{:S(2)}) collective-permute-start(bf16[144,384]{1,0:T(8,128)(2,1)S(1)} %get-tuple-element.44), channel_id=1, source_target_pairs={{0,24},{8,16},{16,8},{24,0},{1,25},{9,17},{17,9},{25,1},{2,26},{10... | collective-permute-start | bytes 331784 | tf_op jit(solution)/shard_map/ppermute | solution.py:467
  43.0 1.6 %collective-permute-done.11.refs_1_ = bf16[144,384]{1,0:T(8,128)(2,1)S(1)} collective-permute-done((bf16[144,384]{1,0:T(8,128)(2,1)S(1)}, bf16[144,384]{1,0:T(8,128)(2,1)S(1)}, u32[]{:S(2)}, u32[]{:S(2)}) %collective-permute-start.11) | collective-permute-done | bytes 110624 | tf_op jit(solution)/shard_map/ppermute | solution.py:467
  44.6 2.6 %collective-permute-done.12.refs_2_ = bf16[144,384]{1,0:T(8,128)(2,1)S(1)} collective-permute-done((bf16[144,384]{1,0:T(8,128)(2,1)S(1)}, bf16[144,384]{1,0:T(8,128)(2,1)S(1)}, u32[]{:S(2)}, u32[]{:S(2)}) %collective-permute-start.12) | collective-permute-done | bytes 110624 | tf_op jit(solution)/shard_map/ppermute | solution.py:467
  47.1 0.9 %collective-permute-done.13.refs_3_ = bf16[144,384]{1,0:T(8,128)(2,1)S(1)} collective-permute-done((bf16[144,384]{1,0:T(8,128)(2,1)S(1)}, bf16[144,384]{1,0:T(8,128)(2,1)S(1)}, u32[]{:S(2)}, u32[]{:S(2)}) %collective-permute-start.13) | collective-permute-done | bytes 110624 | tf_op jit(solution)/shard_map/ppermute | solution.py:467
  48.4 1.7 %collective-permute-start.14 = (bf16[48,384]{1,0:T(8,128)(2,1)S(1)}, bf16[48,384]{1,0:T(8,128)(2,1)S(1)}, u32[]{:S(2)}, u32[]{:S(2)}) collective-permute-start(bf16[48,384]{1,0:T(8,128)(2,1)S(1)} %get-tuple-element.46), channel_id=1, source_target_pairs={{0,6},{2,4},{4,2},{6,0},{1,7},{3,5},{5,3},{7,1},{8,14},{10,12},{12... | collective-permute-start | bytes 110600 | tf_op jit(solution)/shard_map/ppermute | solution.py:467
  50.6 2.3 %collective-permute-start.16 = (bf16[48,384]{1,0:T(8,128)(2,1)S(1)}, bf16[48,384]{1,0:T(8,128)(2,1)S(1)}, u32[]{:S(2)}, u32[]{:S(2)}) collective-permute-start(bf16[48,384]{1,0:T(8,128)(2,1)S(1)} %get-tuple-element.48), channel_id=1, source_target_pairs={{0,2},{2,0},{4,6},{6,4},{1,3},{3,1},{5,7},{7,5},{8,10},{10,8},{12,... | collective-permute-start | bytes 110600 | tf_op jit(solution)/shard_map/ppermute | solution.py:467
  52.9 0.6 %by_request.1 = bf16[24,2,384]{2,1,0:T(2,128)(2,1)} custom-call(bf16[48,384]{1,0:T(8,128)(2,1)S(1)} %add_residual.1.flat_ref.refs_0_), custom_call_target="tpu_custom_call" | custom-call | flops 100000 | bytes 1000000 | tf_op jit(solution)/shard_map/by_request/pallas_call | solution.py:235
  53.5 0.7 %collective-permute-done.14.refs_0_ = bf16[48,384]{1,0:T(8,128)(2,1)S(1)} collective-permute-done((bf16[48,384]{1,0:T(8,128)(2,1)S(1)}, bf16[48,384]{1,0:T(8,128)(2,1)S(1)}, u32[]{:S(2)}, u32[]{:S(2)}) %collective-permute-start.14) | collective-permute-done | bytes 36896 | tf_op jit(solution)/shard_map/ppermute | solution.py:467
  54.2 0.9 %collective-permute-done.15.refs_1_ = bf16[48,384]{1,0:T(8,128)(2,1)S(1)} collective-permute-done((bf16[48,384]{1,0:T(8,128)(2,1)S(1)}, bf16[48,384]{1,0:T(8,128)(2,1)S(1)}, u32[]{:S(2)}, u32[]{:S(2)}) %collective-permute-start.15) | collective-permute-done | bytes 36896 | tf_op jit(solution)/shard_map/ppermute | solution.py:467
  55.2 0.7 %finish.1 = bf16[24,2,384]{2,1,0:T(2,128)(2,1)} custom-call(f32[48,384]{1,0:T(8,128)S(1)} %get-tuple-element.45.own_ref, bf16[48,384]{1,0:T(8,128)(2,1)S(1)} %collective-permute-done.14.refs_0_, bf16[48,384]{1,0:T(8,128)(2,1)S(1)} %collective-permute-done.15.refs_1_, bf16[48,384]{1,0:T(8,128)(2,1)S(1)} %collective-permute-done.16.refs_2_), custom_call_target="tpu_custom_call" | custom-call | tf_op jit(solution)/shard_map/finish/pallas_call | solution.py:455
  (40 shorter events, 2.2 us)
Async XLA Ops:
  0.6 12.3 %copy-start = (bf16[24,4,128,128]{3,2,1,0:T(8,128)(2,1)S(1)}, bf16[24,4,128,128]{3,2,1,0:T(8,128)(2,1)}, u32[]{:S(2)}) copy-start(bf16[24,4,128,128]{3,2,1,0:T(8,128)(2,1)} %s_ref.1) | copy-start | bytes 9437188
  0.6 12.3 %copy-start.5 = (bf16[24,2,512]{2,1,0:T(2,128)(2,1)S(1)}, bf16[24,2,512]{2,1,0:T(2,128)(2,1)}, u32[]{:S(2)}) copy-start(bf16[24,2,512]{2,1,0:T(2,128)(2,1)} %k_ref.1) | copy-start | bytes 147460
  0.7 12.3 %copy-start.6 = (bf16[24,2,512]{2,1,0:T(2,128)(2,1)S(1)}, bf16[24,2,512]{2,1,0:T(2,128)(2,1)}, u32[]{:S(2)}) copy-start(bf16[24,2,512]{2,1,0:T(2,128)(2,1)} %v_ref.1) | copy-start | bytes 147460
  0.7 12.3 %copy-start.10 = (f32[4]{0:T(128)S(1)}, f32[4]{0:T(128)}, u32[]{:S(2)}) copy-start(f32[4]{0:T(128)} %slope_ref.1) | copy-start | bytes 52
  0.7 16.5 %copy-start.7 = (bf16[24,2,384]{2,1,0:T(2,128)(2,1)S(1)}, bf16[24,2,384]{2,1,0:T(2,128)(2,1)}, u32[]{:S(2)}) copy-start(bf16[24,2,384]{2,1,0:T(2,128)(2,1)} %residual_ref.1) | copy-start | bytes 110596
  0.7 21.0 %copy-start.9 = (f32[24,2,2]{0,2,1:T(2,128)S(1)}, f32[24,2,2]{0,2,1:T(2,128)}, u32[]{:S(2)}) copy-start(f32[24,2,2]{0,2,1:T(2,128)} %param.24) | copy-start | bytes 1156
  0.7 28.3 %copy-start.11 = (f32[3072]{0:T(1024)S(1)}, f32[3072]{0:T(1024)}, u32[]{:S(2)}) copy-start(f32[3072]{0:T(1024)} %param.22) | copy-start | bytes 36868
  5.5 16.2 %copy-start.8 = (s32[24,2,2]{0,2,1:T(2,128)S(1)}, s32[24,2,2]{0,2,1:T(2,128)}, u32[]{:S(2)}) copy-start(s32[24,2,2]{0,2,1:T(2,128)} %param.23) | copy-start | bytes 1156
  5.5 1.7 %collective-permute-start = (bf16[4,48,384]{2,1,0:T(8,128)(2,1)}, bf16[4,48,384]{2,1,0:T(8,128)(2,1)S(1)}, u32[]{:S(2)}, u32[]{:S(2)}) collective-permute-start(bf16[4,48,384]{2,1,0:T(8,128)(2,1)} %get-tuple-element.27), channel_id=1, source_target_pairs={{0,1},{1,0},{2,3},{3,2},{4,5},{5,4},{6,7},{7,6},{8,9},{9,8},{10,11... | collective-permute-start | bytes 442376 | tf_op jit(solution)/shard_map/ppermute | solution.py:467
  6.0 1.0 %copy-start.4 = (f32[4,48,384]{2,1,0:T(8,128)S(1)}, f32[4,48,384]{2,1,0:T(8,128)}, u32[]{:S(2)}) copy-start(f32[4,48,384]{2,1,0:T(8,128)} %get-tuple-element.26.x_ref) | copy-start | bytes 884740
  7.2 9.1 %collective-permute-start.1 = (bf16[48,384]{1,0:T(8,128)(2,1)S(1)}, bf16[48,384]{1,0:T(8,128)(2,1)S(1)}, u32[]{:S(2)}, u32[]{:S(2)}) collective-permute-start(bf16[48,384]{1,0:T(8,128)(2,1)S(1)} %get-tuple-element.31), channel_id=1, source_target_pairs={{0,6},{2,4},{4,2},{6,0},{1,7},{3,5},{5,3},{7,1},{8,14},{10,12},{12... | collective-permute-start | bytes 110600 | tf_op jit(solution)/shard_map/ppermute | solution.py:467
  12.3 4.9 %collective-permute-start.2 = (bf16[48,384]{1,0:T(8,128)(2,1)S(1)}, bf16[48,384]{1,0:T(8,128)(2,1)S(1)}, u32[]{:S(2)}, u32[]{:S(2)}) collective-permute-start(bf16[48,384]{1,0:T(8,128)(2,1)S(1)} %get-tuple-element.32), channel_id=1, source_target_pairs={{0,4},{2,6},{4,0},{6,2},{1,5},{3,7},{5,1},{7,3},{8,12},{10,14},{12... | collective-permute-start | bytes 110600 | tf_op jit(solution)/shard_map/ppermute | solution.py:467
  12.3 4.9 %collective-permute-start.3 = (bf16[48,384]{1,0:T(8,128)(2,1)S(1)}, bf16[48,384]{1,0:T(8,128)(2,1)S(1)}, u32[]{:S(2)}, u32[]{:S(2)}) collective-permute-start(bf16[48,384]{1,0:T(8,128)(2,1)S(1)} %get-tuple-element.33), channel_id=1, source_target_pairs={{0,2},{2,0},{4,6},{6,4},{1,3},{3,1},{5,7},{7,5},{8,10},{10,8},{12,... | collective-permute-start | bytes 110600 | tf_op jit(solution)/shard_map/ppermute | solution.py:467
  17.2 5.8 %collective-permute-start.6 = (bf16[48,384]{1,0:T(8,128)(2,1)S(1)}, bf16[48,384]{1,0:T(8,128)(2,1)S(1)}, u32[]{:S(2)}, u32[]{:S(2)}) collective-permute-start(bf16[48,384]{1,0:T(8,128)(2,1)S(1)} %add_residual.1.flat_ref.refs_0_), channel_id=1, source_target_pairs={{0,6},{2,4},{4,2},{6,0},{1,7},{3,5},{5,3},{7,1},{8,14},{10,12},{12... | collective-permute-start | bytes 110600 | tf_op jit(solution)/shard_map/ppermute | solution.py:467
  20.3 4.9 %collective-permute-start.5 = (bf16[48,384]{1,0:T(8,128)(2,1)S(1)}, bf16[48,384]{1,0:T(8,128)(2,1)S(1)}, u32[]{:S(2)}, u32[]{:S(2)}) collective-permute-start(bf16[48,384]{1,0:T(8,128)(2,1)S(1)} %add_residual.1.flat_ref.refs_0_), channel_id=1, source_target_pairs={{0,4},{2,6},{4,0},{6,2},{1,5},{3,7},{5,1},{7,3},{8,12},{10,14},{12... | collective-permute-start | bytes 110600 | tf_op jit(solution)/shard_map/ppermute | solution.py:467
  20.3 4.9 %collective-permute-start.4 = (bf16[48,384]{1,0:T(8,128)(2,1)S(1)}, bf16[48,384]{1,0:T(8,128)(2,1)S(1)}, u32[]{:S(2)}, u32[]{:S(2)}) collective-permute-start(bf16[48,384]{1,0:T(8,128)(2,1)S(1)} %add_residual.1.flat_ref.refs_0_), channel_id=1, source_target_pairs={{0,2},{2,0},{4,6},{6,4},{1,3},{3,1},{5,7},{7,5},{8,10},{10,8},{12,... | collective-permute-start | bytes 110600 | tf_op jit(solution)/shard_map/ppermute | solution.py:467
  25.5 6.5 %collective-permute-start.7 = (bf16[144,384]{1,0:T(8,128)(2,1)S(1)}, bf16[144,384]{1,0:T(8,128)(2,1)S(1)}, u32[]{:S(2)}, u32[]{:S(2)}) collective-permute-start(bf16[144,384]{1,0:T(8,128)(2,1)S(1)} %get-tuple-element.38), channel_id=1, source_target_pairs={{0,8},{8,0},{16,24},{24,16},{1,9},{9,1},{17,25},{25,17},{2,10},{10... | collective-permute-start | bytes 331784 | tf_op jit(solution)/shard_map/ppermute | solution.py:467
  27.0 5.2 %collective-permute-start.8 = (bf16[144,384]{1,0:T(8,128)(2,1)S(1)}, bf16[144,384]{1,0:T(8,128)(2,1)S(1)}, u32[]{:S(2)}, u32[]{:S(2)}) collective-permute-start(bf16[144,384]{1,0:T(8,128)(2,1)S(1)} %get-tuple-element.39), channel_id=1, source_target_pairs={{0,16},{8,24},{16,0},{24,8},{1,17},{9,25},{17,1},{25,9},{2,18},{10... | collective-permute-start | bytes 331784 | tf_op jit(solution)/shard_map/ppermute | solution.py:467
  28.5 5.6 %collective-permute-start.9 = (bf16[144,384]{1,0:T(8,128)(2,1)S(1)}, bf16[144,384]{1,0:T(8,128)(2,1)S(1)}, u32[]{:S(2)}, u32[]{:S(2)}) collective-permute-start(bf16[144,384]{1,0:T(8,128)(2,1)S(1)} %get-tuple-element.40), channel_id=1, source_target_pairs={{0,24},{8,16},{16,8},{24,0},{1,25},{9,17},{17,9},{25,1},{2,26},{10... | collective-permute-start | bytes 331784 | tf_op jit(solution)/shard_map/ppermute | solution.py:467
  29.0 2.0 %copy-start.3 = (bf16[1,1152,4,384]{3,2,1,0:T(4,128)(2,1)S(1)}, bf16[1,1152,4,384]{3,2,1,0:T(4,128)(2,1)}, u32[]{:S(2)}) copy-start(bf16[1,1152,4,384]{3,2,1,0:T(4,128)(2,1)} %w_ref.1) | copy-start | bytes 10616836
  31.0 3.2 %copy-start.1 = (bf16[1,4,384,1152]{3,2,1,0:T(8,128)(2,1)S(1)}, bf16[1,4,384,1152]{3,2,1,0:T(8,128)(2,1)}, u32[]{:S(2)}) copy-start(bf16[1,4,384,1152]{3,2,1,0:T(8,128)(2,1)} %wg_ref.1) | copy-start | bytes 10616836
  31.0 3.2 %copy-start.2 = (bf16[1,4,384,1152]{3,2,1,0:T(8,128)(2,1)S(1)}, bf16[1,4,384,1152]{3,2,1,0:T(8,128)(2,1)}, u32[]{:S(2)}) copy-start(bf16[1,4,384,1152]{3,2,1,0:T(8,128)(2,1)} %wu_ref.1) | copy-start | bytes 10616836
  36.0 2.2 %collective-permute-start.10 = (bf16[144,2432]{1,0:T(8,128)(2,1)S(1)}, bf16[144,2432]{1,0:T(8,128)(2,1)S(1)}, u32[]{:S(2)}, u32[]{:S(2)}) collective-permute-start(bf16[144,2432]{1,0:T(8,128)(2,1)S(1)} %gate_up.1.part_ref), channel_id=1, source_target_pairs={{0,1},{1,0},{2,3},{3,2},{4,5},{5,4},{6,7},{7,6},{8,9},{9,8},{10,11... | collective-permute-start | bytes 2101256 | tf_op jit(solution)/shard_map/ppermute | solution.py:467
  39.4 5.2 %collective-permute-start.11 = (bf16[144,384]{1,0:T(8,128)(2,1)S(1)}, bf16[144,384]{1,0:T(8,128)(2,1)S(1)}, u32[]{:S(2)}, u32[]{:S(2)}) collective-permute-start(bf16[144,384]{1,0:T(8,128)(2,1)S(1)} %get-tuple-element.42), channel_id=1, source_target_pairs={{0,8},{8,0},{16,24},{24,16},{1,9},{9,1},{17,25},{25,17},{2,10},{10... | collective-permute-start | bytes 331784 | tf_op jit(solution)/shard_map/ppermute | solution.py:467
  40.9 6.3 %collective-permute-start.12 = (bf16[144,384]{1,0:T(8,128)(2,1)S(1)}, bf16[144,384]{1,0:T(8,128)(2,1)S(1)}, u32[]{:S(2)}, u32[]{:S(2)}) collective-permute-start(bf16[144,384]{1,0:T(8,128)(2,1)S(1)} %get-tuple-element.43), channel_id=1, source_target_pairs={{0,16},{8,24},{16,0},{24,8},{1,17},{9,25},{17,1},{25,9},{2,18},{10... | collective-permute-start | bytes 331784 | tf_op jit(solution)/shard_map/ppermute | solution.py:467
  42.4 5.7 %collective-permute-start.13 = (bf16[144,384]{1,0:T(8,128)(2,1)S(1)}, bf16[144,384]{1,0:T(8,128)(2,1)S(1)}, u32[]{:S(2)}, u32[]{:S(2)}) collective-permute-start(bf16[144,384]{1,0:T(8,128)(2,1)S(1)} %get-tuple-element.44), channel_id=1, source_target_pairs={{0,24},{8,16},{16,8},{24,0},{1,25},{9,17},{17,9},{25,1},{2,26},{10... | collective-permute-start | bytes 331784 | tf_op jit(solution)/shard_map/ppermute | solution.py:467
  48.4 5.8 %collective-permute-start.14 = (bf16[48,384]{1,0:T(8,128)(2,1)S(1)}, bf16[48,384]{1,0:T(8,128)(2,1)S(1)}, u32[]{:S(2)}, u32[]{:S(2)}) collective-permute-start(bf16[48,384]{1,0:T(8,128)(2,1)S(1)} %get-tuple-element.46), channel_id=1, source_target_pairs={{0,6},{2,4},{4,2},{6,0},{1,7},{3,5},{5,3},{7,1},{8,14},{10,12},{12... | collective-permute-start | bytes 110600 | tf_op jit(solution)/shard_map/ppermute | solution.py:467
  50.2 5.0 %collective-permute-start.15 = (bf16[48,384]{1,0:T(8,128)(2,1)S(1)}, bf16[48,384]{1,0:T(8,128)(2,1)S(1)}, u32[]{:S(2)}, u32[]{:S(2)}) collective-permute-start(bf16[48,384]{1,0:T(8,128)(2,1)S(1)} %get-tuple-element.47), channel_id=1, source_target_pairs={{0,4},{2,6},{4,0},{6,2},{1,5},{3,7},{5,1},{7,3},{8,12},{10,14},{12... | collective-permute-start | bytes 110600 | tf_op jit(solution)/shard_map/ppermute | solution.py:467
  50.6 4.6 %collective-permute-start.16 = (bf16[48,384]{1,0:T(8,128)(2,1)S(1)}, bf16[48,384]{1,0:T(8,128)(2,1)S(1)}, u32[]{:S(2)}, u32[]{:S(2)}) collective-permute-start(bf16[48,384]{1,0:T(8,128)(2,1)S(1)} %get-tuple-element.48), channel_id=1, source_target_pairs={{0,2},{2,0},{4,6},{6,4},{1,3},{3,1},{5,7},{7,5},{8,10},{10,8},{12,... | collective-permute-start | bytes 110600 | tf_op jit(solution)/shard_map/ppermute | solution.py:467

commit v3 on v2

--- a/solution.py
+++ b/solution.py
@@ -21,6 +21,18 @@
     return jax.ShapeDtypeStruct(shape, dtype)
 
 
+def in_vmem(shape, dtype):
+    return pltpu.VMEM(shape, dtype)
+
+
+def from_hbm(x):
+    return pltpu.with_memory_space_constraint(x, pltpu.HBM)
+
+
+def hbm_specs(count):
+    return [pl.BlockSpec(memory_space=pltpu.HBM)] * count
+
+
 def whole_vmem(count):
     return [pl.BlockSpec(memory_space=pltpu.VMEM)] * count
 
@@ -33,9 +45,43 @@
     return jnp.dot(a, b, preferred_element_type=F32)
 
 
+def load_columns(w_hbm, weight, sems, side):
+    groups, _, piece = weight.shape
+    if groups == 1:
+        return [pltpu.make_async_copy(w_hbm, weight.at[0], sems.at[0])]
+    return [
+        pltpu.make_async_copy(
+            w_hbm.at[:, pl.ds(pl.multiple_of((2 * a + side) * piece, 128), piece)],
+            weight.at[a],
+            sems.at[a],
+        )
+        for a in range(groups)
+    ]
+
+
+def columns_shape(out_weight, groups):
+    rows, width = out_weight.shape
+    piece = width // (2 * groups)
+    return (groups, rows, piece) if piece % 128 == 0 else (1, rows, width)
+
+
+def project_columns(loads, weight, normed, side, out_ref):
+    groups, _, piece = out_ref.shape
+    if len(loads) == groups:
+        for a, copy in enumerate(loads):
+            copy.wait()
+            out_ref[a] = dot(normed, weight[a]).astype(out_ref.dtype)
+        return
+    loads[0].wait()
+    for a in range(groups):
+        both = dot(normed, weight[0, :, 2 * a * piece : 2 * (a + 1) * piece])
+        out = jnp.where(side == 0, both[:, :piece], both[:, piece:])
+        out_ref[a] = out.astype(out_ref.dtype)
+
+
 def attention_kernel(
-    slope_hbm, q_hbm, k_hbm, v_hbm, s_hbm, gain_hbm, w_hbm, mine_ref, other_ref,
-    slope, q_all, k_all, v_all, states, gain, weight, small_sem, state_sem, weight_sem,
+    slope_hbm, q_hbm, k_hbm, v_hbm, s_hbm, gain_hbm, w_hbm, other_ref, normed_ref, states,
+    slope, q_all, k_all, v_all, gain, weight, small_sem, state_sem, weight_sem,
 ):
     small = [
         pltpu.make_async_copy(source, target, small_sem.at[i])
@@ -53,8 +99,8 @@
         )
         for i in range(blocks)
     ]
-    weight_load = pltpu.make_async_copy(w_hbm, weight, weight_sem)
-    for copy in small + loads + [weight_load]:
+    weight_loads = load_columns(w_hbm, weight, weight_sem, 1 - lax.axis_index("side"))
+    for copy in small + loads + weight_loads:
         copy.start()
     for copy in small:
         copy.wait()
@@ -87,14 +133,8 @@
             parts.append((out * gain[:, at]).astype(BF))
         normed.append(jnp.concatenate(parts, 1) if heads > 1 else parts[0])
     normed = jnp.concatenate(normed, 0) if blocks > 1 else normed[0]
-    weight_load.wait()
-    side = lax.axis_index("side")
-    groups, _, piece = mine_ref.shape
-    for a in range(groups):
-        both = dot(normed, weight[:, 2 * a * piece : 2 * (a + 1) * piece])
-        low, high = both[:, :piece], both[:, piece:]
-        mine_ref[a] = jnp.where(side == 0, low, high)
-        other_ref[a] = jnp.where(side == 0, high, low).astype(BF)
+    normed_ref[...] = normed
+    project_columns(weight_loads, weight, normed, 1 - lax.axis_index("side"), other_ref)
 
 
 def attention(slopes, queries, new_keys, new_values, head_states, gain, out_weight, groups):
@@ -102,88 +142,109 @@
     piece = out_weight.shape[1] // (2 * groups)
     rows = requests * tokens
     vec = pltpu.VMEM(queries.shape, BF)
+    operands = (slopes, queries, new_keys, new_values, head_states, gain, out_weight)
     return pl.pallas_call(
         attention_kernel,
-        in_specs=[pl.BlockSpec(memory_space=pltpu.HBM)] * 7,
-        out_specs=whole_vmem(2),
-        out_shape=[struct((groups, rows, piece), F32), struct((groups, rows, piece), BF)],
+        in_specs=hbm_specs(7),
+        out_specs=whole_vmem(3),
+        out_shape=[
+            in_vmem((groups, rows, piece), BF),
+            in_vmem((rows, width), BF),
+            in_vmem(head_states.shape, BF),
+        ],
         scratch_shapes=[
             pltpu.SMEM(slopes.shape, F32), vec, vec, vec,
-            pltpu.VMEM(head_states.shape, BF),
             pltpu.VMEM(gain.shape, F32),
-            pltpu.VMEM(out_weight.shape, BF),
+            pltpu.VMEM(columns_shape(out_weight, groups), BF),
             pltpu.SemaphoreType.DMA((5,)),
             pltpu.SemaphoreType.DMA((requests,)),
-            pltpu.SemaphoreType.DMA,
+            pltpu.SemaphoreType.DMA((groups,)),
         ],
-        compiler_params=params(BIG_LIMIT),
+        compiler_params=params(),
         name="attention",
-    )(slopes, queries, new_keys, new_values, head_states, gain, out_weight)
-
-
-def state_kernel(slope_ref, k_ref, v_ref, s_ref, after_ref, so_ref, done_ref):
+    )(*[from_hbm(x) if x.size > 1 else x for x in operands])
+
+
+def project_kernel(w_hbm, normed_ref, mine_ref, weight, weight_sem):
+    loads = load_columns(w_hbm, weight, weight_sem, lax.axis_index("side"))
+    for copy in loads:
+        copy.start()
+    normed = normed_ref[...]
+    project_columns(loads, weight, normed, lax.axis_index("side"), mine_ref)
+
+
+def project(out_weight, normed, groups):
+    piece = out_weight.shape[1] // (2 * groups)
+    return pl.pallas_call(
+        project_kernel,
+        in_specs=hbm_specs(1) + whole_vmem(1),
+        out_specs=whole_vmem(1)[0],
+        out_shape=in_vmem((groups, normed.shape[0], piece), F32),
+        scratch_shapes=[
+            pltpu.VMEM(columns_shape(out_weight, groups), BF),
+            pltpu.SemaphoreType.DMA((groups,)),
+        ],
+        compiler_params=params(),
+        cost_estimate=cost(10**8, 2 * 10**6),
+        name="project",
+    )(from_hbm(out_weight), normed)
+
+
+def state_kernel(slope_ref, k_ref, v_ref, s_ref, after_ref, so_hbm, done_ref, out, sems):
     del after_ref
     done_ref[...] = jnp.zeros_like(done_ref)
     requests, tokens, _ = k_ref.shape
     heads, size = s_ref.shape[1], s_ref.shape[2]
-    rows = requests * tokens
+    block = 8 if requests % 8 == 0 else requests
+    rows = block * tokens
     row = lax.broadcasted_iota(jnp.int32, (rows, size), 0)
     second = row % tokens == 1
     owner = row // tokens
-    for h in range(heads):
-        at = slice(h * size, (h + 1) * size)
-        k16 = k_ref[:, :, at].reshape(rows, size)
-        v = v_ref[:, :, at].reshape(rows, size).astype(F32)
-        decay = jnp.exp(jnp.full((rows, size), -slope_ref[h], F32))
-        weighted = jnp.where(second, v, decay * v)
-        spread = jnp.concatenate(
-            [jnp.where(owner == r, weighted, 0.0).astype(BF) for r in range(requests)], 1
-        )
-        update = lax.dot_general(
-            k16, spread, (((0,), (0,)), ((), ())), preferred_element_type=F32
-        )
-        keep = jnp.exp(jnp.full((size, size), -2.0 * slope_ref[h], F32))
-        for r in range(requests):
-            so_ref[r, h] = (
-                keep * s_ref[r, h].astype(F32) + update[:, r * size : (r + 1) * size]
-            ).astype(BF)
+    stores = []
+    for i in range(requests // block):
+        here = slice(i * block, (i + 1) * block)
+        for h in range(heads):
+            at = slice(h * size, (h + 1) * size)
+            k16 = k_ref[here, :, at].reshape(rows, size)
+            v = v_ref[here, :, at].reshape(rows, size).astype(F32)
+            decay = jnp.exp(jnp.full((rows, size), -slope_ref[h], F32))
+            weighted = jnp.where(second, v, decay * v)
+            spread = jnp.concatenate(
+                [jnp.where(owner == r, weighted, 0.0).astype(BF) for r in range(block)], 1
+            )
+            update = lax.dot_general(
+                k16, spread, (((0,), (0,)), ((), ())), preferred_element_type=F32
+            )
+            keep = jnp.exp(jnp.full((size, size), -2.0 * slope_ref[h], F32))
+            for r in range(block):
+                out[i * block + r, h] = (
+                    keep * s_ref[i * block + r, h].astype(F32)
+                    + update[:, r * size : (r + 1) * size]
+                ).astype(BF)
+        part = pl.ds(i * block, block)
+        stores.append(pltpu.make_async_copy(out.at[part], so_hbm.at[part], sems.at[i]))
+        stores[-1].start()
+    for copy in stores:
+        copy.wait()
 
 
 def new_state(slopes, new_keys, new_values, head_states, after):
-    requests, tokens, width = new_keys.shape
-    heads, size = head_states.shape[1:3]
-    block = 8 if requests % 8 == 0 else requests
-    vec = pl.BlockSpec((block, tokens, width), lambda i: (i, 0, 0))
-    state = pl.BlockSpec((block, heads, size, size), lambda i: (i, 0, 0, 0))
     return pl.pallas_call(
         state_kernel,
-        grid=(requests // block,),
         in_specs=[
-            pl.BlockSpec(memory_space=pltpu.SMEM), vec, vec, state,
+            pl.BlockSpec(memory_space=pltpu.SMEM), *whole_vmem(3),
             pl.BlockSpec(memory_space=pl.ANY),
         ],
-        out_specs=[state, pl.BlockSpec((8, 128), lambda i: (0, 0))],
+        out_specs=[*hbm_specs(1), *whole_vmem(1)],
         out_shape=[struct(head_states.shape, BF), struct((8, 128), F32)],
+        scratch_shapes=[
+            pltpu.VMEM(head_states.shape, BF),
+            pltpu.SemaphoreType.DMA((head_states.shape[0],)),
+        ],
         compiler_params=params(),
         cost_estimate=cost(10**8, 8 * 10**6),
         name="new_state",
     )(slopes, new_keys, new_values, head_states, after)
-
-
-def hold_kernel(x_ref, out_ref):
-    out_ref[...] = x_ref[...]
-
-
-def hold(x):
-    return pl.pallas_call(
-        hold_kernel,
-        in_specs=whole_vmem(1),
-        out_specs=pl.BlockSpec(memory_space=pltpu.VMEM),
-        out_shape=struct(x.shape, x.dtype),
-        compiler_params=params(),
-        cost_estimate=cost(10**5, 10**6),
-        name="hold",
-    )(x)
 
 
 def split_kernel(mine_ref, recv_ref, own_ref, *send_refs):
@@ -291,7 +352,8 @@
     )(ids, gates, after)
 
 
-def dispatch_kernel(count, pick_ref, *refs):
+def dispatch_kernel(count, after_ref, pick_ref, *refs):
+    del after_ref
     x_refs, out_refs = refs[:-count], refs[-count:]
     capacity = out_refs[0].shape[0] // len(x_refs)
     picked = [
@@ -305,21 +367,20 @@
         out_ref[...] = jnp.concatenate(rows, 0).astype(BF)
 
 
-def dispatch(pick, xs, count):
+def dispatch(after, pick, xs, count):
     piece = xs[0].shape[1]
     rows = len(xs) * pick.shape[1] // count
     return pl.pallas_call(
         functools.partial(dispatch_kernel, count),
-        in_specs=whole_vmem(1 + len(xs)),
+        in_specs=[pl.BlockSpec(memory_space=pl.ANY)] + whole_vmem(1 + len(xs)),
         out_specs=whole_vmem(count),
         out_shape=[struct((rows, piece), BF)] * count,
         compiler_params=params(),
         name="dispatch",
-    )(pick, *xs)
-
-
-def gate_up_kernel(gain_ref, wg_ref, wu_ref, after_ref, *refs):
-    del after_ref
+    )(after, pick, *xs)
+
+
+def gate_up_kernel(gain_ref, wg_ref, wu_ref, *refs):
     x_refs, (out_ref, placed) = refs[:-2], refs[-2:]
     me, side = lax.axis_index("heads"), lax.axis_index("side")
     groups, total, piece = placed.shape
@@ -331,8 +392,14 @@
         at = me ^ k
         x = jnp.concatenate([x[k * capacity : (k + 1) * capacity] for x in xs], 0)
         squares = squares + jnp.sum(x * x, -1, keepdims=True)
-        placed[at] = (x * gain_ref[pl.ds(at * 2 + side, 1), :]).astype(BF)
-    lhs = jnp.concatenate([placed[a] for a in range(groups)], 1)
+        placed[at] = x.astype(BF)
+    parts = []
+    for a in range(groups):
+        low = gain_ref[:, 2 * a * piece : (2 * a + 1) * piece]
+        high = gain_ref[:, (2 * a + 1) * piece : (2 * a + 2) * piece]
+        gain = jnp.where(side == 0, low, high)
+        parts.append((placed[a].astype(F32) * gain).astype(BF))
+    lhs = jnp.concatenate(parts, 1)
     wide = 384 if hidden % 384 == 0 else hidden
     for n in range(0, hidden, wide):
         rhs = wg_ref[0, :, :, n : n + wide].reshape(groups * piece, wide)
@@ -347,44 +414,81 @@
     out_ref[:, 2 * hidden :] = extra.astype(BF)
 
 
-def gate_up(gain, w_gate, w_up, after, xs):
+def gate_up(gain, w_gate, w_up, xs):
     _, groups, piece, hidden = w_gate.shape
     total = xs[0].shape[0] // groups * len(xs)
     return pl.pallas_call(
         gate_up_kernel,
-        in_specs=whole_vmem(3) + [pl.BlockSpec(memory_space=pl.ANY)] + whole_vmem(len(xs)),
+        in_specs=whole_vmem(3 + len(xs)),
         out_specs=pl.BlockSpec(memory_space=pltpu.VMEM),
         out_shape=struct((total, 2 * hidden + 128), BF),
         scratch_shapes=[pltpu.VMEM((groups, total, piece), BF)],
         compiler_params=params(),
         name="gate_up",
-    )(gain, w_gate, w_up, after, *xs)
-
-
-def regroup_kernel(w_ref, after_ref, out_ref):
+    )(gain, w_gate, w_up, *xs)
+
+
+def regroup_kernel(w_hbm, after_ref, out_ref, weight, sems):
     del after_ref
-    count = w_ref.shape[1]
-    step = 64 if count % 64 == 0 else 32
-
-    def one(i, carry):
-        at = pl.ds(pl.multiple_of(i * step, step), step)
-        out_ref[:, at, :] = w_ref[0, at].swapaxes(0, 1)
-        return carry
-
-    lax.fori_loop(0, count // step, one, 0)
+    count = weight.shape[0]
+    parts = sems.shape[0]
+    size = count // parts
+    loads = [
+        pltpu.make_async_copy(
+            w_hbm.at[0, pl.ds(i * size, size)], weight.at[pl.ds(i * size, size)], sems.at[i]
+        )
+        for i in range(parts)
+    ]
+    for copy in loads:
+        copy.start()
+    step = 48 if size % 48 == 0 else 32 if size % 32 == 0 else size
+    for i, copy in enumerate(loads):
+        copy.wait()
+
+        def one(j, carry, i=i):
+            at = pl.ds(pl.multiple_of(i * size + j * step, 16), step)
+            out_ref[:, at, :] = weight[at].swapaxes(0, 1)
+            return carry
+
+        lax.fori_loop(0, size // step, one, 0)
 
 
 def regroup(w_down, after):
     _, hidden, groups, piece = w_down.shape
+    parts = 4 if hidden % 64 == 0 else 1
     return pl.pallas_call(
         regroup_kernel,
-        in_specs=[whole_vmem(1)[0], pl.BlockSpec(memory_space=pl.ANY)],
-        out_specs=pl.BlockSpec(memory_space=pltpu.VMEM),
-        out_shape=struct((groups, hidden, piece), BF),
+        in_specs=[*hbm_specs(1), pl.BlockSpec(memory_space=pl.ANY)],
+        out_specs=whole_vmem(1)[0],
+        out_shape=in_vmem((groups, hidden, piece), BF),
+        scratch_shapes=[
+            pltpu.VMEM((hidden, groups, piece), BF),
+            pltpu.SemaphoreType.DMA((parts,)),
+        ],
         compiler_params=params(),
         cost_estimate=cost(10**8, 7 * 10**6),
         name="regroup_down",
-    )(w_down, after)
+    )(from_hbm(w_down), after)
+
+
+def load_kernel(w_hbm, after_ref, out_ref, sem):
+    del after_ref
+    copy = pltpu.make_async_copy(w_hbm, out_ref, sem)
+    copy.start()
+    copy.wait()
+
+
+def load(w, after):
+    return pl.pallas_call(
+        load_kernel,
+        in_specs=[*hbm_specs(1), pl.BlockSpec(memory_space=pl.ANY)],
+        out_specs=whole_vmem(1)[0],
+        out_shape=in_vmem(w.shape, w.dtype),
+        scratch_shapes=[pltpu.SemaphoreType.DMA],
+        compiler_params=params(),
+        cost_estimate=cost(10**6, 7 * 10**6),
+        name="load_weight",
+    )(from_hbm(w), after)
 
 
 def down_kernel(width, part_ref, recv_ref, w_ref, *out_refs):
@@ -417,7 +521,8 @@
     )(part, recv, weights)
 
 
-def combine_kernel(count, high_ref, low_ref, *refs):
+def combine_kernel(count, high_ref, low_ref, after_ref, *refs):
+    del after_ref
     y_refs, out_refs, total = refs[:count], refs[count:-1], refs[-1]
     me = lax.axis_index("heads")
     groups = total.shape[0]
@@ -430,17 +535,17 @@
         out_ref[...] = total[me ^ k].astype(out_ref.dtype)
 
 
-def combine(high, low, ys, groups):
+def combine(high, low, after, ys, groups):
     rows, piece = high.shape[0], ys[0].shape[1]
     return pl.pallas_call(
         functools.partial(combine_kernel, len(ys)),
-        in_specs=whole_vmem(2 + len(ys)),
+        in_specs=whole_vmem(2) + [pl.BlockSpec(memory_space=pl.ANY)] + whole_vmem(len(ys)),
         out_specs=whole_vmem(groups),
         out_shape=[struct((rows, piece), F32)] + [struct((rows, piece), BF)] * (groups - 1),
         scratch_shapes=[pltpu.VMEM((groups, rows, piece), F32)],
         compiler_params=params(),
         name="combine",
-    )(high, low, *ys)
+    )(high, low, after, *ys)
 
 
 def finish_kernel(own_ref, *refs):
@@ -477,29 +582,30 @@
 ):
     groups, count = lax.axis_size("heads"), lax.axis_size("dp")
     width = norm_gain.shape[0]
-    piece = residual.shape[2]
-    mine, other = attention(
+    other, normed, states = attention(
         slopes, queries, new_keys, new_values, head_states,
         head_gain.reshape(1, -1), out_weight, groups,
     )
-    own, *sends = split(hold(mine), swap(other, "side", 1))
-    recvs = swaps(sends, "heads")
-    state_out, done = new_state(slopes, new_keys, new_values, head_states, own)
-    flat = add_residual(residual, done, own, recvs)
+    mine = project(out_weight, normed, groups)
+    own, *sends = split(mine, swap(other, "side", 1))
+    weights = regroup(w_down, own)
+    flat = add_residual(residual, weights, own, swaps(sends, "heads"))
     resid_out = by_request(flat, residual.shape)
     capacity = max(2, 3 * expert_ids.shape[2] * flat.shape[0] // (2 * count))
     pick, high, low = route(
-        jnp.transpose(expert_ids, (1, 2, 0)), jnp.transpose(expert_gates, (1, 2, 0)), done,
+        jnp.transpose(expert_ids, (1, 2, 0)), jnp.transpose(expert_gates, (1, 2, 0)), flat,
         capacity, count,
     )
+    w_gate = load(w_gate, flat)
     gathered = [flat] + swaps([flat] * (groups - 1), "heads")[::-1]
-    own, *sends = dispatch(pick, gathered, count)
+    own, *sends = dispatch(w_gate, pick, gathered, count)
+    w_up = load(w_up, own)
     xs = [own] + swaps(sends, "dp")[::-1]
-    weights = regroup(w_down, own)
-    part = gate_up(norm_gain.reshape(-1, piece), w_gate, w_up, weights, xs)
+    part = gate_up(norm_gain.reshape(1, -1), w_gate, w_up, xs)
     own, *sends = down(width, part, swap(part, "side", 1), weights, count)
+    state_out, done = new_state(slopes, new_keys, new_values, states, own)
     ys = [own] + swaps(sends, "dp")[::-1]
-    own, *sends = combine(high, low, ys, groups)
+    own, *sends = combine(high, low, done, ys, groups)
     return state_out, resid_out, finish(own, swaps(sends, "heads"), residual.shape)
 
 

time: 56 us -> 54.1 us (0.966)
  Pallas kernels: 14.4 us -> 20.1 us
  waiting for transfers between devices: 15.4 us -> 11 us
  local copies, waits for them, and re-layouts: 3.01 us -> 0.04 us
    pallas_call x6 -> x8, Pallas kernels: 11.2 us -> 16.9 us  [the longest x2 4.04 us: load(): pl.pallas_call(load_kernel, in_specs=[*hbm_specs(1), pl.BlockSpec(memory_...]
    ppermute x17, waiting for transfers between devices: 15.4 us -> 11 us  [swap(): return lax.ppermute(x, axis, [(i, i ^ k) for i in range(size)])]
    unnamed x24 -> x14, local copies, waits for them, and re-layouts: 3 us -> 0.04 us
  transfers between devices with their start and end apart: 17 -> 17, of which waited for: 13 -> 8; matrix products, arithmetic and copies ran while one was open for 0% -> 0% of each run, Pallas kernels for 9% -> 22%
where the time goes in v3:
time: 54.1 us; the launch traced here: 53.9 us
  starting transfers between devices  21.9 us (40%)
  Pallas kernels  20.1 us (37%)
  waiting for transfers between devices  11 us (20%)
  between operations  0.81 us (1%)
    ppermute x17, starting transfers between devices, swap(): return lax.ppermute(x, axis, [(i, i ^ k) for i in range(size)])  21.9 us
    ppermute x17, waiting for transfers between devices, swap(): return lax.ppermute(x, axis, [(i, i ^ k) for i in range(size)])  11 us
    pallas_call x2, Pallas kernels, load(): pl.pallas_call(load_kernel, in_specs=[*hbm_specs(1), pl.BlockSpec(memory_...  4.04 us
    pallas_call x1, Pallas kernels, attention(): pl.pallas_call(attention_kernel, in_specs=hbm_specs(7), out_specs=whole_v...  3.93 us
    pallas_call x1, Pallas kernels, new_state(): pl.pallas_call(state_kernel, in_specs=[pl.BlockSpec(memory_space=pltpu.SM...  2.89 us
    pallas_call x1, Pallas kernels, regroup(): pl.pallas_call(regroup_kernel, in_specs=[*hbm_specs(1), pl.BlockSpec(memo...  2.23 us
    pallas_call x1, Pallas kernels, project(): pl.pallas_call(project_kernel, in_specs=hbm_specs(1) + whole_vmem(1), out...  1.81 us
    pallas_call x1, Pallas kernels, gate_up(): pl.pallas_call(gate_up_kernel, in_specs=whole_vmem(3 + len(xs)), out_spec...  1.69 us
  transfers between devices with their start and end apart: 17, of which 8 were waited for; matrix products, arithmetic and copies ran while one was open for 0% of the time, Pallas kernels for 22%

profile of v3, /device:TPU:0, one launch (start us, length us, event | category | flops | bytes accessed | tf_op | source)
XLA Modules:
  0.0 53.9 jit_solution(3375143211469586726)
XLA Ops:
  0.6 3.9 %attention.1 = (bf16[4,48,384]{2,1,0:T(8,128)(2,1)S(1)}, bf16[48,512]{1,0:T(8,128)(2,1)S(1)}, bf16[24,4,128,128]{3,2,1,0:T(8,128)(2,1)S(1)}) custom-call(f32[4]{0:T(128)} %slope_ref.1, bf16[24,2,512]{2,1,0:T(2,128)(2,1)} %q_hbm.1, bf16[24,2,512]{2,1,0:T(2,128)(2,1)} %k_ref.1, bf16[24,2,512]{2,1,0:T(2,128)(2,1)} %v_ref.1, bf16[24,4,128,128]{3,2,1,0:T(8,128)(2,1)} %s_hbm.1, ...), custom_call_target="tpu_custom_call" | custom-call | tf_op jit(solution)/shard_map/attention/pallas_call | solution.py:146
  4.6 0.5 collective-permute-start
  5.1 1.8 %project.1.mine_ref = f32[4,48,384]{2,1,0:T(8,128)S(1)} custom-call(bf16[512,3072]{1,0:T(8,128)(2,1)} %w_hbm.6, bf16[48,512]{1,0:T(8,128)(2,1)S(1)} %get-tuple-element.28.normed_ref), custom_call_target="tpu_custom_call" | custom-call | flops 100000000 | bytes 2000000 | tf_op jit(solution)/shard_map/project/pallas_call | solution.py:178
  7.0 4.7 %collective-permute-start.1 = (bf16[48,384]{1,0:T(8,128)(2,1)S(1)}, bf16[48,384]{1,0:T(8,128)(2,1)S(1)}, u32[]{:S(2)}, u32[]{:S(2)}) collective-permute-start(bf16[48,384]{1,0:T(8,128)(2,1)S(1)} %get-tuple-element.31), channel_id=1, source_target_pairs={{0,6},{2,4},{4,2},{6,0},{1,7},{3,5},{5,3},{7,1},{8,14},{10,12},{12... | collective-permute-start | bytes 110600 | tf_op jit(solution)/shard_map/ppermute | solution.py:572
  11.7 0.6 %collective-permute-start.3 = (bf16[48,384]{1,0:T(8,128)(2,1)S(1)}, bf16[48,384]{1,0:T(8,128)(2,1)S(1)}, u32[]{:S(2)}, u32[]{:S(2)}) collective-permute-start(bf16[48,384]{1,0:T(8,128)(2,1)S(1)} %get-tuple-element.33), channel_id=1, source_target_pairs={{0,2},{2,0},{4,6},{6,4},{1,3},{3,1},{5,7},{7,5},{8,10},{10,8},{12,... | collective-permute-start | bytes 110600 | tf_op jit(solution)/shard_map/ppermute | solution.py:572
  12.3 2.2 %regroup_down.1.after_ref.w_ref = bf16[4,1152,384]{2,1,0:T(8,128)(2,1)S(1)} custom-call(bf16[1,1152,4,384]{3,2,1,0:T(4,128)(2,1)} %w_hbm.7, f32[48,384]{1,0:T(8,128)S(1)} %get-tuple-element.30.after_ref.own_ref), custom_call_target="tpu_custom_call" | custom-call | flops 100000000 | bytes 7000000 | tf_op jit(solution)/shard_map/regroup_down/pallas_call | solution.py:459
  14.6 1.9 %collective-permute-done.2.refs_1_ = bf16[48,384]{1,0:T(8,128)(2,1)S(1)} collective-permute-done((bf16[48,384]{1,0:T(8,128)(2,1)S(1)}, bf16[48,384]{1,0:T(8,128)(2,1)S(1)}, u32[]{:S(2)}, u32[]{:S(2)}) %collective-permute-start.2) | collective-permute-done | bytes 36896 | tf_op jit(solution)/shard_map/ppermute | solution.py:572
  16.6 1.9 %collective-permute-start.6 = (bf16[48,384]{1,0:T(8,128)(2,1)S(1)}, bf16[48,384]{1,0:T(8,128)(2,1)S(1)}, u32[]{:S(2)}, u32[]{:S(2)}) collective-permute-start(bf16[48,384]{1,0:T(8,128)(2,1)S(1)} %add_residual.1.after_ref.refs_0_.flat_ref), channel_id=1, source_target_pairs={{0,6},{2,4},{4,2},{6,0},{1,7},{3,5},{5,3},{7,1},{8,14},{10,12},{12... | collective-permute-start | bytes 110600 | tf_op jit(solution)/shard_map/ppermute | solution.py:572
  18.7 2.3 %collective-permute-start.4 = (bf16[48,384]{1,0:T(8,128)(2,1)S(1)}, bf16[48,384]{1,0:T(8,128)(2,1)S(1)}, u32[]{:S(2)}, u32[]{:S(2)}) collective-permute-start(bf16[48,384]{1,0:T(8,128)(2,1)S(1)} %add_residual.1.after_ref.refs_0_.flat_ref), channel_id=1, source_target_pairs={{0,2},{2,0},{4,6},{6,4},{1,3},{3,1},{5,7},{7,5},{8,10},{10,8},{12,... | collective-permute-start | bytes 110600 | tf_op jit(solution)/shard_map/ppermute | solution.py:572
  21.3 2.0 %load_weight.2.after_ref.wg_ref = bf16[1,4,384,1152]{3,2,1,0:T(8,128)(2,1)S(1)} custom-call(bf16[1,4,384,1152]{3,2,1,0:T(8,128)(2,1)} %w_hbm.8, bf16[48,384]{1,0:T(8,128)(2,1)S(1)} %add_residual.1.after_ref.refs_0_.flat_ref), custom_call_target="tpu_custom_call" | custom-call | flops 1000000 | bytes 7000000 | tf_op jit(solution)/shard_map/load_weight/pallas_call | solution.py:482
  23.3 0.4 collective-permute-done.5.refs_2_
  24.1 1.6 %collective-permute-start.7 = (bf16[144,384]{1,0:T(8,128)(2,1)S(1)}, bf16[144,384]{1,0:T(8,128)(2,1)S(1)}, u32[]{:S(2)}, u32[]{:S(2)}) collective-permute-start(bf16[144,384]{1,0:T(8,128)(2,1)S(1)} %get-tuple-element.36), channel_id=1, source_target_pairs={{0,8},{8,0},{16,24},{24,16},{1,9},{9,1},{17,25},{25,17},{2,10},{10... | collective-permute-start | bytes 331784 | tf_op jit(solution)/shard_map/ppermute | solution.py:572
  25.6 1.5 %collective-permute-start.8 = (bf16[144,384]{1,0:T(8,128)(2,1)S(1)}, bf16[144,384]{1,0:T(8,128)(2,1)S(1)}, u32[]{:S(2)}, u32[]{:S(2)}) collective-permute-start(bf16[144,384]{1,0:T(8,128)(2,1)S(1)} %get-tuple-element.37), channel_id=1, source_target_pairs={{0,16},{8,24},{16,0},{24,8},{1,17},{9,25},{17,1},{25,9},{2,18},{10... | collective-permute-start | bytes 331784 | tf_op jit(solution)/shard_map/ppermute | solution.py:572
  27.1 0.5 collective-permute-start.9
  27.6 2.0 %load_weight.3.wu_ref = bf16[1,4,384,1152]{3,2,1,0:T(8,128)(2,1)S(1)} custom-call(bf16[1,4,384,1152]{3,2,1,0:T(8,128)(2,1)} %w_hbm.9, bf16[144,384]{1,0:T(8,128)(2,1)S(1)} %get-tuple-element.35.after_ref.refs_0_), custom_call_target="tpu_custom_call" | custom-call | flops 1000000 | bytes 7000000 | tf_op jit(solution)/shard_map/load_weight/pallas_call | solution.py:482
  29.7 1.2 %collective-permute-done.8.refs_2_ = bf16[144,384]{1,0:T(8,128)(2,1)S(1)} collective-permute-done((bf16[144,384]{1,0:T(8,128)(2,1)S(1)}, bf16[144,384]{1,0:T(8,128)(2,1)S(1)}, u32[]{:S(2)}, u32[]{:S(2)}) %collective-permute-start.8) | collective-permute-done | bytes 110624 | tf_op jit(solution)/shard_map/ppermute | solution.py:572
  30.8 2.0 %collective-permute-done.9.refs_3_ = bf16[144,384]{1,0:T(8,128)(2,1)S(1)} collective-permute-done((bf16[144,384]{1,0:T(8,128)(2,1)S(1)}, bf16[144,384]{1,0:T(8,128)(2,1)S(1)}, u32[]{:S(2)}, u32[]{:S(2)}) %collective-permute-start.9) | collective-permute-done | bytes 110624 | tf_op jit(solution)/shard_map/ppermute | solution.py:572
  32.8 1.7 %gate_up.1.part_ref = bf16[144,2432]{1,0:T(8,128)(2,1)S(1)} custom-call(f32[1,3072]{1,0:T(1,128)S(1)} %bitcast.4, bf16[1,4,384,1152]{3,2,1,0:T(8,128)(2,1)S(1)} %load_weight.2.after_ref.wg_ref, bf16[1,4,384,1152]{3,2,1,0:T(8,128)(2,1)S(1)} %load_weight.3.wu_ref, bf16[144,384]{1,0:T(8,128)(2,1)S(1)} %get-tuple-element.35.after_ref.refs_0_, ...), custom_call_target="tpu_custom_call" | custom-call | tf_op jit(solution)/shard_map/gate_up/pallas_call | solution.py:420
  34.6 2.1 %collective-permute-done.10.recv_ref = bf16[144,2432]{1,0:T(8,128)(2,1)S(1)} collective-permute-done((bf16[144,2432]{1,0:T(8,128)(2,1)S(1)}, bf16[144,2432]{1,0:T(8,128)(2,1)S(1)}, u32[]{:S(2)}, u32[]{:S(2)}) %collective-permute-start.10) | collective-permute-done | bytes 700448 | tf_op jit(solution)/shard_map/ppermute | solution.py:572
  36.8 1.2 %down.1 = (bf16[144,384]{1,0:T(8,128)(2,1)S(1)}, bf16[144,384]{1,0:T(8,128)(2,1)S(1)}, bf16[144,384]{1,0:T(8,128)(2,1)S(1)}, bf16[144,384]{1,0:T(8,128)(2,1)S(1)}) custom-call(bf16[144,2432]{1,0:T(8,128)(2,1)S(1)} %gate_up.1.part_ref, bf16[144,2432]{1,0:T(8,128)(2,1)S(1)} %collective-permute-done.10.recv_ref, ...), custom_call_target="tpu_custom_call" | custom-call | tf_op jit(solution)/shard_map/down/pallas_call | solution.py:514
  38.0 0.6 %collective-permute-start.11 = (bf16[144,384]{1,0:T(8,128)(2,1)S(1)}, bf16[144,384]{1,0:T(8,128)(2,1)S(1)}, u32[]{:S(2)}, u32[]{:S(2)}) collective-permute-start(bf16[144,384]{1,0:T(8,128)(2,1)S(1)} %get-tuple-element.44), channel_id=1, source_target_pairs={{0,8},{8,0},{16,24},{24,16},{1,9},{9,1},{17,25},{25,17},{2,10},{10... | collective-permute-start | bytes 331784 | tf_op jit(solution)/shard_map/ppermute | solution.py:572
  38.6 0.5 collective-permute-start.12
  39.1 2.4 %collective-permute-start.13 = (bf16[144,384]{1,0:T(8,128)(2,1)S(1)}, bf16[144,384]{1,0:T(8,128)(2,1)S(1)}, u32[]{:S(2)}, u32[]{:S(2)}) collective-permute-start(bf16[144,384]{1,0:T(8,128)(2,1)S(1)} %get-tuple-element.46), channel_id=1, source_target_pairs={{0,24},{8,16},{16,8},{24,0},{1,25},{9,17},{17,9},{25,1},{2,26},{10... | collective-permute-start | bytes 331784 | tf_op jit(solution)/shard_map/ppermute | solution.py:572
  41.6 2.9 %new_state.1 = (bf16[24,4,128,128]{3,2,1,0:T(8,128)(2,1)}, f32[8,128]{1,0:T(8,128)S(1)}) custom-call(f32[4]{0:T(128)S(1)} %copy-done.6, bf16[24,2,512]{2,1,0:T(2,128)(2,1)S(1)} %copy-done, bf16[24,2,512]{2,1,0:T(2,128)(2,1)S(1)} %copy-done.1, bf16[24,4,128,128]{3,2,1,0:T(8,128)(2,1)S(1)} %get-tuple-element.27.s_ref, ...), custom_call_target="tpu_custom_call" | custom-call | flops 100000000 | bytes 8000000 | tf_op jit(solution)/shard_map/new_state/pallas_call | solution.py:232
  44.5 1.3 %collective-permute-done.12.refs_2_ = bf16[144,384]{1,0:T(8,128)(2,1)S(1)} collective-permute-done((bf16[144,384]{1,0:T(8,128)(2,1)S(1)}, bf16[144,384]{1,0:T(8,128)(2,1)S(1)}, u32[]{:S(2)}, u32[]{:S(2)}) %collective-permute-start.12) | collective-permute-done | bytes 110624 | tf_op jit(solution)/shard_map/ppermute | solution.py:572
  46.1 2.1 %collective-permute-start.14 = (bf16[48,384]{1,0:T(8,128)(2,1)S(1)}, bf16[48,384]{1,0:T(8,128)(2,1)S(1)}, u32[]{:S(2)}, u32[]{:S(2)}) collective-permute-start(bf16[48,384]{1,0:T(8,128)(2,1)S(1)} %get-tuple-element.48), channel_id=1, source_target_pairs={{0,6},{2,4},{4,2},{6,0},{1,7},{3,5},{5,3},{7,1},{8,14},{10,12},{12... | collective-permute-start | bytes 110600 | tf_op jit(solution)/shard_map/ppermute | solution.py:572
  48.3 0.6 %collective-permute-start.15 = (bf16[48,384]{1,0:T(8,128)(2,1)S(1)}, bf16[48,384]{1,0:T(8,128)(2,1)S(1)}, u32[]{:S(2)}, u32[]{:S(2)}) collective-permute-start(bf16[48,384]{1,0:T(8,128)(2,1)S(1)} %get-tuple-element.49), channel_id=1, source_target_pairs={{0,4},{2,6},{4,0},{6,2},{1,5},{3,7},{5,1},{7,3},{8,12},{10,14},{12... | collective-permute-start | bytes 110600 | tf_op jit(solution)/shard_map/ppermute | solution.py:572
  48.9 1.7 %collective-permute-start.16 = (bf16[48,384]{1,0:T(8,128)(2,1)S(1)}, bf16[48,384]{1,0:T(8,128)(2,1)S(1)}, u32[]{:S(2)}, u32[]{:S(2)}) collective-permute-start(bf16[48,384]{1,0:T(8,128)(2,1)S(1)} %get-tuple-element.50), channel_id=1, source_target_pairs={{0,2},{2,0},{4,6},{6,4},{1,3},{3,1},{5,7},{7,5},{8,10},{10,8},{12,... | collective-permute-start | bytes 110600 | tf_op jit(solution)/shard_map/ppermute | solution.py:572
  50.6 0.6 %by_request.1 = bf16[24,2,384]{2,1,0:T(2,128)(2,1)} custom-call(bf16[48,384]{1,0:T(8,128)(2,1)S(1)} %add_residual.1.after_ref.refs_0_.flat_ref), custom_call_target="tpu_custom_call" | custom-call | flops 100000 | bytes 1000000 | tf_op jit(solution)/shard_map/by_request/pallas_call | solution.py:296
  51.2 0.7 %collective-permute-done.14.refs_0_ = bf16[48,384]{1,0:T(8,128)(2,1)S(1)} collective-permute-done((bf16[48,384]{1,0:T(8,128)(2,1)S(1)}, bf16[48,384]{1,0:T(8,128)(2,1)S(1)}, u32[]{:S(2)}, u32[]{:S(2)}) %collective-permute-start.14) | collective-permute-done | bytes 36896 | tf_op jit(solution)/shard_map/ppermute | solution.py:572
  51.9 1.3 %collective-permute-done.15.refs_1_ = bf16[48,384]{1,0:T(8,128)(2,1)S(1)} collective-permute-done((bf16[48,384]{1,0:T(8,128)(2,1)S(1)}, bf16[48,384]{1,0:T(8,128)(2,1)S(1)}, u32[]{:S(2)}, u32[]{:S(2)}) %collective-permute-start.15) | collective-permute-done | bytes 36896 | tf_op jit(solution)/shard_map/ppermute | solution.py:572
  53.3 0.7 %finish.1 = bf16[24,2,384]{2,1,0:T(2,128)(2,1)} custom-call(f32[48,384]{1,0:T(8,128)S(1)} %get-tuple-element.47.own_ref, bf16[48,384]{1,0:T(8,128)(2,1)S(1)} %collective-permute-done.14.refs_0_, bf16[48,384]{1,0:T(8,128)(2,1)S(1)} %collective-permute-done.15.refs_1_, bf16[48,384]{1,0:T(8,128)(2,1)S(1)} %collective-permute-done.16.refs_2_), custom_call_target="tpu_custom_call" | custom-call | tf_op jit(solution)/shard_map/finish/pallas_call | solution.py:560
  (31 shorter events, 1.4 us)
Async XLA Ops:
  4.6 2.3 %collective-permute-start = (bf16[4,48,384]{2,1,0:T(8,128)(2,1)S(1)}, bf16[4,48,384]{2,1,0:T(8,128)(2,1)S(1)}, u32[]{:S(2)}, u32[]{:S(2)}) collective-permute-start(bf16[4,48,384]{2,1,0:T(8,128)(2,1)S(1)} %get-tuple-element.29), channel_id=1, source_target_pairs={{0,1},{1,0},{2,3},{3,2},{4,5},{5,4},{6,7},{7,6},{8,9},{9,8},{10,11... | collective-permute-start | bytes 442376 | tf_op jit(solution)/shard_map/ppermute | solution.py:572
  7.0 7.6 %collective-permute-start.1 = (bf16[48,384]{1,0:T(8,128)(2,1)S(1)}, bf16[48,384]{1,0:T(8,128)(2,1)S(1)}, u32[]{:S(2)}, u32[]{:S(2)}) collective-permute-start(bf16[48,384]{1,0:T(8,128)(2,1)S(1)} %get-tuple-element.31), channel_id=1, source_target_pairs={{0,6},{2,4},{4,2},{6,0},{1,7},{3,5},{5,3},{7,1},{8,14},{10,12},{12... | collective-permute-start | bytes 110600 | tf_op jit(solution)/shard_map/ppermute | solution.py:572
  11.7 4.9 %collective-permute-start.2 = (bf16[48,384]{1,0:T(8,128)(2,1)S(1)}, bf16[48,384]{1,0:T(8,128)(2,1)S(1)}, u32[]{:S(2)}, u32[]{:S(2)}) collective-permute-start(bf16[48,384]{1,0:T(8,128)(2,1)S(1)} %get-tuple-element.32), channel_id=1, source_target_pairs={{0,4},{2,6},{4,0},{6,2},{1,5},{3,7},{5,1},{7,3},{8,12},{10,14},{12... | collective-permute-start | bytes 110600 | tf_op jit(solution)/shard_map/ppermute | solution.py:572
  11.7 4.9 %collective-permute-start.3 = (bf16[48,384]{1,0:T(8,128)(2,1)S(1)}, bf16[48,384]{1,0:T(8,128)(2,1)S(1)}, u32[]{:S(2)}, u32[]{:S(2)}) collective-permute-start(bf16[48,384]{1,0:T(8,128)(2,1)S(1)} %get-tuple-element.33), channel_id=1, source_target_pairs={{0,2},{2,0},{4,6},{6,4},{1,3},{3,1},{5,7},{7,5},{8,10},{10,8},{12,... | collective-permute-start | bytes 110600 | tf_op jit(solution)/shard_map/ppermute | solution.py:572
  12.3 4.2 %copy-start.2 = (bf16[24,2,384]{2,1,0:T(2,128)(2,1)S(1)}, bf16[24,2,384]{2,1,0:T(2,128)(2,1)}, u32[]{:S(2)}) copy-start(bf16[24,2,384]{2,1,0:T(2,128)(2,1)} %residual_ref.1) | copy-start | bytes 110596
  14.5 6.5 %copy-start.4 = (s32[24,2,2]{0,2,1:T(2,128)S(1)}, s32[24,2,2]{0,2,1:T(2,128)}, u32[]{:S(2)}) copy-start(s32[24,2,2]{0,2,1:T(2,128)} %param.23) | copy-start | bytes 1156
  14.5 6.5 %copy-start.5 = (f32[24,2,2]{0,2,1:T(2,128)S(1)}, f32[24,2,2]{0,2,1:T(2,128)}, u32[]{:S(2)}) copy-start(f32[24,2,2]{0,2,1:T(2,128)} %param.24) | copy-start | bytes 1156
  16.6 6.7 %collective-permute-start.6 = (bf16[48,384]{1,0:T(8,128)(2,1)S(1)}, bf16[48,384]{1,0:T(8,128)(2,1)S(1)}, u32[]{:S(2)}, u32[]{:S(2)}) collective-permute-start(bf16[48,384]{1,0:T(8,128)(2,1)S(1)} %add_residual.1.after_ref.refs_0_.flat_ref), channel_id=1, source_target_pairs={{0,6},{2,4},{4,2},{6,0},{1,7},{3,5},{5,3},{7,1},{8,14},{10,12},{12... | collective-permute-start | bytes 110600 | tf_op jit(solution)/shard_map/ppermute | solution.py:572
  18.5 5.3 %collective-permute-start.5 = (bf16[48,384]{1,0:T(8,128)(2,1)S(1)}, bf16[48,384]{1,0:T(8,128)(2,1)S(1)}, u32[]{:S(2)}, u32[]{:S(2)}) collective-permute-start(bf16[48,384]{1,0:T(8,128)(2,1)S(1)} %add_residual.1.after_ref.refs_0_.flat_ref), channel_id=1, source_target_pairs={{0,4},{2,6},{4,0},{6,2},{1,5},{3,7},{5,1},{7,3},{8,12},{10,14},{12... | collective-permute-start | bytes 110600 | tf_op jit(solution)/shard_map/ppermute | solution.py:572
  18.7 5.0 %collective-permute-start.4 = (bf16[48,384]{1,0:T(8,128)(2,1)S(1)}, bf16[48,384]{1,0:T(8,128)(2,1)S(1)}, u32[]{:S(2)}, u32[]{:S(2)}) collective-permute-start(bf16[48,384]{1,0:T(8,128)(2,1)S(1)} %add_residual.1.after_ref.refs_0_.flat_ref), channel_id=1, source_target_pairs={{0,2},{2,0},{4,6},{6,4},{1,3},{3,1},{5,7},{7,5},{8,10},{10,8},{12,... | collective-permute-start | bytes 110600 | tf_op jit(solution)/shard_map/ppermute | solution.py:572
  24.1 5.6 %collective-permute-start.7 = (bf16[144,384]{1,0:T(8,128)(2,1)S(1)}, bf16[144,384]{1,0:T(8,128)(2,1)S(1)}, u32[]{:S(2)}, u32[]{:S(2)}) collective-permute-start(bf16[144,384]{1,0:T(8,128)(2,1)S(1)} %get-tuple-element.36), channel_id=1, source_target_pairs={{0,8},{8,0},{16,24},{24,16},{1,9},{9,1},{17,25},{25,17},{2,10},{10... | collective-permute-start | bytes 331784 | tf_op jit(solution)/shard_map/ppermute | solution.py:572
  25.6 5.2 %collective-permute-start.8 = (bf16[144,384]{1,0:T(8,128)(2,1)S(1)}, bf16[144,384]{1,0:T(8,128)(2,1)S(1)}, u32[]{:S(2)}, u32[]{:S(2)}) collective-permute-start(bf16[144,384]{1,0:T(8,128)(2,1)S(1)} %get-tuple-element.37), channel_id=1, source_target_pairs={{0,16},{8,24},{16,0},{24,8},{1,17},{9,25},{17,1},{25,9},{2,18},{10... | collective-permute-start | bytes 331784 | tf_op jit(solution)/shard_map/ppermute | solution.py:572
  27.1 5.6 %collective-permute-start.9 = (bf16[144,384]{1,0:T(8,128)(2,1)S(1)}, bf16[144,384]{1,0:T(8,128)(2,1)S(1)}, u32[]{:S(2)}, u32[]{:S(2)}) collective-permute-start(bf16[144,384]{1,0:T(8,128)(2,1)S(1)} %get-tuple-element.38), channel_id=1, source_target_pairs={{0,24},{8,16},{16,8},{24,0},{1,25},{9,17},{17,9},{25,1},{2,26},{10... | collective-permute-start | bytes 331784 | tf_op jit(solution)/shard_map/ppermute | solution.py:572
  27.6 5.2 %copy-start.3 = (f32[3072]{0:T(1024)S(1)}, f32[3072]{0:T(1024)}, u32[]{:S(2)}) copy-start(f32[3072]{0:T(1024)} %param.22) | copy-start | bytes 36868
  34.5 7.1 %copy-start = (bf16[24,2,512]{2,1,0:T(2,128)(2,1)S(1)}, bf16[24,2,512]{2,1,0:T(2,128)(2,1)}, u32[]{:S(2)}) copy-start(bf16[24,2,512]{2,1,0:T(2,128)(2,1)} %k_ref.1) | copy-start | bytes 147460
  34.5 7.1 %copy-start.1 = (bf16[24,2,512]{2,1,0:T(2,128)(2,1)S(1)}, bf16[24,2,512]{2,1,0:T(2,128)(2,1)}, u32[]{:S(2)}) copy-start(bf16[24,2,512]{2,1,0:T(2,128)(2,1)} %v_ref.1) | copy-start | bytes 147460
  34.5 7.0 %copy-start.6 = (f32[4]{0:T(128)S(1)}, f32[4]{0:T(128)}, u32[]{:S(2)}) copy-start(f32[4]{0:T(128)} %slope_ref.1) | copy-start | bytes 52
  34.5 2.2 %collective-permute-start.10 = (bf16[144,2432]{1,0:T(8,128)(2,1)S(1)}, bf16[144,2432]{1,0:T(8,128)(2,1)S(1)}, u32[]{:S(2)}, u32[]{:S(2)}) collective-permute-start(bf16[144,2432]{1,0:T(8,128)(2,1)S(1)} %gate_up.1.part_ref), channel_id=1, source_target_pairs={{0,1},{1,0},{2,3},{3,2},{4,5},{5,4},{6,7},{7,6},{8,9},{9,8},{10,11... | collective-permute-start | bytes 2101256 | tf_op jit(solution)/shard_map/ppermute | solution.py:572
  38.0 6.5 %collective-permute-start.11 = (bf16[144,384]{1,0:T(8,128)(2,1)S(1)}, bf16[144,384]{1,0:T(8,128)(2,1)S(1)}, u32[]{:S(2)}, u32[]{:S(2)}) collective-permute-start(bf16[144,384]{1,0:T(8,128)(2,1)S(1)} %get-tuple-element.44), channel_id=1, source_target_pairs={{0,8},{8,0},{16,24},{24,16},{1,9},{9,1},{17,25},{25,17},{2,10},{10... | collective-permute-start | bytes 331784 | tf_op jit(solution)/shard_map/ppermute | solution.py:572
  38.6 7.2 %collective-permute-start.12 = (bf16[144,384]{1,0:T(8,128)(2,1)S(1)}, bf16[144,384]{1,0:T(8,128)(2,1)S(1)}, u32[]{:S(2)}, u32[]{:S(2)}) collective-permute-start(bf16[144,384]{1,0:T(8,128)(2,1)S(1)} %get-tuple-element.45), channel_id=1, source_target_pairs={{0,16},{8,24},{16,0},{24,8},{1,17},{9,25},{17,1},{25,9},{2,18},{10... | collective-permute-start | bytes 331784 | tf_op jit(solution)/shard_map/ppermute | solution.py:572
  39.1 6.7 %collective-permute-start.13 = (bf16[144,384]{1,0:T(8,128)(2,1)S(1)}, bf16[144,384]{1,0:T(8,128)(2,1)S(1)}, u32[]{:S(2)}, u32[]{:S(2)}) collective-permute-start(bf16[144,384]{1,0:T(8,128)(2,1)S(1)} %get-tuple-element.46), channel_id=1, source_target_pairs={{0,24},{8,16},{16,8},{24,0},{1,25},{9,17},{17,9},{25,1},{2,26},{10... | collective-permute-start | bytes 331784 | tf_op jit(solution)/shard_map/ppermute | solution.py:572
  46.1 5.8 %collective-permute-start.14 = (bf16[48,384]{1,0:T(8,128)(2,1)S(1)}, bf16[48,384]{1,0:T(8,128)(2,1)S(1)}, u32[]{:S(2)}, u32[]{:S(2)}) collective-permute-start(bf16[48,384]{1,0:T(8,128)(2,1)S(1)} %get-tuple-element.48), channel_id=1, source_target_pairs={{0,6},{2,4},{4,2},{6,0},{1,7},{3,5},{5,3},{7,1},{8,14},{10,12},{12... | collective-permute-start | bytes 110600 | tf_op jit(solution)/shard_map/ppermute | solution.py:572
  48.3 5.0 %collective-permute-start.15 = (bf16[48,384]{1,0:T(8,128)(2,1)S(1)}, bf16[48,384]{1,0:T(8,128)(2,1)S(1)}, u32[]{:S(2)}, u32[]{:S(2)}) collective-permute-start(bf16[48,384]{1,0:T(8,128)(2,1)S(1)} %get-tuple-element.49), channel_id=1, source_target_pairs={{0,4},{2,6},{4,0},{6,2},{1,5},{3,7},{5,1},{7,3},{8,12},{10,14},{12... | collective-permute-start | bytes 110600 | tf_op jit(solution)/shard_map/ppermute | solution.py:572
  48.9 4.4 %collective-permute-start.16 = (bf16[48,384]{1,0:T(8,128)(2,1)S(1)}, bf16[48,384]{1,0:T(8,128)(2,1)S(1)}, u32[]{:S(2)}, u32[]{:S(2)}) collective-permute-start(bf16[48,384]{1,0:T(8,128)(2,1)S(1)} %get-tuple-element.50), channel_id=1, source_target_pairs={{0,2},{2,0},{4,6},{6,4},{1,3},{3,1},{5,7},{7,5},{8,10},{10,8},{12,... | collective-permute-start | bytes 110600 | tf_op jit(solution)/shard_map/ppermute | solution.py:572

commit v4 on v3

--- a/solution.py
+++ b/solution.py
@@ -67,12 +67,14 @@
 
 def project_columns(loads, weight, normed, side, out_ref):
     groups, _, piece = out_ref.shape
-    if len(loads) == groups:
-        for a, copy in enumerate(loads):
-            copy.wait()
+    if weight.shape[0] == groups:
+        for a in range(groups):
+            if loads:
+                loads[a].wait()
             out_ref[a] = dot(normed, weight[a]).astype(out_ref.dtype)
         return
-    loads[0].wait()
+    for copy in loads:
+        copy.wait()
     for a in range(groups):
         both = dot(normed, weight[0, :, 2 * a * piece : 2 * (a + 1) * piece])
         out = jnp.where(side == 0, both[:, :piece], both[:, piece:])
@@ -80,8 +82,8 @@
 
 
 def attention_kernel(
-    slope_hbm, q_hbm, k_hbm, v_hbm, s_hbm, gain_hbm, w_hbm, other_ref, normed_ref, states,
-    slope, q_all, k_all, v_all, gain, weight, small_sem, state_sem, weight_sem,
+    slope_hbm, q_hbm, k_hbm, v_hbm, s_hbm, gain_hbm, w_hbm, other_ref, normed_ref, states, mine_weight,
+    slope, q_all, k_all, v_all, gain, weight, small_sem, state_sem, weight_sem, mine_sem,
 ):
     small = [
         pltpu.make_async_copy(source, target, small_sem.at[i])
@@ -99,8 +101,10 @@
         )
         for i in range(blocks)
     ]
-    weight_loads = load_columns(w_hbm, weight, weight_sem, 1 - lax.axis_index("side"))
-    for copy in small + loads + weight_loads:
+    side = lax.axis_index("side")
+    weight_loads = load_columns(w_hbm, weight, weight_sem, 1 - side)
+    mine_loads = load_columns(w_hbm, mine_weight, mine_sem, side)
+    for copy in small + loads + weight_loads + mine_loads:
         copy.start()
     for copy in small:
         copy.wait()
@@ -120,9 +124,11 @@
             k = k_all[here, :, at].reshape(rows, size).astype(F32)
             v = v_all[here, :, at].reshape(rows, size).astype(F32)
             decay = jnp.exp(jnp.full((rows, size), -slope[h], F32))
+            side_by_side = [states[i * block + r, h] for r in range(block)]
+            every = dot(q16, jnp.concatenate(side_by_side, 1))
             read = jnp.zeros((rows, size), F32)
             for r in range(block):
-                read = jnp.where(owner == r, dot(q16, states[i * block + r, h]), read)
+                read = jnp.where(owner == r, every[:, r * size : (r + 1) * size], read)
             k_before = pltpu.roll(k, 1, 0)
             v_before = pltpu.roll(v, 1, 0)
             same = jnp.sum(q * k, -1, keepdims=True)
@@ -134,7 +140,9 @@
         normed.append(jnp.concatenate(parts, 1) if heads > 1 else parts[0])
     normed = jnp.concatenate(normed, 0) if blocks > 1 else normed[0]
     normed_ref[...] = normed
-    project_columns(weight_loads, weight, normed, 1 - lax.axis_index("side"), other_ref)
+    project_columns(weight_loads, weight, normed, 1 - side, other_ref)
+    for copy in mine_loads:
+        copy.wait()
 
 
 def attention(slopes, queries, new_keys, new_values, head_states, gain, out_weight, groups):
@@ -146,11 +154,12 @@
     return pl.pallas_call(
         attention_kernel,
         in_specs=hbm_specs(7),
-        out_specs=whole_vmem(3),
+        out_specs=whole_vmem(4),
         out_shape=[
             in_vmem((groups, rows, piece), BF),
             in_vmem((rows, width), BF),
             in_vmem(head_states.shape, BF),
+            in_vmem(columns_shape(out_weight, groups), BF),
         ],
         scratch_shapes=[
             pltpu.SMEM(slopes.shape, F32), vec, vec, vec,
@@ -159,35 +168,27 @@
             pltpu.SemaphoreType.DMA((5,)),
             pltpu.SemaphoreType.DMA((requests,)),
             pltpu.SemaphoreType.DMA((groups,)),
+            pltpu.SemaphoreType.DMA((groups,)),
         ],
         compiler_params=params(),
         name="attention",
     )(*[from_hbm(x) if x.size > 1 else x for x in operands])
 
 
-def project_kernel(w_hbm, normed_ref, mine_ref, weight, weight_sem):
-    loads = load_columns(w_hbm, weight, weight_sem, lax.axis_index("side"))
-    for copy in loads:
-        copy.start()
-    normed = normed_ref[...]
-    project_columns(loads, weight, normed, lax.axis_index("side"), mine_ref)
-
-
-def project(out_weight, normed, groups):
-    piece = out_weight.shape[1] // (2 * groups)
+def project_kernel(normed_ref, weight, mine_ref):
+    project_columns([], weight, normed_ref[...], lax.axis_index("side"), mine_ref)
+
+
+def project(normed, weight, shape):
     return pl.pallas_call(
         project_kernel,
-        in_specs=hbm_specs(1) + whole_vmem(1),
+        in_specs=whole_vmem(2),
         out_specs=whole_vmem(1)[0],
-        out_shape=in_vmem((groups, normed.shape[0], piece), F32),
-        scratch_shapes=[
-            pltpu.VMEM(columns_shape(out_weight, groups), BF),
-            pltpu.SemaphoreType.DMA((groups,)),
-        ],
+        out_shape=in_vmem(shape, F32),
         compiler_params=params(),
         cost_estimate=cost(10**8, 2 * 10**6),
         name="project",
-    )(from_hbm(out_weight), normed)
+    )(normed, weight)
 
 
 def state_kernel(slope_ref, k_ref, v_ref, s_ref, after_ref, so_hbm, done_ref, out, sems):
@@ -352,8 +353,7 @@
     )(ids, gates, after)
 
 
-def dispatch_kernel(count, after_ref, pick_ref, *refs):
-    del after_ref
+def dispatch_kernel(count, pick_ref, *refs):
     x_refs, out_refs = refs[:-count], refs[-count:]
     capacity = out_refs[0].shape[0] // len(x_refs)
     picked = [
@@ -367,27 +367,34 @@
         out_ref[...] = jnp.concatenate(rows, 0).astype(BF)
 
 
-def dispatch(after, pick, xs, count):
+def dispatch(pick, xs, count):
     piece = xs[0].shape[1]
     rows = len(xs) * pick.shape[1] // count
     return pl.pallas_call(
         functools.partial(dispatch_kernel, count),
-        in_specs=[pl.BlockSpec(memory_space=pl.ANY)] + whole_vmem(1 + len(xs)),
+        in_specs=whole_vmem(1 + len(xs)),
         out_specs=whole_vmem(count),
         out_shape=[struct((rows, piece), BF)] * count,
         compiler_params=params(),
         name="dispatch",
-    )(after, pick, *xs)
-
-
-def gate_up_kernel(gain_ref, wg_ref, wu_ref, *refs):
-    x_refs, (out_ref, placed) = refs[:-2], refs[-2:]
+    )(pick, *xs)
+
+
+def products(lhs, wg_ref, wu_ref, start, stop, out_ref):
+    _, groups, piece, _ = wg_ref.shape
+    for i, w_ref in enumerate((wg_ref, wu_ref)):
+        rhs = w_ref[0, :, :, start:stop].reshape(groups * piece, stop - start)
+        at = i * (stop - start)
+        out_ref[:, at : at + stop - start] = dot(lhs, rhs).astype(BF)
+
+
+def first_kernel(split, gain_ref, wg_ref, wu_ref, *refs):
+    x_refs, (out_ref, lhs_ref, placed) = refs[:-3], refs[-3:]
     me, side = lax.axis_index("heads"), lax.axis_index("side")
     groups, total, piece = placed.shape
-    hidden = wg_ref.shape[3]
     capacity = total // len(x_refs)
     squares = jnp.zeros((total, 1), F32)
-    xs = [x_ref[...].astype(F32) for x_ref in x_refs]
+    xs = [x_ref[...].astype(F32) for x_ref in (x_refs[0], *x_refs[:0:-1])]
     for k in range(groups):
         at = me ^ k
         x = jnp.concatenate([x[k * capacity : (k + 1) * capacity] for x in xs], 0)
@@ -400,32 +407,46 @@
         gain = jnp.where(side == 0, low, high)
         parts.append((placed[a].astype(F32) * gain).astype(BF))
     lhs = jnp.concatenate(parts, 1)
-    wide = 384 if hidden % 384 == 0 else hidden
-    for n in range(0, hidden, wide):
-        rhs = wg_ref[0, :, :, n : n + wide].reshape(groups * piece, wide)
-        out_ref[:, n : n + wide] = dot(lhs, rhs).astype(BF)
-    for n in range(0, hidden, wide):
-        rhs = wu_ref[0, :, :, n : n + wide].reshape(groups * piece, wide)
-        out_ref[:, hidden + n : hidden + n + wide] = dot(lhs, rhs).astype(BF)
+    lhs_ref[...] = lhs
+    products(lhs, wg_ref, wu_ref, 0, split, out_ref)
     coarse = squares.astype(BF)
     fine = (squares - coarse.astype(F32)).astype(BF)
     lane = lax.broadcasted_iota(jnp.int32, (total, 128), 1)
     extra = jnp.where(lane == 0, coarse.astype(F32), jnp.where(lane == 1, fine.astype(F32), 0.0))
-    out_ref[:, 2 * hidden :] = extra.astype(BF)
-
-
-def gate_up(gain, w_gate, w_up, xs):
-    _, groups, piece, hidden = w_gate.shape
+    out_ref[:, 2 * split :] = extra.astype(BF)
+
+
+def first_units(split, gain, w_gate, w_up, xs):
+    _, groups, piece, _ = w_gate.shape
     total = xs[0].shape[0] // groups * len(xs)
     return pl.pallas_call(
-        gate_up_kernel,
+        functools.partial(first_kernel, split),
         in_specs=whole_vmem(3 + len(xs)),
-        out_specs=pl.BlockSpec(memory_space=pltpu.VMEM),
-        out_shape=struct((total, 2 * hidden + 128), BF),
+        out_specs=whole_vmem(2),
+        out_shape=[
+            in_vmem((total, 2 * split + 128), BF),
+            in_vmem((total, groups * piece), BF),
+        ],
         scratch_shapes=[pltpu.VMEM((groups, total, piece), BF)],
         compiler_params=params(),
-        name="gate_up",
+        name="first_units",
     )(gain, w_gate, w_up, *xs)
+
+
+def other_kernel(split, lhs_ref, wg_ref, wu_ref, out_ref):
+    products(lhs_ref[...], wg_ref, wu_ref, split, wg_ref.shape[3], out_ref)
+
+
+def other_units(split, lhs, w_gate, w_up):
+    return pl.pallas_call(
+        functools.partial(other_kernel, split),
+        in_specs=whole_vmem(3),
+        out_specs=whole_vmem(1)[0],
+        out_shape=in_vmem((lhs.shape[0], 2 * (w_gate.shape[3] - split)), BF),
+        compiler_params=params(),
+        cost_estimate=cost(10**9, 4 * 10**6),
+        name="other_units",
+    )(lhs, w_gate, w_up)
 
 
 def regroup_kernel(w_hbm, after_ref, out_ref, weight, sems):
@@ -471,54 +492,59 @@
     )(from_hbm(w_down), after)
 
 
-def load_kernel(w_hbm, after_ref, out_ref, sem):
-    del after_ref
-    copy = pltpu.make_async_copy(w_hbm, out_ref, sem)
-    copy.start()
-    copy.wait()
-
-
-def load(w, after):
-    return pl.pallas_call(
-        load_kernel,
-        in_specs=[*hbm_specs(1), pl.BlockSpec(memory_space=pl.ANY)],
-        out_specs=whole_vmem(1)[0],
-        out_shape=in_vmem(w.shape, w.dtype),
-        scratch_shapes=[pltpu.SemaphoreType.DMA],
-        compiler_params=params(),
-        cost_estimate=cost(10**6, 7 * 10**6),
-        name="load_weight",
-    )(from_hbm(w), after)
-
-
-def down_kernel(width, part_ref, recv_ref, w_ref, *out_refs):
-    groups, hidden, piece = w_ref.shape
-    capacity = part_ref.shape[0] // len(out_refs)
-    extra = part_ref[:, 2 * hidden :].astype(F32) + recv_ref[:, 2 * hidden :].astype(F32)
-    squares = extra[:, 0:1] + extra[:, 1:2]
-    scale = lax.rsqrt(squares / width + 1e-06)
+def activation(part_ref, recv_ref, hidden, scale):
     gate = (part_ref[:, :hidden].astype(F32) + recv_ref[:, :hidden].astype(F32)) * scale
     up = (
         part_ref[:, hidden : 2 * hidden].astype(F32) + recv_ref[:, hidden : 2 * hidden].astype(F32)
     ) * scale
-    act = (gate / (1.0 + jnp.exp(-gate)) * up).astype(BF)
-    outs = [dot(act, w_ref[a]) for a in range(groups)]
+    return (gate / (1.0 + jnp.exp(-gate)) * up).astype(BF)
+
+
+def down_first_kernel(width, split, part_ref, recv_ref, w_ref, sum_ref, scale_ref):
+    extra = part_ref[:, 2 * split :].astype(F32) + recv_ref[:, 2 * split :].astype(F32)
+    squares = extra[:, 0:1] + extra[:, 1:2]
+    scale = lax.rsqrt(squares / width + 1e-06)
+    scale_ref[...] = jnp.broadcast_to(scale, scale_ref.shape)
+    act = activation(part_ref, recv_ref, split, scale)
+    for a in range(w_ref.shape[0]):
+        sum_ref[a] = dot(act, w_ref[a, :split])
+
+
+def down_first(width, split, part, recv, weights):
+    groups, _, piece = weights.shape
+    total = part.shape[0]
+    return pl.pallas_call(
+        functools.partial(down_first_kernel, width, split),
+        in_specs=whole_vmem(3),
+        out_specs=whole_vmem(2),
+        out_shape=[in_vmem((groups, total, piece), F32), in_vmem((total, 128), F32)],
+        compiler_params=params(),
+        cost_estimate=cost(10**9, 4 * 10**6),
+        name="down_first",
+    )(part, recv, weights)
+
+
+def down_kernel(split, part_ref, recv_ref, w_ref, sum_ref, scale_ref, *out_refs):
+    groups, hidden, _ = w_ref.shape
+    capacity = part_ref.shape[0] // len(out_refs)
+    act = activation(part_ref, recv_ref, hidden - split, scale_ref[:, 0:1])
+    outs = [sum_ref[a] + dot(act, w_ref[a, split:]) for a in range(groups)]
     for d, out_ref in zip((0, *range(len(out_refs) - 1, 0, -1)), out_refs):
         rows = [out[d * capacity : (d + 1) * capacity] for out in outs]
         out_ref[...] = jnp.concatenate(rows, 0).astype(BF)
 
 
-def down(width, part, recv, weights, count):
-    groups, hidden, piece = weights.shape
+def down(split, part, recv, weights, sums, scale, count):
+    groups, _, piece = weights.shape
     rows = part.shape[0] // count * groups
     return pl.pallas_call(
-        functools.partial(down_kernel, width),
-        in_specs=whole_vmem(3),
+        functools.partial(down_kernel, split),
+        in_specs=whole_vmem(5),
         out_specs=whole_vmem(count),
-        out_shape=[struct((rows, piece), BF)] * count,
+        out_shape=[in_vmem((rows, piece), BF)] * count,
         compiler_params=params(),
         name="down",
-    )(part, recv, weights)
+    )(part, recv, weights, sums, scale)
 
 
 def combine_kernel(count, high_ref, low_ref, after_ref, *refs):
@@ -582,11 +608,11 @@
 ):
     groups, count = lax.axis_size("heads"), lax.axis_size("dp")
     width = norm_gain.shape[0]
-    other, normed, states = attention(
+    other, normed, states, weight = attention(
         slopes, queries, new_keys, new_values, head_states,
         head_gain.reshape(1, -1), out_weight, groups,
     )
-    mine = project(out_weight, normed, groups)
+    mine = project(normed, weight, other.shape)
     own, *sends = split(mine, swap(other, "side", 1))
     weights = regroup(w_down, own)
     flat = add_residual(residual, weights, own, swaps(sends, "heads"))
@@ -596,13 +622,17 @@
         jnp.transpose(expert_ids, (1, 2, 0)), jnp.transpose(expert_gates, (1, 2, 0)), flat,
         capacity, count,
     )
-    w_gate = load(w_gate, flat)
     gathered = [flat] + swaps([flat] * (groups - 1), "heads")[::-1]
-    own, *sends = dispatch(w_gate, pick, gathered, count)
-    w_up = load(w_up, own)
-    xs = [own] + swaps(sends, "dp")[::-1]
-    part = gate_up(norm_gain.reshape(1, -1), w_gate, w_up, xs)
-    own, *sends = down(width, part, swap(part, "side", 1), weights, count)
+    own, *sends = dispatch(pick, gathered, count)
+    xs = [own] + swaps(sends, "dp")
+    hidden = w_gate.shape[3]
+    split_at = hidden // 256 * 128
+    part, lhs = first_units(split_at, norm_gain.reshape(1, -1), w_gate, w_up, xs)
+    other_part = other_units(split_at, lhs, w_gate, w_up)
+    sums, scale = down_first(width, split_at, part, swap(part, "side", 1), weights)
+    own, *sends = down(
+        split_at, other_part, swap(other_part, "side", 1), weights, sums, scale, count
+    )
     state_out, done = new_state(slopes, new_keys, new_values, states, own)
     ys = [own] + swaps(sends, "dp")[::-1]
     own, *sends = combine(high, low, done, ys, groups)

time: 54.1 us -> 53.1 us (0.982)
  Pallas kernels: 20.1 us -> 15 us
  waiting for transfers between devices: 11 us -> 14.2 us
  starting transfers between devices: 21.9 us -> 22.8 us
    pallas_call x6, Pallas kernels: 9.11 us -> 3.71 us  [the longest x1 0.87 us: other_units(): pl.pallas_call(functools.partial(other_kernel, split), in_specs=whole_vme...]
    ppermute x17 -> x18, waiting for transfers between devices: 11 us -> 14.2 us  [swap(): return lax.ppermute(x, axis, [(i, i ^ k) for i in range(size)])]
    ppermute x17 -> x18, starting transfers between devices: 21.9 us -> 22.8 us  [swap(): return lax.ppermute(x, axis, [(i, i ^ k) for i in range(size)])]
  transfers between devices with their start and end apart: 17 -> 18, of which waited for: 8 -> 13; matrix products, arithmetic and copies ran while one was open for 0% -> 0% of each run, Pallas kernels for 22% -> 15%
where the time goes in v4:
time: 53.1 us; the launch traced here: 52.9 us
  starting transfers between devices  22.8 us (43%)
  Pallas kernels  15 us (28%)
  waiting for transfers between devices  14.2 us (27%)
  between operations  0.81 us (2%)
    ppermute x18, starting transfers between devices, swap(): return lax.ppermute(x, axis, [(i, i ^ k) for i in range(size)])  22.8 us
    ppermute x18, waiting for transfers between devices, swap(): return lax.ppermute(x, axis, [(i, i ^ k) for i in range(size)])  14.2 us
    pallas_call x1, Pallas kernels, attention(): pl.pallas_call(attention_kernel, in_specs=hbm_specs(7), out_specs=whole_v...  4.15 us
    pallas_call x1, Pallas kernels, new_state(): pl.pallas_call(state_kernel, in_specs=[pl.BlockSpec(memory_space=pltpu.SM...  2.88 us
    pallas_call x1, Pallas kernels, regroup(): pl.pallas_call(regroup_kernel, in_specs=[*hbm_specs(1), pl.BlockSpec(memo...  2.37 us
  transfers between devices with their start and end apart: 18, of which 13 were waited for; matrix products, arithmetic and copies ran while one was open for 0% of the time, Pallas kernels for 15%

profile of v4, /device:TPU:0, one launch (start us, length us, event | category | flops | bytes accessed | tf_op | source)
XLA Modules:
  0.0 52.9 jit_solution(6420167147479421195)
XLA Ops:
  0.6 4.1 %attention.1 = (bf16[4,48,384]{2,1,0:T(8,128)(2,1)S(1)}, bf16[48,512]{1,0:T(8,128)(2,1)S(1)}, bf16[24,4,128,128]{3,2,1,0:T(8,128)(2,1)S(1)}, bf16[4,512,384]{2,1,0:T(8,128)(2,1)S(1)}) custom-call(f32[4]{0:T(128)} %slope_ref.1, bf16[24,2,512]{2,1,0:T(2,128)(2,1)} %q_hbm.1, bf16[24,2,512]{2,1,0:T(2,128)(2,1)} %k_ref.1, bf16[24,2,512]{2,1,0:T(2,128)(2,1)} %v_ref.1, ...), custom_call_target="tpu_custom_call" | custom-call | tf_op jit(solution)/shard_map/attention/pallas_call | solution.py:154
  5.7 0.7 %collective-permute-done.recv_ref = bf16[4,48,384]{2,1,0:T(8,128)(2,1)S(1)} collective-permute-done((bf16[4,48,384]{2,1,0:T(8,128)(2,1)S(1)}, bf16[4,48,384]{2,1,0:T(8,128)(2,1)S(1)}, u32[]{:S(2)}, u32[]{:S(2)}) %collective-permute-start) | collective-permute-done | bytes 147488 | tf_op jit(solution)/shard_map/ppermute | solution.py:598
  6.3 5.0 %collective-permute-start.1 = (bf16[48,384]{1,0:T(8,128)(2,1)S(1)}, bf16[48,384]{1,0:T(8,128)(2,1)S(1)}, u32[]{:S(2)}, u32[]{:S(2)}) collective-permute-start(bf16[48,384]{1,0:T(8,128)(2,1)S(1)} %get-tuple-element.37), channel_id=1, source_target_pairs={{0,6},{2,4},{4,2},{6,0},{1,7},{3,5},{5,3},{7,1},{8,14},{10,12},{12... | collective-permute-start | bytes 110600 | tf_op jit(solution)/shard_map/ppermute | solution.py:598
  11.4 0.6 %collective-permute-start.3 = (bf16[48,384]{1,0:T(8,128)(2,1)S(1)}, bf16[48,384]{1,0:T(8,128)(2,1)S(1)}, u32[]{:S(2)}, u32[]{:S(2)}) collective-permute-start(bf16[48,384]{1,0:T(8,128)(2,1)S(1)} %get-tuple-element.39), channel_id=1, source_target_pairs={{0,2},{2,0},{4,6},{6,4},{1,3},{3,1},{5,7},{7,5},{8,10},{10,8},{12,... | collective-permute-start | bytes 110600 | tf_op jit(solution)/shard_map/ppermute | solution.py:598
  12.0 2.4 %regroup_down.1.after_ref.w_ref = bf16[4,1152,384]{2,1,0:T(8,128)(2,1)S(1)} custom-call(bf16[1,1152,4,384]{3,2,1,0:T(4,128)(2,1)} %w_hbm.3, f32[48,384]{1,0:T(8,128)S(1)} %get-tuple-element.36.after_ref.own_ref), custom_call_target="tpu_custom_call" | custom-call | flops 100000000 | bytes 7000000 | tf_op jit(solution)/shard_map/regroup_down/pallas_call | solution.py:480
  14.5 1.8 %collective-permute-done.2.refs_1_ = bf16[48,384]{1,0:T(8,128)(2,1)S(1)} collective-permute-done((bf16[48,384]{1,0:T(8,128)(2,1)S(1)}, bf16[48,384]{1,0:T(8,128)(2,1)S(1)}, u32[]{:S(2)}, u32[]{:S(2)}) %collective-permute-start.2) | collective-permute-done | bytes 36896 | tf_op jit(solution)/shard_map/ppermute | solution.py:598
  16.3 2.1 %collective-permute-start.6 = (bf16[48,384]{1,0:T(8,128)(2,1)S(1)}, bf16[48,384]{1,0:T(8,128)(2,1)S(1)}, u32[]{:S(2)}, u32[]{:S(2)}) collective-permute-start(bf16[48,384]{1,0:T(8,128)(2,1)S(1)} %add_residual.1.after_ref.refs_0_.flat_ref), channel_id=1, source_target_pairs={{0,6},{2,4},{4,2},{6,0},{1,7},{3,5},{5,3},{7,1},{8,14},{10,12},{12... | collective-permute-start | bytes 110600 | tf_op jit(solution)/shard_map/ppermute | solution.py:598
  18.5 2.3 %collective-permute-start.4 = (bf16[48,384]{1,0:T(8,128)(2,1)S(1)}, bf16[48,384]{1,0:T(8,128)(2,1)S(1)}, u32[]{:S(2)}, u32[]{:S(2)}) collective-permute-start(bf16[48,384]{1,0:T(8,128)(2,1)S(1)} %add_residual.1.after_ref.refs_0_.flat_ref), channel_id=1, source_target_pairs={{0,2},{2,0},{4,6},{6,4},{1,3},{3,1},{5,7},{7,5},{8,10},{10,8},{12,... | collective-permute-start | bytes 110600 | tf_op jit(solution)/shard_map/ppermute | solution.py:598
  21.0 1.2 %collective-permute-done.6.refs_3_ = bf16[48,384]{1,0:T(8,128)(2,1)S(1)} collective-permute-done((bf16[48,384]{1,0:T(8,128)(2,1)S(1)}, bf16[48,384]{1,0:T(8,128)(2,1)S(1)}, u32[]{:S(2)}, u32[]{:S(2)}) %collective-permute-start.6) | collective-permute-done | bytes 36896 | tf_op jit(solution)/shard_map/ppermute | solution.py:598
  22.2 1.4 %collective-permute-done.5.refs_2_ = bf16[48,384]{1,0:T(8,128)(2,1)S(1)} collective-permute-done((bf16[48,384]{1,0:T(8,128)(2,1)S(1)}, bf16[48,384]{1,0:T(8,128)(2,1)S(1)}, u32[]{:S(2)}, u32[]{:S(2)}) %collective-permute-start.5) | collective-permute-done | bytes 36896 | tf_op jit(solution)/shard_map/ppermute | solution.py:598
  24.0 2.5 %collective-permute-start.7 = (bf16[144,384]{1,0:T(8,128)(2,1)S(1)}, bf16[144,384]{1,0:T(8,128)(2,1)S(1)}, u32[]{:S(2)}, u32[]{:S(2)}) collective-permute-start(bf16[144,384]{1,0:T(8,128)(2,1)S(1)} %get-tuple-element.42), channel_id=1, source_target_pairs={{0,24},{8,16},{16,8},{24,0},{1,25},{9,17},{17,9},{25,1},{2,26},{10... | collective-permute-start | bytes 331784 | tf_op jit(solution)/shard_map/ppermute | solution.py:598
  27.0 0.5 %collective-permute-start.9 = (bf16[144,384]{1,0:T(8,128)(2,1)S(1)}, bf16[144,384]{1,0:T(8,128)(2,1)S(1)}, u32[]{:S(2)}, u32[]{:S(2)}) collective-permute-start(bf16[144,384]{1,0:T(8,128)(2,1)S(1)} %get-tuple-element.44), channel_id=1, source_target_pairs={{0,8},{8,0},{16,24},{24,16},{1,9},{9,1},{17,25},{25,17},{2,10},{10... | collective-permute-start | bytes 331784 | tf_op jit(solution)/shard_map/ppermute | solution.py:598
  27.5 2.5 %collective-permute-done.7.refs_1_ = bf16[144,384]{1,0:T(8,128)(2,1)S(1)} collective-permute-done((bf16[144,384]{1,0:T(8,128)(2,1)S(1)}, bf16[144,384]{1,0:T(8,128)(2,1)S(1)}, u32[]{:S(2)}, u32[]{:S(2)}) %collective-permute-start.7) | collective-permute-done | bytes 110624 | tf_op jit(solution)/shard_map/ppermute | solution.py:598
  30.0 1.2 %collective-permute-done.8.refs_2_ = bf16[144,384]{1,0:T(8,128)(2,1)S(1)} collective-permute-done((bf16[144,384]{1,0:T(8,128)(2,1)S(1)}, bf16[144,384]{1,0:T(8,128)(2,1)S(1)}, u32[]{:S(2)}, u32[]{:S(2)}) %collective-permute-start.8) | collective-permute-done | bytes 110624 | tf_op jit(solution)/shard_map/ppermute | solution.py:598
  31.7 0.7 %first_units.1 = (bf16[144,1152]{1,0:T(8,128)(2,1)S(1)}, bf16[144,1536]{1,0:T(8,128)(2,1)S(1)}) custom-call(f32[1,3072]{1,0:T(1,128)S(1)} %bitcast.4, bf16[1,4,384,1152]{3,2,1,0:T(8,128)(2,1)S(1)} %copy-done, bf16[1,4,384,1152]{3,2,1,0:T(8,128)(2,1)S(1)} %copy-done.1, bf16[144,384]{1,0:T(8,128)(2,1)S(1)} %get-tuple-element.41.refs_0_, ...), custom_call_target="tpu_custom_call" | custom-call | tf_op jit(solution)/shard_map/first_units/pallas_call | solution.py:422
  32.5 0.9 %other_units.1.part_ref = bf16[144,1280]{1,0:T(8,128)(2,1)S(1)} custom-call(bf16[144,1536]{1,0:T(8,128)(2,1)S(1)} %get-tuple-element.45.lhs_ref, bf16[1,4,384,1152]{3,2,1,0:T(8,128)(2,1)S(1)} %copy-done, bf16[1,4,384,1152]{3,2,1,0:T(8,128)(2,1)S(1)} %copy-done.1), custom_call_target="tpu_custom_call" | custom-call | flops 1000000000 | bytes 4000000 | tf_op jit(solution)/shard_map/other_units/pallas_call | solution.py:441
  33.4 0.6 %collective-permute-start.10 = (bf16[144,1280]{1,0:T(8,128)(2,1)S(1)}, bf16[144,1280]{1,0:T(8,128)(2,1)S(1)}, u32[]{:S(2)}, u32[]{:S(2)}) collective-permute-start(bf16[144,1280]{1,0:T(8,128)(2,1)S(1)} %other_units.1.part_ref), channel_id=1, source_target_pairs={{0,1},{1,0},{2,3},{3,2},{4,5},{5,4},{6,7},{7,6},{8,9},{9,8},{10,11... | collective-permute-start | bytes 1105928 | tf_op jit(solution)/shard_map/ppermute | solution.py:598
  34.2 0.7 %down_first.1 = (f32[4,144,384]{2,1,0:T(8,128)S(1)}, f32[144,128]{1,0:T(8,128)S(1)}) custom-call(bf16[144,1152]{1,0:T(8,128)(2,1)S(1)} %get-tuple-element.46.part_ref, bf16[144,1152]{1,0:T(8,128)(2,1)S(1)} %collective-permute-done.11.recv_ref, bf16[4,1152,384]{2,1,0:T(8,128)(2,1)S(1)} %regroup_down.1.after_ref.w_ref), custom_call_target="tpu_custom_call" | custom-call | flops 1000000000 | bytes 4000000 | tf_op jit(solution)/shard_map/down_first/pallas_call | solution.py:516
  35.3 0.8 %down.1 = (bf16[144,384]{1,0:T(8,128)(2,1)S(1)}, bf16[144,384]{1,0:T(8,128)(2,1)S(1)}, bf16[144,384]{1,0:T(8,128)(2,1)S(1)}, bf16[144,384]{1,0:T(8,128)(2,1)S(1)}) custom-call(bf16[144,1280]{1,0:T(8,128)(2,1)S(1)} %other_units.1.part_ref, bf16[144,1280]{1,0:T(8,128)(2,1)S(1)} %collective-permute-done.10.recv_ref, ...), custom_call_target="tpu_custom_call" | custom-call | tf_op jit(solution)/shard_map/down/pallas_call | solution.py:540
  36.1 0.8 %collective-permute-start.12 = (bf16[144,384]{1,0:T(8,128)(2,1)S(1)}, bf16[144,384]{1,0:T(8,128)(2,1)S(1)}, u32[]{:S(2)}, u32[]{:S(2)}) collective-permute-start(bf16[144,384]{1,0:T(8,128)(2,1)S(1)} %get-tuple-element.54), channel_id=1, source_target_pairs={{0,8},{8,0},{16,24},{24,16},{1,9},{9,1},{17,25},{25,17},{2,10},{10... | collective-permute-start | bytes 331784 | tf_op jit(solution)/shard_map/ppermute | solution.py:598
  36.9 1.3 %collective-permute-start.13 = (bf16[144,384]{1,0:T(8,128)(2,1)S(1)}, bf16[144,384]{1,0:T(8,128)(2,1)S(1)}, u32[]{:S(2)}, u32[]{:S(2)}) collective-permute-start(bf16[144,384]{1,0:T(8,128)(2,1)S(1)} %get-tuple-element.55), channel_id=1, source_target_pairs={{0,16},{8,24},{16,0},{24,8},{1,17},{9,25},{17,1},{25,9},{2,18},{10... | collective-permute-start | bytes 331784 | tf_op jit(solution)/shard_map/ppermute | solution.py:598
  38.2 1.4 %collective-permute-start.14 = (bf16[144,384]{1,0:T(8,128)(2,1)S(1)}, bf16[144,384]{1,0:T(8,128)(2,1)S(1)}, u32[]{:S(2)}, u32[]{:S(2)}) collective-permute-start(bf16[144,384]{1,0:T(8,128)(2,1)S(1)} %get-tuple-element.56), channel_id=1, source_target_pairs={{0,24},{8,16},{16,8},{24,0},{1,25},{9,17},{17,9},{25,1},{2,26},{10... | collective-permute-start | bytes 331784 | tf_op jit(solution)/shard_map/ppermute | solution.py:598
  39.6 2.9 %new_state.1 = (bf16[24,4,128,128]{3,2,1,0:T(8,128)(2,1)}, f32[8,128]{1,0:T(8,128)S(1)}) custom-call(f32[4]{0:T(128)S(1)} %copy-done.8, bf16[24,2,512]{2,1,0:T(2,128)(2,1)S(1)} %copy-done.2, bf16[24,2,512]{2,1,0:T(2,128)(2,1)S(1)} %copy-done.3, bf16[24,4,128,128]{3,2,1,0:T(8,128)(2,1)S(1)} %get-tuple-element.32.s_ref, ...), custom_call_target="tpu_custom_call" | custom-call | flops 100000000 | bytes 8000000 | tf_op jit(solution)/shard_map/new_state/pallas_call | solution.py:233
  42.5 0.6 %collective-permute-done.13.refs_2_ = bf16[144,384]{1,0:T(8,128)(2,1)S(1)} collective-permute-done((bf16[144,384]{1,0:T(8,128)(2,1)S(1)}, bf16[144,384]{1,0:T(8,128)(2,1)S(1)}, u32[]{:S(2)}, u32[]{:S(2)}) %collective-permute-start.13) | collective-permute-done | bytes 110624 | tf_op jit(solution)/shard_map/ppermute | solution.py:598
  43.2 1.6 %collective-permute-done.14.refs_3_ = bf16[144,384]{1,0:T(8,128)(2,1)S(1)} collective-permute-done((bf16[144,384]{1,0:T(8,128)(2,1)S(1)}, bf16[144,384]{1,0:T(8,128)(2,1)S(1)}, u32[]{:S(2)}, u32[]{:S(2)}) %collective-permute-start.14) | collective-permute-done | bytes 110624 | tf_op jit(solution)/shard_map/ppermute | solution.py:598
  45.1 2.1 %collective-permute-start.15 = (bf16[48,384]{1,0:T(8,128)(2,1)S(1)}, bf16[48,384]{1,0:T(8,128)(2,1)S(1)}, u32[]{:S(2)}, u32[]{:S(2)}) collective-permute-start(bf16[48,384]{1,0:T(8,128)(2,1)S(1)} %get-tuple-element.58), channel_id=1, source_target_pairs={{0,6},{2,4},{4,2},{6,0},{1,7},{3,5},{5,3},{7,1},{8,14},{10,12},{12... | collective-permute-start | bytes 110600 | tf_op jit(solution)/shard_map/ppermute | solution.py:598
  47.2 0.5 collective-permute-start.16
  47.8 1.8 %collective-permute-start.17 = (bf16[48,384]{1,0:T(8,128)(2,1)S(1)}, bf16[48,384]{1,0:T(8,128)(2,1)S(1)}, u32[]{:S(2)}, u32[]{:S(2)}) collective-permute-start(bf16[48,384]{1,0:T(8,128)(2,1)S(1)} %get-tuple-element.60), channel_id=1, source_target_pairs={{0,2},{2,0},{4,6},{6,4},{1,3},{3,1},{5,7},{7,5},{8,10},{10,8},{12,... | collective-permute-start | bytes 110600 | tf_op jit(solution)/shard_map/ppermute | solution.py:598
  49.6 0.6 %by_request.1 = bf16[24,2,384]{2,1,0:T(2,128)(2,1)} custom-call(bf16[48,384]{1,0:T(8,128)(2,1)S(1)} %add_residual.1.after_ref.refs_0_.flat_ref), custom_call_target="tpu_custom_call" | custom-call | flops 100000 | bytes 1000000 | tf_op jit(solution)/shard_map/by_request/pallas_call | solution.py:297
  50.2 0.8 %collective-permute-done.15.refs_0_ = bf16[48,384]{1,0:T(8,128)(2,1)S(1)} collective-permute-done((bf16[48,384]{1,0:T(8,128)(2,1)S(1)}, bf16[48,384]{1,0:T(8,128)(2,1)S(1)}, u32[]{:S(2)}, u32[]{:S(2)}) %collective-permute-start.15) | collective-permute-done | bytes 36896 | tf_op jit(solution)/shard_map/ppermute | solution.py:598
  51.0 1.2 %collective-permute-done.16.refs_1_ = bf16[48,384]{1,0:T(8,128)(2,1)S(1)} collective-permute-done((bf16[48,384]{1,0:T(8,128)(2,1)S(1)}, bf16[48,384]{1,0:T(8,128)(2,1)S(1)}, u32[]{:S(2)}, u32[]{:S(2)}) %collective-permute-start.16) | collective-permute-done | bytes 36896 | tf_op jit(solution)/shard_map/ppermute | solution.py:598
  52.3 0.7 %finish.1 = bf16[24,2,384]{2,1,0:T(2,128)(2,1)} custom-call(f32[48,384]{1,0:T(8,128)S(1)} %get-tuple-element.57.own_ref, bf16[48,384]{1,0:T(8,128)(2,1)S(1)} %collective-permute-done.15.refs_0_, bf16[48,384]{1,0:T(8,128)(2,1)S(1)} %collective-permute-done.16.refs_1_, bf16[48,384]{1,0:T(8,128)(2,1)S(1)} %collective-permute-done.17.refs_2_), custom_call_target="tpu_custom_call" | custom-call | tf_op jit(solution)/shard_map/finish/pallas_call | solution.py:586
  (37 shorter events, 3.7 us)
Async XLA Ops:
  4.8 1.5 %collective-permute-start = (bf16[4,48,384]{2,1,0:T(8,128)(2,1)S(1)}, bf16[4,48,384]{2,1,0:T(8,128)(2,1)S(1)}, u32[]{:S(2)}, u32[]{:S(2)}) collective-permute-start(bf16[4,48,384]{2,1,0:T(8,128)(2,1)S(1)} %get-tuple-element.35), channel_id=1, source_target_pairs={{0,1},{1,0},{2,3},{3,2},{4,5},{5,4},{6,7},{7,6},{8,9},{9,8},{10,11... | collective-permute-start | bytes 442376 | tf_op jit(solution)/shard_map/ppermute | solution.py:598
  6.3 8.1 %collective-permute-start.1 = (bf16[48,384]{1,0:T(8,128)(2,1)S(1)}, bf16[48,384]{1,0:T(8,128)(2,1)S(1)}, u32[]{:S(2)}, u32[]{:S(2)}) collective-permute-start(bf16[48,384]{1,0:T(8,128)(2,1)S(1)} %get-tuple-element.37), channel_id=1, source_target_pairs={{0,6},{2,4},{4,2},{6,0},{1,7},{3,5},{5,3},{7,1},{8,14},{10,12},{12... | collective-permute-start | bytes 110600 | tf_op jit(solution)/shard_map/ppermute | solution.py:598
  11.4 4.9 %collective-permute-start.2 = (bf16[48,384]{1,0:T(8,128)(2,1)S(1)}, bf16[48,384]{1,0:T(8,128)(2,1)S(1)}, u32[]{:S(2)}, u32[]{:S(2)}) collective-permute-start(bf16[48,384]{1,0:T(8,128)(2,1)S(1)} %get-tuple-element.38), channel_id=1, source_target_pairs={{0,4},{2,6},{4,0},{6,2},{1,5},{3,7},{5,1},{7,3},{8,12},{10,14},{12... | collective-permute-start | bytes 110600 | tf_op jit(solution)/shard_map/ppermute | solution.py:598
  11.4 4.9 %collective-permute-start.3 = (bf16[48,384]{1,0:T(8,128)(2,1)S(1)}, bf16[48,384]{1,0:T(8,128)(2,1)S(1)}, u32[]{:S(2)}, u32[]{:S(2)}) collective-permute-start(bf16[48,384]{1,0:T(8,128)(2,1)S(1)} %get-tuple-element.39), channel_id=1, source_target_pairs={{0,2},{2,0},{4,6},{6,4},{1,3},{3,1},{5,7},{7,5},{8,10},{10,8},{12,... | collective-permute-start | bytes 110600 | tf_op jit(solution)/shard_map/ppermute | solution.py:598
  12.0 4.2 %copy-start.4 = (bf16[24,2,384]{2,1,0:T(2,128)(2,1)S(1)}, bf16[24,2,384]{2,1,0:T(2,128)(2,1)}, u32[]{:S(2)}) copy-start(bf16[24,2,384]{2,1,0:T(2,128)(2,1)} %residual_ref.1) | copy-start | bytes 110596
  12.0 19.7 %copy-start.1 = (bf16[1,4,384,1152]{3,2,1,0:T(8,128)(2,1)S(1)}, bf16[1,4,384,1152]{3,2,1,0:T(8,128)(2,1)}, u32[]{:S(2)}) copy-start(bf16[1,4,384,1152]{3,2,1,0:T(8,128)(2,1)} %wu_ref.3) | copy-start | bytes 10616836
  14.4 6.3 %copy-start.6 = (s32[24,2,2]{0,2,1:T(2,128)S(1)}, s32[24,2,2]{0,2,1:T(2,128)}, u32[]{:S(2)}) copy-start(s32[24,2,2]{0,2,1:T(2,128)} %param.23) | copy-start | bytes 1156
  14.4 6.3 %copy-start.7 = (f32[24,2,2]{0,2,1:T(2,128)S(1)}, f32[24,2,2]{0,2,1:T(2,128)}, u32[]{:S(2)}) copy-start(f32[24,2,2]{0,2,1:T(2,128)} %param.24) | copy-start | bytes 1156
  14.4 17.3 %copy-start = (bf16[1,4,384,1152]{3,2,1,0:T(8,128)(2,1)S(1)}, bf16[1,4,384,1152]{3,2,1,0:T(8,128)(2,1)}, u32[]{:S(2)}) copy-start(bf16[1,4,384,1152]{3,2,1,0:T(8,128)(2,1)} %wg_ref.3) | copy-start | bytes 10616836
  14.4 17.3 %copy-start.5 = (f32[3072]{0:T(1024)S(1)}, f32[3072]{0:T(1024)}, u32[]{:S(2)}) copy-start(f32[3072]{0:T(1024)} %param.22) | copy-start | bytes 36868
  16.3 5.9 %collective-permute-start.6 = (bf16[48,384]{1,0:T(8,128)(2,1)S(1)}, bf16[48,384]{1,0:T(8,128)(2,1)S(1)}, u32[]{:S(2)}, u32[]{:S(2)}) collective-permute-start(bf16[48,384]{1,0:T(8,128)(2,1)S(1)} %add_residual.1.after_ref.refs_0_.flat_ref), channel_id=1, source_target_pairs={{0,6},{2,4},{4,2},{6,0},{1,7},{3,5},{5,3},{7,1},{8,14},{10,12},{12... | collective-permute-start | bytes 110600 | tf_op jit(solution)/shard_map/ppermute | solution.py:598
  18.4 5.3 %collective-permute-start.5 = (bf16[48,384]{1,0:T(8,128)(2,1)S(1)}, bf16[48,384]{1,0:T(8,128)(2,1)S(1)}, u32[]{:S(2)}, u32[]{:S(2)}) collective-permute-start(bf16[48,384]{1,0:T(8,128)(2,1)S(1)} %add_residual.1.after_ref.refs_0_.flat_ref), channel_id=1, source_target_pairs={{0,4},{2,6},{4,0},{6,2},{1,5},{3,7},{5,1},{7,3},{8,12},{10,14},{12... | collective-permute-start | bytes 110600 | tf_op jit(solution)/shard_map/ppermute | solution.py:598
  18.5 5.2 %collective-permute-start.4 = (bf16[48,384]{1,0:T(8,128)(2,1)S(1)}, bf16[48,384]{1,0:T(8,128)(2,1)S(1)}, u32[]{:S(2)}, u32[]{:S(2)}) collective-permute-start(bf16[48,384]{1,0:T(8,128)(2,1)S(1)} %add_residual.1.after_ref.refs_0_.flat_ref), channel_id=1, source_target_pairs={{0,2},{2,0},{4,6},{6,4},{1,3},{3,1},{5,7},{7,5},{8,10},{10,8},{12,... | collective-permute-start | bytes 110600 | tf_op jit(solution)/shard_map/ppermute | solution.py:598
  24.0 6.0 %collective-permute-start.7 = (bf16[144,384]{1,0:T(8,128)(2,1)S(1)}, bf16[144,384]{1,0:T(8,128)(2,1)S(1)}, u32[]{:S(2)}, u32[]{:S(2)}) collective-permute-start(bf16[144,384]{1,0:T(8,128)(2,1)S(1)} %get-tuple-element.42), channel_id=1, source_target_pairs={{0,24},{8,16},{16,8},{24,0},{1,25},{9,17},{17,9},{25,1},{2,26},{10... | collective-permute-start | bytes 331784 | tf_op jit(solution)/shard_map/ppermute | solution.py:598
  26.5 4.7 %collective-permute-start.8 = (bf16[144,384]{1,0:T(8,128)(2,1)S(1)}, bf16[144,384]{1,0:T(8,128)(2,1)S(1)}, u32[]{:S(2)}, u32[]{:S(2)}) collective-permute-start(bf16[144,384]{1,0:T(8,128)(2,1)S(1)} %get-tuple-element.43), channel_id=1, source_target_pairs={{0,16},{8,24},{16,0},{24,8},{1,17},{9,25},{17,1},{25,9},{2,18},{10... | collective-permute-start | bytes 331784 | tf_op jit(solution)/shard_map/ppermute | solution.py:598
  27.0 4.7 %collective-permute-start.9 = (bf16[144,384]{1,0:T(8,128)(2,1)S(1)}, bf16[144,384]{1,0:T(8,128)(2,1)S(1)}, u32[]{:S(2)}, u32[]{:S(2)}) collective-permute-start(bf16[144,384]{1,0:T(8,128)(2,1)S(1)} %get-tuple-element.44), channel_id=1, source_target_pairs={{0,8},{8,0},{16,24},{24,16},{1,9},{9,1},{17,25},{25,17},{2,10},{10... | collective-permute-start | bytes 331784 | tf_op jit(solution)/shard_map/ppermute | solution.py:598
  32.5 1.7 %collective-permute-start.11 = (bf16[144,1152]{1,0:T(8,128)(2,1)S(1)}, bf16[144,1152]{1,0:T(8,128)(2,1)S(1)}, u32[]{:S(2)}, u32[]{:S(2)}) collective-permute-start(bf16[144,1152]{1,0:T(8,128)(2,1)S(1)} %get-tuple-element.46.part_ref), channel_id=1, source_target_pairs={{0,1},{1,0},{2,3},{3,2},{4,5},{5,4},{6,7},{7,6},{8,9},{9,8},{10,11... | collective-permute-start | bytes 995336 | tf_op jit(solution)/shard_map/ppermute | solution.py:598
  33.4 1.9 %collective-permute-start.10 = (bf16[144,1280]{1,0:T(8,128)(2,1)S(1)}, bf16[144,1280]{1,0:T(8,128)(2,1)S(1)}, u32[]{:S(2)}, u32[]{:S(2)}) collective-permute-start(bf16[144,1280]{1,0:T(8,128)(2,1)S(1)} %other_units.1.part_ref), channel_id=1, source_target_pairs={{0,1},{1,0},{2,3},{3,2},{4,5},{5,4},{6,7},{7,6},{8,9},{9,8},{10,11... | collective-permute-start | bytes 1105928 | tf_op jit(solution)/shard_map/ppermute | solution.py:598
  34.8 4.8 %copy-start.2 = (bf16[24,2,512]{2,1,0:T(2,128)(2,1)S(1)}, bf16[24,2,512]{2,1,0:T(2,128)(2,1)}, u32[]{:S(2)}) copy-start(bf16[24,2,512]{2,1,0:T(2,128)(2,1)} %k_ref.1) | copy-start | bytes 147460
  34.9 4.8 %copy-start.3 = (bf16[24,2,512]{2,1,0:T(2,128)(2,1)S(1)}, bf16[24,2,512]{2,1,0:T(2,128)(2,1)}, u32[]{:S(2)}) copy-start(bf16[24,2,512]{2,1,0:T(2,128)(2,1)} %v_ref.1) | copy-start | bytes 147460
  34.9 4.8 %copy-start.8 = (f32[4]{0:T(128)S(1)}, f32[4]{0:T(128)}, u32[]{:S(2)}) copy-start(f32[4]{0:T(128)} %slope_ref.1) | copy-start | bytes 52
  36.1 6.5 %collective-permute-start.12 = (bf16[144,384]{1,0:T(8,128)(2,1)S(1)}, bf16[144,384]{1,0:T(8,128)(2,1)S(1)}, u32[]{:S(2)}, u32[]{:S(2)}) collective-permute-start(bf16[144,384]{1,0:T(8,128)(2,1)S(1)} %get-tuple-element.54), channel_id=1, source_target_pairs={{0,8},{8,0},{16,24},{24,16},{1,9},{9,1},{17,25},{25,17},{2,10},{10... | collective-permute-start | bytes 331784 | tf_op jit(solution)/shard_map/ppermute | solution.py:598
  36.9 6.3 %collective-permute-start.13 = (bf16[144,384]{1,0:T(8,128)(2,1)S(1)}, bf16[144,384]{1,0:T(8,128)(2,1)S(1)}, u32[]{:S(2)}, u32[]{:S(2)}) collective-permute-start(bf16[144,384]{1,0:T(8,128)(2,1)S(1)} %get-tuple-element.55), channel_id=1, source_target_pairs={{0,16},{8,24},{16,0},{24,8},{1,17},{9,25},{17,1},{25,9},{2,18},{10... | collective-permute-start | bytes 331784 | tf_op jit(solution)/shard_map/ppermute | solution.py:598
  38.2 6.6 %collective-permute-start.14 = (bf16[144,384]{1,0:T(8,128)(2,1)S(1)}, bf16[144,384]{1,0:T(8,128)(2,1)S(1)}, u32[]{:S(2)}, u32[]{:S(2)}) collective-permute-start(bf16[144,384]{1,0:T(8,128)(2,1)S(1)} %get-tuple-element.56), channel_id=1, source_target_pairs={{0,24},{8,16},{16,8},{24,0},{1,25},{9,17},{17,9},{25,1},{2,26},{10... | collective-permute-start | bytes 331784 | tf_op jit(solution)/shard_map/ppermute | solution.py:598
  45.1 5.9 %collective-permute-start.15 = (bf16[48,384]{1,0:T(8,128)(2,1)S(1)}, bf16[48,384]{1,0:T(8,128)(2,1)S(1)}, u32[]{:S(2)}, u32[]{:S(2)}) collective-permute-start(bf16[48,384]{1,0:T(8,128)(2,1)S(1)} %get-tuple-element.58), channel_id=1, source_target_pairs={{0,6},{2,4},{4,2},{6,0},{1,7},{3,5},{5,3},{7,1},{8,14},{10,12},{12... | collective-permute-start | bytes 110600 | tf_op jit(solution)/shard_map/ppermute | solution.py:598
  47.2 5.0 %collective-permute-start.16 = (bf16[48,384]{1,0:T(8,128)(2,1)S(1)}, bf16[48,384]{1,0:T(8,128)(2,1)S(1)}, u32[]{:S(2)}, u32[]{:S(2)}) collective-permute-start(bf16[48,384]{1,0:T(8,128)(2,1)S(1)} %get-tuple-element.59), channel_id=1, source_target_pairs={{0,4},{2,6},{4,0},{6,2},{1,5},{3,7},{5,1},{7,3},{8,12},{10,14},{12... | collective-permute-start | bytes 110600 | tf_op jit(solution)/shard_map/ppermute | solution.py:598
  47.8 4.5 %collective-permute-start.17 = (bf16[48,384]{1,0:T(8,128)(2,1)S(1)}, bf16[48,384]{1,0:T(8,128)(2,1)S(1)}, u32[]{:S(2)}, u32[]{:S(2)}) collective-permute-start(bf16[48,384]{1,0:T(8,128)(2,1)S(1)} %get-tuple-element.60), channel_id=1, source_target_pairs={{0,2},{2,0},{4,6},{6,4},{1,3},{3,1},{5,7},{7,5},{8,10},{10,8},{12,... | collective-permute-start | bytes 110600 | tf_op jit(solution)/shard_map/ppermute | solution.py:598

commit v5 on v4

--- a/solution.py
+++ b/solution.py
@@ -45,13 +45,18 @@
     return jnp.dot(a, b, preferred_element_type=F32)
 
 
-def load_columns(w_hbm, weight, sems, side):
+def side_of(a, mine):
+    side = lax.axis_index("side")
+    return jnp.where((lax.axis_index("heads") == a) == mine, side, 1 - side)
+
+
+def load_columns(w_hbm, weight, sems, mine):
     groups, _, piece = weight.shape
     if groups == 1:
         return [pltpu.make_async_copy(w_hbm, weight.at[0], sems.at[0])]
     return [
         pltpu.make_async_copy(
-            w_hbm.at[:, pl.ds(pl.multiple_of((2 * a + side) * piece, 128), piece)],
+            w_hbm.at[:, pl.ds(pl.multiple_of((2 * a + side_of(a, mine)) * piece, 128), piece)],
             weight.at[a],
             sems.at[a],
         )
@@ -65,7 +70,7 @@
     return (groups, rows, piece) if piece % 128 == 0 else (1, rows, width)
 
 
-def project_columns(loads, weight, normed, side, out_ref):
+def project_columns(loads, weight, normed, mine, out_ref):
     groups, _, piece = out_ref.shape
     if weight.shape[0] == groups:
         for a in range(groups):
@@ -77,7 +82,7 @@
         copy.wait()
     for a in range(groups):
         both = dot(normed, weight[0, :, 2 * a * piece : 2 * (a + 1) * piece])
-        out = jnp.where(side == 0, both[:, :piece], both[:, piece:])
+        out = jnp.where(side_of(a, mine) == 0, both[:, :piece], both[:, piece:])
         out_ref[a] = out.astype(out_ref.dtype)
 
 
@@ -101,9 +106,8 @@
         )
         for i in range(blocks)
     ]
-    side = lax.axis_index("side")
-    weight_loads = load_columns(w_hbm, weight, weight_sem, 1 - side)
-    mine_loads = load_columns(w_hbm, mine_weight, mine_sem, side)
+    weight_loads = load_columns(w_hbm, weight, weight_sem, False)
+    mine_loads = load_columns(w_hbm, mine_weight, mine_sem, True)
     for copy in small + loads + weight_loads + mine_loads:
         copy.start()
     for copy in small:
@@ -140,7 +144,7 @@
         normed.append(jnp.concatenate(parts, 1) if heads > 1 else parts[0])
     normed = jnp.concatenate(normed, 0) if blocks > 1 else normed[0]
     normed_ref[...] = normed
-    project_columns(weight_loads, weight, normed, 1 - side, other_ref)
+    project_columns(weight_loads, weight, normed, False, other_ref)
     for copy in mine_loads:
         copy.wait()
 
@@ -176,7 +180,7 @@
 
 
 def project_kernel(normed_ref, weight, mine_ref):
-    project_columns([], weight, normed_ref[...], lax.axis_index("side"), mine_ref)
+    project_columns([], weight, normed_ref[...], True, mine_ref)
 
 
 def project(normed, weight, shape):
@@ -270,20 +274,22 @@
 
 def residual_kernel(residual_ref, after_ref, own_ref, *refs):
     del after_ref
-    recv_refs, flat_ref = refs[:-1], refs[-1]
+    count = (len(refs) - 1) // 2
+    recv_refs, flat_refs = refs[:count], refs[count:]
     total = own_ref[...]
     for recv_ref in recv_refs:
         total = total + recv_ref[...].astype(F32)
     total = residual_ref[...].astype(F32).reshape(total.shape) + total
-    flat_ref[...] = total.astype(BF)
+    for flat_ref in flat_refs:
+        flat_ref[...] = total.astype(BF)
 
 
 def add_residual(residual, after, own, recvs):
     return pl.pallas_call(
         residual_kernel,
         in_specs=[whole_vmem(1)[0], pl.BlockSpec(memory_space=pl.ANY)] + whole_vmem(1 + len(recvs)),
-        out_specs=pl.BlockSpec(memory_space=pltpu.VMEM),
-        out_shape=struct(own.shape, BF),
+        out_specs=whole_vmem(1 + len(recvs)),
+        out_shape=[in_vmem(own.shape, BF)] * (1 + len(recvs)),
         compiler_params=params(),
         name="add_residual",
     )(residual, after, own, *recvs)
@@ -396,7 +402,7 @@
     squares = jnp.zeros((total, 1), F32)
     xs = [x_ref[...].astype(F32) for x_ref in (x_refs[0], *x_refs[:0:-1])]
     for k in range(groups):
-        at = me ^ k
+        at = me ^ ((groups - k) % groups)
         x = jnp.concatenate([x[k * capacity : (k + 1) * capacity] for x in xs], 0)
         squares = squares + jnp.sum(x * x, -1, keepdims=True)
         placed[at] = x.astype(BF)
@@ -553,7 +559,7 @@
     me = lax.axis_index("heads")
     groups = total.shape[0]
     capacity = y_refs[0].shape[0] // groups
-    ys = [y_ref[...].astype(F32) for y_ref in y_refs]
+    ys = [y_ref[...].astype(F32) for y_ref in (y_refs[0], *y_refs[:0:-1])]
     for a in range(groups):
         y = jnp.concatenate([y[a * capacity : (a + 1) * capacity] for y in ys], 0).astype(BF)
         total[a] = dot(high_ref[...], y) + dot(low_ref[...], y)
@@ -600,6 +606,16 @@
 
 def swaps(sends, axis):
     return [swap(x, axis, k) for k, x in zip(range(len(sends), 0, -1), sends)]
+
+
+def cross_swaps(sends):
+    size = lax.axis_size("heads")
+    return [
+        lax.ppermute(
+            x, ("heads", "side"), [(2 * i + s, 2 * (i ^ k) + 1 - s) for i in range(size) for s in (0, 1)]
+        )
+        for k, x in zip(range(len(sends), 0, -1), sends)
+    ]
 
 
 def local(
@@ -615,18 +631,18 @@
     mine = project(normed, weight, other.shape)
     own, *sends = split(mine, swap(other, "side", 1))
     weights = regroup(w_down, own)
-    flat = add_residual(residual, weights, own, swaps(sends, "heads"))
+    flat, *sends = add_residual(residual, weights, own, cross_swaps(sends))
     resid_out = by_request(flat, residual.shape)
     capacity = max(2, 3 * expert_ids.shape[2] * flat.shape[0] // (2 * count))
     pick, high, low = route(
         jnp.transpose(expert_ids, (1, 2, 0)), jnp.transpose(expert_gates, (1, 2, 0)), flat,
         capacity, count,
     )
-    gathered = [flat] + swaps([flat] * (groups - 1), "heads")[::-1]
+    gathered = [flat] + swaps(sends, "heads")
     own, *sends = dispatch(pick, gathered, count)
     xs = [own] + swaps(sends, "dp")
     hidden = w_gate.shape[3]
-    split_at = hidden // 256 * 128
+    split_at = max(128, hidden // 384 * 256)
     part, lhs = first_units(split_at, norm_gain.reshape(1, -1), w_gate, w_up, xs)
     other_part = other_units(split_at, lhs, w_gate, w_up)
     sums, scale = down_first(width, split_at, part, swap(part, "side", 1), weights)
@@ -634,7 +650,7 @@
         split_at, other_part, swap(other_part, "side", 1), weights, sums, scale, count
     )
     state_out, done = new_state(slopes, new_keys, new_values, states, own)
-    ys = [own] + swaps(sends, "dp")[::-1]
+    ys = [own] + swaps(sends, "dp")
     own, *sends = combine(high, low, done, ys, groups)
     return state_out, resid_out, finish(own, swaps(sends, "heads"), residual.shape)
 

time: 53.1 us -> 52.6 us (level)
    ppermute x18 -> x15, starting transfers between devices: 22.8 us -> 17.2 us  [swap(): return lax.ppermute(x, axis, [(i, i ^ k) for i in range(size)])]
    ppermute x0 -> x3, starting transfers between devices: none -> 5.39 us  [cross_swaps(): lax.ppermute(x, ('heads', 'side'), [(2 * i + s, 2 * (i ^ k) + 1 - s) for...]
    ppermute x18 -> x15, waiting for transfers between devices: 14.2 us -> 12.7 us  [swap(): return lax.ppermute(x, axis, [(i, i ^ k) for i in range(size)])]
    ppermute x0 -> x3, waiting for transfers between devices: none -> 1.27 us  [cross_swaps(): lax.ppermute(x, ('heads', 'side'), [(2 * i + s, 2 * (i ^ k) + 1 - s) for...]
  transfers between devices with their start and end apart: 18 -> 18, of which waited for: 13 -> 12; matrix products, arithmetic and copies ran while one was open for 0% -> 0% of each run, Pallas kernels for 15% -> 15%
where the time goes in v5:
time: 52.6 us; the launch traced here: 52.4 us
  starting transfers between devices  22.6 us (43%)
  Pallas kernels  15 us (29%)
  waiting for transfers between devices  14 us (27%)
  between operations  0.81 us (2%)
    ppermute x15, starting transfers between devices, swap(): return lax.ppermute(x, axis, [(i, i ^ k) for i in range(size)])  17.2 us
    ppermute x15, waiting for transfers between devices, swap(): return lax.ppermute(x, axis, [(i, i ^ k) for i in range(size)])  12.7 us
    ppermute x3, starting transfers between devices, cross_swaps(): lax.ppermute(x, ('heads', 'side'), [(2 * i + s, 2 * (i ^ k) + 1 - s) for...  5.39 us
    pallas_call x1, Pallas kernels, attention(): pl.pallas_call(attention_kernel, in_specs=hbm_specs(7), out_specs=whole_v...  4.16 us
    pallas_call x1, Pallas kernels, new_state(): pl.pallas_call(state_kernel, in_specs=[pl.BlockSpec(memory_space=pltpu.SM...  2.88 us
    pallas_call x1, Pallas kernels, regroup(): pl.pallas_call(regroup_kernel, in_specs=[*hbm_specs(1), pl.BlockSpec(memo...  2.37 us
    ppermute x3, waiting for transfers between devices, cross_swaps(): lax.ppermute(x, ('heads', 'side'), [(2 * i + s, 2 * (i ^ k) + 1 - s) for...  1.27 us
  transfers between devices with their start and end apart: 18, of which 12 were waited for; matrix products, arithmetic and copies ran while one was open for 0% of the time, Pallas kernels for 15%

profile of v5, /device:TPU:0, one launch (start us, length us, event | category | flops | bytes accessed | tf_op | source)
XLA Modules:
  0.0 52.4 jit_solution(2365563176551510223)
XLA Ops:
  0.6 4.2 %attention.1 = (bf16[4,48,384]{2,1,0:T(8,128)(2,1)S(1)}, bf16[48,512]{1,0:T(8,128)(2,1)S(1)}, bf16[24,4,128,128]{3,2,1,0:T(8,128)(2,1)S(1)}, bf16[4,512,384]{2,1,0:T(8,128)(2,1)S(1)}) custom-call(f32[4]{0:T(128)} %slope_ref.1, bf16[24,2,512]{2,1,0:T(2,128)(2,1)} %q_hbm.1, bf16[24,2,512]{2,1,0:T(2,128)(2,1)} %k_ref.1, bf16[24,2,512]{2,1,0:T(2,128)(2,1)} %v_ref.1, ...), custom_call_target="tpu_custom_call" | custom-call | tf_op jit(solution)/shard_map/attention/pallas_call | solution.py:158
  4.8 0.5 collective-permute-start
  5.7 0.7 %collective-permute-done.recv_ref = bf16[4,48,384]{2,1,0:T(8,128)(2,1)S(1)} collective-permute-done((bf16[4,48,384]{2,1,0:T(8,128)(2,1)S(1)}, bf16[4,48,384]{2,1,0:T(8,128)(2,1)S(1)}, u32[]{:S(2)}, u32[]{:S(2)}) %collective-permute-start) | collective-permute-done | bytes 147488 | tf_op jit(solution)/shard_map/ppermute | solution.py:604
  6.4 4.8 %collective-permute-start.1 = (bf16[48,384]{1,0:T(8,128)(2,1)S(1)}, bf16[48,384]{1,0:T(8,128)(2,1)S(1)}, u32[]{:S(2)}, u32[]{:S(2)}) collective-permute-start(bf16[48,384]{1,0:T(8,128)(2,1)S(1)} %get-tuple-element.41), channel_id=1, source_target_pairs={{0,7},{1,6},{2,5},{3,4},{4,3},{5,2},{6,1},{7,0},{8,15},{9,14},{10,... | collective-permute-start | bytes 110600 | tf_op jit(solution)/shard_map/ppermute | solution.py:614
  11.1 0.6 %collective-permute-start.3 = (bf16[48,384]{1,0:T(8,128)(2,1)S(1)}, bf16[48,384]{1,0:T(8,128)(2,1)S(1)}, u32[]{:S(2)}, u32[]{:S(2)}) collective-permute-start(bf16[48,384]{1,0:T(8,128)(2,1)S(1)} %get-tuple-element.43), channel_id=1, source_target_pairs={{0,3},{1,2},{2,1},{3,0},{4,7},{5,6},{6,5},{7,4},{8,11},{9,10},{10,... | collective-permute-start | bytes 110600 | tf_op jit(solution)/shard_map/ppermute | solution.py:614
  11.8 2.4 %regroup_down.1.after_ref.w_ref = bf16[4,1152,384]{2,1,0:T(8,128)(2,1)S(1)} custom-call(bf16[1,1152,4,384]{3,2,1,0:T(4,128)(2,1)} %w_hbm.3, f32[48,384]{1,0:T(8,128)S(1)} %get-tuple-element.40.after_ref.own_ref), custom_call_target="tpu_custom_call" | custom-call | flops 100000000 | bytes 7000000 | tf_op jit(solution)/shard_map/regroup_down/pallas_call | solution.py:486
  14.2 1.3 %collective-permute-done.2.refs_1_ = bf16[48,384]{1,0:T(8,128)(2,1)S(1)} collective-permute-done((bf16[48,384]{1,0:T(8,128)(2,1)S(1)}, bf16[48,384]{1,0:T(8,128)(2,1)S(1)}, u32[]{:S(2)}, u32[]{:S(2)}) %collective-permute-start.2) | collective-permute-done | bytes 36896 | tf_op jit(solution)/shard_map/ppermute | solution.py:614
  15.5 2.3 %collective-permute-start.4 = (bf16[48,384]{1,0:T(8,128)(2,1)S(1)}, bf16[48,384]{1,0:T(8,128)(2,1)S(1)}, u32[]{:S(2)}, u32[]{:S(2)}) collective-permute-start(bf16[48,384]{1,0:T(8,128)(2,1)S(1)} %get-tuple-element.46), channel_id=1, source_target_pairs={{0,6},{2,4},{4,2},{6,0},{1,7},{3,5},{5,3},{7,1},{8,14},{10,12},{12... | collective-permute-start | bytes 110600 | tf_op jit(solution)/shard_map/ppermute | solution.py:604
  18.0 2.0 %collective-permute-start.6 = (bf16[48,384]{1,0:T(8,128)(2,1)S(1)}, bf16[48,384]{1,0:T(8,128)(2,1)S(1)}, u32[]{:S(2)}, u32[]{:S(2)}) collective-permute-start(bf16[48,384]{1,0:T(8,128)(2,1)S(1)} %get-tuple-element.48), channel_id=1, source_target_pairs={{0,2},{2,0},{4,6},{6,4},{1,3},{3,1},{5,7},{7,5},{8,10},{10,8},{12,... | collective-permute-start | bytes 110600 | tf_op jit(solution)/shard_map/ppermute | solution.py:604
  20.2 1.5 %collective-permute-done.4.refs_1_ = bf16[48,384]{1,0:T(8,128)(2,1)S(1)} collective-permute-done((bf16[48,384]{1,0:T(8,128)(2,1)S(1)}, bf16[48,384]{1,0:T(8,128)(2,1)S(1)}, u32[]{:S(2)}, u32[]{:S(2)}) %collective-permute-start.4) | collective-permute-done | bytes 36896 | tf_op jit(solution)/shard_map/ppermute | solution.py:604
  21.8 1.2 %collective-permute-done.5.refs_2_ = bf16[48,384]{1,0:T(8,128)(2,1)S(1)} collective-permute-done((bf16[48,384]{1,0:T(8,128)(2,1)S(1)}, bf16[48,384]{1,0:T(8,128)(2,1)S(1)}, u32[]{:S(2)}, u32[]{:S(2)}) %collective-permute-start.5) | collective-permute-done | bytes 36896 | tf_op jit(solution)/shard_map/ppermute | solution.py:604
  23.3 2.5 %collective-permute-start.7 = (bf16[144,384]{1,0:T(8,128)(2,1)S(1)}, bf16[144,384]{1,0:T(8,128)(2,1)S(1)}, u32[]{:S(2)}, u32[]{:S(2)}) collective-permute-start(bf16[144,384]{1,0:T(8,128)(2,1)S(1)} %get-tuple-element.50), channel_id=1, source_target_pairs={{0,24},{8,16},{16,8},{24,0},{1,25},{9,17},{17,9},{25,1},{2,26},{10... | collective-permute-start | bytes 331784 | tf_op jit(solution)/shard_map/ppermute | solution.py:604
  25.8 0.5 collective-permute-start.8
  26.3 0.5 %collective-permute-start.9 = (bf16[144,384]{1,0:T(8,128)(2,1)S(1)}, bf16[144,384]{1,0:T(8,128)(2,1)S(1)}, u32[]{:S(2)}, u32[]{:S(2)}) collective-permute-start(bf16[144,384]{1,0:T(8,128)(2,1)S(1)} %get-tuple-element.52), channel_id=1, source_target_pairs={{0,8},{8,0},{16,24},{24,16},{1,9},{9,1},{17,25},{25,17},{2,10},{10... | collective-permute-start | bytes 331784 | tf_op jit(solution)/shard_map/ppermute | solution.py:604
  26.8 2.4 %collective-permute-done.7.refs_1_ = bf16[144,384]{1,0:T(8,128)(2,1)S(1)} collective-permute-done((bf16[144,384]{1,0:T(8,128)(2,1)S(1)}, bf16[144,384]{1,0:T(8,128)(2,1)S(1)}, u32[]{:S(2)}, u32[]{:S(2)}) %collective-permute-start.7) | collective-permute-done | bytes 110624 | tf_op jit(solution)/shard_map/ppermute | solution.py:604
  29.3 2.1 %collective-permute-done.8.refs_2_ = bf16[144,384]{1,0:T(8,128)(2,1)S(1)} collective-permute-done((bf16[144,384]{1,0:T(8,128)(2,1)S(1)}, bf16[144,384]{1,0:T(8,128)(2,1)S(1)}, u32[]{:S(2)}, u32[]{:S(2)}) %collective-permute-start.8) | collective-permute-done | bytes 110624 | tf_op jit(solution)/shard_map/ppermute | solution.py:604
  31.4 1.0 %first_units.1 = (bf16[144,1664]{1,0:T(8,128)(2,1)S(1)}, bf16[144,1536]{1,0:T(8,128)(2,1)S(1)}) custom-call(f32[1,3072]{1,0:T(1,128)S(1)} %bitcast.4, bf16[1,4,384,1152]{3,2,1,0:T(8,128)(2,1)S(1)} %copy-done, bf16[1,4,384,1152]{3,2,1,0:T(8,128)(2,1)S(1)} %copy-done.1, bf16[144,384]{1,0:T(8,128)(2,1)S(1)} %get-tuple-element.49.refs_0_, ...), custom_call_target="tpu_custom_call" | custom-call | tf_op jit(solution)/shard_map/first_units/pallas_call | solution.py:428
  32.5 0.6 %other_units.1.part_ref = bf16[144,768]{1,0:T(8,128)(2,1)S(1)} custom-call(bf16[144,1536]{1,0:T(8,128)(2,1)S(1)} %get-tuple-element.53.lhs_ref, bf16[1,4,384,1152]{3,2,1,0:T(8,128)(2,1)S(1)} %copy-done, bf16[1,4,384,1152]{3,2,1,0:T(8,128)(2,1)S(1)} %copy-done.1), custom_call_target="tpu_custom_call" | custom-call | flops 1000000000 | bytes 4000000 | tf_op jit(solution)/shard_map/other_units/pallas_call | solution.py:447
  33.1 0.6 %collective-permute-start.10 = (bf16[144,768]{1,0:T(8,128)(2,1)S(1)}, bf16[144,768]{1,0:T(8,128)(2,1)S(1)}, u32[]{:S(2)}, u32[]{:S(2)}) collective-permute-start(bf16[144,768]{1,0:T(8,128)(2,1)S(1)} %other_units.1.part_ref), channel_id=1, source_target_pairs={{0,1},{1,0},{2,3},{3,2},{4,5},{5,4},{6,7},{7,6},{8,9},{9,8},{10,11... | collective-permute-start | bytes 663560 | tf_op jit(solution)/shard_map/ppermute | solution.py:604
  33.7 0.6 %collective-permute-done.11.recv_ref = bf16[144,1664]{1,0:T(8,128)(2,1)S(1)} collective-permute-done((bf16[144,1664]{1,0:T(8,128)(2,1)S(1)}, bf16[144,1664]{1,0:T(8,128)(2,1)S(1)}, u32[]{:S(2)}, u32[]{:S(2)}) %collective-permute-start.11) | collective-permute-done | bytes 479264 | tf_op jit(solution)/shard_map/ppermute | solution.py:604
  34.3 0.9 %down_first.1 = (f32[4,144,384]{2,1,0:T(8,128)S(1)}, f32[144,128]{1,0:T(8,128)S(1)}) custom-call(bf16[144,1664]{1,0:T(8,128)(2,1)S(1)} %get-tuple-element.54.part_ref, bf16[144,1664]{1,0:T(8,128)(2,1)S(1)} %collective-permute-done.11.recv_ref, bf16[4,1152,384]{2,1,0:T(8,128)(2,1)S(1)} %regroup_down.1.after_ref.w_ref), custom_call_target="tpu_custom_call" | custom-call | flops 1000000000 | bytes 4000000 | tf_op jit(solution)/shard_map/down_first/pallas_call | solution.py:522
  35.2 0.6 %down.1 = (bf16[144,384]{1,0:T(8,128)(2,1)S(1)}, bf16[144,384]{1,0:T(8,128)(2,1)S(1)}, bf16[144,384]{1,0:T(8,128)(2,1)S(1)}, bf16[144,384]{1,0:T(8,128)(2,1)S(1)}) custom-call(bf16[144,768]{1,0:T(8,128)(2,1)S(1)} %other_units.1.part_ref, bf16[144,768]{1,0:T(8,128)(2,1)S(1)} %collective-permute-done.10.recv_ref, ...), custom_call_target="tpu_custom_call" | custom-call | tf_op jit(solution)/shard_map/down/pallas_call | solution.py:546
  35.8 1.8 %collective-permute-start.12 = (bf16[144,384]{1,0:T(8,128)(2,1)S(1)}, bf16[144,384]{1,0:T(8,128)(2,1)S(1)}, u32[]{:S(2)}, u32[]{:S(2)}) collective-permute-start(bf16[144,384]{1,0:T(8,128)(2,1)S(1)} %get-tuple-element.62), channel_id=1, source_target_pairs={{0,24},{8,16},{16,8},{24,0},{1,25},{9,17},{17,9},{25,1},{2,26},{10... | collective-permute-start | bytes 331784 | tf_op jit(solution)/shard_map/ppermute | solution.py:604
  37.6 1.3 %collective-permute-start.13 = (bf16[144,384]{1,0:T(8,128)(2,1)S(1)}, bf16[144,384]{1,0:T(8,128)(2,1)S(1)}, u32[]{:S(2)}, u32[]{:S(2)}) collective-permute-start(bf16[144,384]{1,0:T(8,128)(2,1)S(1)} %get-tuple-element.63), channel_id=1, source_target_pairs={{0,16},{8,24},{16,0},{24,8},{1,17},{9,25},{17,1},{25,9},{2,18},{10... | collective-permute-start | bytes 331784 | tf_op jit(solution)/shard_map/ppermute | solution.py:604
  39.4 2.9 %new_state.1 = (bf16[24,4,128,128]{3,2,1,0:T(8,128)(2,1)}, f32[8,128]{1,0:T(8,128)S(1)}) custom-call(f32[4]{0:T(128)S(1)} %copy-done.8, bf16[24,2,512]{2,1,0:T(2,128)(2,1)S(1)} %copy-done.2, bf16[24,2,512]{2,1,0:T(2,128)(2,1)S(1)} %copy-done.3, bf16[24,4,128,128]{3,2,1,0:T(8,128)(2,1)S(1)} %get-tuple-element.36.s_ref, ...), custom_call_target="tpu_custom_call" | custom-call | flops 100000000 | bytes 8000000 | tf_op jit(solution)/shard_map/new_state/pallas_call | solution.py:237
  42.6 1.7 %collective-permute-done.13.refs_2_ = bf16[144,384]{1,0:T(8,128)(2,1)S(1)} collective-permute-done((bf16[144,384]{1,0:T(8,128)(2,1)S(1)}, bf16[144,384]{1,0:T(8,128)(2,1)S(1)}, u32[]{:S(2)}, u32[]{:S(2)}) %collective-permute-start.13) | collective-permute-done | bytes 110624 | tf_op jit(solution)/shard_map/ppermute | solution.py:604
  44.6 2.3 %collective-permute-start.15 = (bf16[48,384]{1,0:T(8,128)(2,1)S(1)}, bf16[48,384]{1,0:T(8,128)(2,1)S(1)}, u32[]{:S(2)}, u32[]{:S(2)}) collective-permute-start(bf16[48,384]{1,0:T(8,128)(2,1)S(1)} %get-tuple-element.66), channel_id=1, source_target_pairs={{0,6},{2,4},{4,2},{6,0},{1,7},{3,5},{5,3},{7,1},{8,14},{10,12},{12... | collective-permute-start | bytes 110600 | tf_op jit(solution)/shard_map/ppermute | solution.py:604
  46.9 2.1 %collective-permute-start.17 = (bf16[48,384]{1,0:T(8,128)(2,1)S(1)}, bf16[48,384]{1,0:T(8,128)(2,1)S(1)}, u32[]{:S(2)}, u32[]{:S(2)}) collective-permute-start(bf16[48,384]{1,0:T(8,128)(2,1)S(1)} %get-tuple-element.68), channel_id=1, source_target_pairs={{0,2},{2,0},{4,6},{6,4},{1,3},{3,1},{5,7},{7,5},{8,10},{10,8},{12,... | collective-permute-start | bytes 110600 | tf_op jit(solution)/shard_map/ppermute | solution.py:604
  49.1 0.6 %by_request.1 = bf16[24,2,384]{2,1,0:T(2,128)(2,1)} custom-call(bf16[48,384]{1,0:T(8,128)(2,1)S(1)} %get-tuple-element.44.after_ref.refs_0_.flat_ref), custom_call_target="tpu_custom_call" | custom-call | flops 100000 | bytes 1000000 | tf_op jit(solution)/shard_map/by_request/pallas_call | solution.py:303
  49.7 0.8 %collective-permute-done.15.refs_0_ = bf16[48,384]{1,0:T(8,128)(2,1)S(1)} collective-permute-done((bf16[48,384]{1,0:T(8,128)(2,1)S(1)}, bf16[48,384]{1,0:T(8,128)(2,1)S(1)}, u32[]{:S(2)}, u32[]{:S(2)}) %collective-permute-start.15) | collective-permute-done | bytes 36896 | tf_op jit(solution)/shard_map/ppermute | solution.py:604
  50.4 1.4 %collective-permute-done.16.refs_1_ = bf16[48,384]{1,0:T(8,128)(2,1)S(1)} collective-permute-done((bf16[48,384]{1,0:T(8,128)(2,1)S(1)}, bf16[48,384]{1,0:T(8,128)(2,1)S(1)}, u32[]{:S(2)}, u32[]{:S(2)}) %collective-permute-start.16) | collective-permute-done | bytes 36896 | tf_op jit(solution)/shard_map/ppermute | solution.py:604
  51.8 0.7 %finish.1 = bf16[24,2,384]{2,1,0:T(2,128)(2,1)} custom-call(f32[48,384]{1,0:T(8,128)S(1)} %get-tuple-element.65.own_ref, bf16[48,384]{1,0:T(8,128)(2,1)S(1)} %collective-permute-done.15.refs_0_, bf16[48,384]{1,0:T(8,128)(2,1)S(1)} %collective-permute-done.16.refs_1_, bf16[48,384]{1,0:T(8,128)(2,1)S(1)} %collective-permute-done.17.refs_2_), custom_call_target="tpu_custom_call" | custom-call | tf_op jit(solution)/shard_map/finish/pallas_call | solution.py:592
  (37 shorter events, 2.5 us)
Async XLA Ops:
  4.8 1.5 %collective-permute-start = (bf16[4,48,384]{2,1,0:T(8,128)(2,1)S(1)}, bf16[4,48,384]{2,1,0:T(8,128)(2,1)S(1)}, u32[]{:S(2)}, u32[]{:S(2)}) collective-permute-start(bf16[4,48,384]{2,1,0:T(8,128)(2,1)S(1)} %get-tuple-element.39), channel_id=1, source_target_pairs={{0,1},{1,0},{2,3},{3,2},{4,5},{5,4},{6,7},{7,6},{8,9},{9,8},{10,11... | collective-permute-start | bytes 442376 | tf_op jit(solution)/shard_map/ppermute | solution.py:604
  6.4 7.8 %collective-permute-start.1 = (bf16[48,384]{1,0:T(8,128)(2,1)S(1)}, bf16[48,384]{1,0:T(8,128)(2,1)S(1)}, u32[]{:S(2)}, u32[]{:S(2)}) collective-permute-start(bf16[48,384]{1,0:T(8,128)(2,1)S(1)} %get-tuple-element.41), channel_id=1, source_target_pairs={{0,7},{1,6},{2,5},{3,4},{4,3},{5,2},{6,1},{7,0},{8,15},{9,14},{10,... | collective-permute-start | bytes 110600 | tf_op jit(solution)/shard_map/ppermute | solution.py:614
  11.1 4.3 %collective-permute-start.2 = (bf16[48,384]{1,0:T(8,128)(2,1)S(1)}, bf16[48,384]{1,0:T(8,128)(2,1)S(1)}, u32[]{:S(2)}, u32[]{:S(2)}) collective-permute-start(bf16[48,384]{1,0:T(8,128)(2,1)S(1)} %get-tuple-element.42), channel_id=1, source_target_pairs={{0,5},{1,4},{2,7},{3,6},{4,1},{5,0},{6,3},{7,2},{8,13},{9,12},{10,... | collective-permute-start | bytes 110600 | tf_op jit(solution)/shard_map/ppermute | solution.py:614
  11.1 4.3 %collective-permute-start.3 = (bf16[48,384]{1,0:T(8,128)(2,1)S(1)}, bf16[48,384]{1,0:T(8,128)(2,1)S(1)}, u32[]{:S(2)}, u32[]{:S(2)}) collective-permute-start(bf16[48,384]{1,0:T(8,128)(2,1)S(1)} %get-tuple-element.43), channel_id=1, source_target_pairs={{0,3},{1,2},{2,1},{3,0},{4,7},{5,6},{6,5},{7,4},{8,11},{9,10},{10,... | collective-permute-start | bytes 110600 | tf_op jit(solution)/shard_map/ppermute | solution.py:614
  11.8 3.7 %copy-start.4 = (bf16[24,2,384]{2,1,0:T(2,128)(2,1)S(1)}, bf16[24,2,384]{2,1,0:T(2,128)(2,1)}, u32[]{:S(2)}) copy-start(bf16[24,2,384]{2,1,0:T(2,128)(2,1)} %residual_ref.1) | copy-start | bytes 110596
  11.8 19.7 %copy-start.1 = (bf16[1,4,384,1152]{3,2,1,0:T(8,128)(2,1)S(1)}, bf16[1,4,384,1152]{3,2,1,0:T(8,128)(2,1)}, u32[]{:S(2)}) copy-start(bf16[1,4,384,1152]{3,2,1,0:T(8,128)(2,1)} %wu_ref.3) | copy-start | bytes 10616836
  14.1 5.8 %copy-start.6 = (s32[24,2,2]{0,2,1:T(2,128)S(1)}, s32[24,2,2]{0,2,1:T(2,128)}, u32[]{:S(2)}) copy-start(s32[24,2,2]{0,2,1:T(2,128)} %param.23) | copy-start | bytes 1156
  14.1 5.8 %copy-start.7 = (f32[24,2,2]{0,2,1:T(2,128)S(1)}, f32[24,2,2]{0,2,1:T(2,128)}, u32[]{:S(2)}) copy-start(f32[24,2,2]{0,2,1:T(2,128)} %param.24) | copy-start | bytes 1156
  14.2 17.3 %copy-start = (bf16[1,4,384,1152]{3,2,1,0:T(8,128)(2,1)S(1)}, bf16[1,4,384,1152]{3,2,1,0:T(8,128)(2,1)}, u32[]{:S(2)}) copy-start(bf16[1,4,384,1152]{3,2,1,0:T(8,128)(2,1)} %wg_ref.3) | copy-start | bytes 10616836
  14.2 17.3 %copy-start.5 = (f32[3072]{0:T(1024)S(1)}, f32[3072]{0:T(1024)}, u32[]{:S(2)}) copy-start(f32[3072]{0:T(1024)} %param.22) | copy-start | bytes 36868
  15.5 6.2 %collective-permute-start.4 = (bf16[48,384]{1,0:T(8,128)(2,1)S(1)}, bf16[48,384]{1,0:T(8,128)(2,1)S(1)}, u32[]{:S(2)}, u32[]{:S(2)}) collective-permute-start(bf16[48,384]{1,0:T(8,128)(2,1)S(1)} %get-tuple-element.46), channel_id=1, source_target_pairs={{0,6},{2,4},{4,2},{6,0},{1,7},{3,5},{5,3},{7,1},{8,14},{10,12},{12... | collective-permute-start | bytes 110600 | tf_op jit(solution)/shard_map/ppermute | solution.py:604
  17.9 5.1 %collective-permute-start.5 = (bf16[48,384]{1,0:T(8,128)(2,1)S(1)}, bf16[48,384]{1,0:T(8,128)(2,1)S(1)}, u32[]{:S(2)}, u32[]{:S(2)}) collective-permute-start(bf16[48,384]{1,0:T(8,128)(2,1)S(1)} %get-tuple-element.47), channel_id=1, source_target_pairs={{0,4},{2,6},{4,0},{6,2},{1,5},{3,7},{5,1},{7,3},{8,12},{10,14},{12... | collective-permute-start | bytes 110600 | tf_op jit(solution)/shard_map/ppermute | solution.py:604
  18.0 4.9 %collective-permute-start.6 = (bf16[48,384]{1,0:T(8,128)(2,1)S(1)}, bf16[48,384]{1,0:T(8,128)(2,1)S(1)}, u32[]{:S(2)}, u32[]{:S(2)}) collective-permute-start(bf16[48,384]{1,0:T(8,128)(2,1)S(1)} %get-tuple-element.48), channel_id=1, source_target_pairs={{0,2},{2,0},{4,6},{6,4},{1,3},{3,1},{5,7},{7,5},{8,10},{10,8},{12,... | collective-permute-start | bytes 110600 | tf_op jit(solution)/shard_map/ppermute | solution.py:604
  23.3 6.0 %collective-permute-start.7 = (bf16[144,384]{1,0:T(8,128)(2,1)S(1)}, bf16[144,384]{1,0:T(8,128)(2,1)S(1)}, u32[]{:S(2)}, u32[]{:S(2)}) collective-permute-start(bf16[144,384]{1,0:T(8,128)(2,1)S(1)} %get-tuple-element.50), channel_id=1, source_target_pairs={{0,24},{8,16},{16,8},{24,0},{1,25},{9,17},{17,9},{25,1},{2,26},{10... | collective-permute-start | bytes 331784 | tf_op jit(solution)/shard_map/ppermute | solution.py:604
  25.8 5.6 %collective-permute-start.8 = (bf16[144,384]{1,0:T(8,128)(2,1)S(1)}, bf16[144,384]{1,0:T(8,128)(2,1)S(1)}, u32[]{:S(2)}, u32[]{:S(2)}) collective-permute-start(bf16[144,384]{1,0:T(8,128)(2,1)S(1)} %get-tuple-element.51), channel_id=1, source_target_pairs={{0,16},{8,24},{16,0},{24,8},{1,17},{9,25},{17,1},{25,9},{2,18},{10... | collective-permute-start | bytes 331784 | tf_op jit(solution)/shard_map/ppermute | solution.py:604
  26.3 5.1 %collective-permute-start.9 = (bf16[144,384]{1,0:T(8,128)(2,1)S(1)}, bf16[144,384]{1,0:T(8,128)(2,1)S(1)}, u32[]{:S(2)}, u32[]{:S(2)}) collective-permute-start(bf16[144,384]{1,0:T(8,128)(2,1)S(1)} %get-tuple-element.52), channel_id=1, source_target_pairs={{0,8},{8,0},{16,24},{24,16},{1,9},{9,1},{17,25},{25,17},{2,10},{10... | collective-permute-start | bytes 331784 | tf_op jit(solution)/shard_map/ppermute | solution.py:604
  32.4 1.9 %collective-permute-start.11 = (bf16[144,1664]{1,0:T(8,128)(2,1)S(1)}, bf16[144,1664]{1,0:T(8,128)(2,1)S(1)}, u32[]{:S(2)}, u32[]{:S(2)}) collective-permute-start(bf16[144,1664]{1,0:T(8,128)(2,1)S(1)} %get-tuple-element.54.part_ref), channel_id=1, source_target_pairs={{0,1},{1,0},{2,3},{3,2},{4,5},{5,4},{6,7},{7,6},{8,9},{9,8},{10,11... | collective-permute-start | bytes 1437704 | tf_op jit(solution)/shard_map/ppermute | solution.py:604
  33.1 2.1 %collective-permute-start.10 = (bf16[144,768]{1,0:T(8,128)(2,1)S(1)}, bf16[144,768]{1,0:T(8,128)(2,1)S(1)}, u32[]{:S(2)}, u32[]{:S(2)}) collective-permute-start(bf16[144,768]{1,0:T(8,128)(2,1)S(1)} %other_units.1.part_ref), channel_id=1, source_target_pairs={{0,1},{1,0},{2,3},{3,2},{4,5},{5,4},{6,7},{7,6},{8,9},{9,8},{10,11... | collective-permute-start | bytes 663560 | tf_op jit(solution)/shard_map/ppermute | solution.py:604
  35.2 4.2 %copy-start.2 = (bf16[24,2,512]{2,1,0:T(2,128)(2,1)S(1)}, bf16[24,2,512]{2,1,0:T(2,128)(2,1)}, u32[]{:S(2)}) copy-start(bf16[24,2,512]{2,1,0:T(2,128)(2,1)} %k_ref.1) | copy-start | bytes 147460
  35.2 4.2 %copy-start.3 = (bf16[24,2,512]{2,1,0:T(2,128)(2,1)S(1)}, bf16[24,2,512]{2,1,0:T(2,128)(2,1)}, u32[]{:S(2)}) copy-start(bf16[24,2,512]{2,1,0:T(2,128)(2,1)} %v_ref.1) | copy-start | bytes 147460
  35.2 4.2 %copy-start.8 = (f32[4]{0:T(128)S(1)}, f32[4]{0:T(128)}, u32[]{:S(2)}) copy-start(f32[4]{0:T(128)} %slope_ref.1) | copy-start | bytes 52
  35.8 6.7 %collective-permute-start.12 = (bf16[144,384]{1,0:T(8,128)(2,1)S(1)}, bf16[144,384]{1,0:T(8,128)(2,1)S(1)}, u32[]{:S(2)}, u32[]{:S(2)}) collective-permute-start(bf16[144,384]{1,0:T(8,128)(2,1)S(1)} %get-tuple-element.62), channel_id=1, source_target_pairs={{0,24},{8,16},{16,8},{24,0},{1,25},{9,17},{17,9},{25,1},{2,26},{10... | collective-permute-start | bytes 331784 | tf_op jit(solution)/shard_map/ppermute | solution.py:604
  37.6 6.7 %collective-permute-start.13 = (bf16[144,384]{1,0:T(8,128)(2,1)S(1)}, bf16[144,384]{1,0:T(8,128)(2,1)S(1)}, u32[]{:S(2)}, u32[]{:S(2)}) collective-permute-start(bf16[144,384]{1,0:T(8,128)(2,1)S(1)} %get-tuple-element.63), channel_id=1, source_target_pairs={{0,16},{8,24},{16,0},{24,8},{1,17},{9,25},{17,1},{25,9},{2,18},{10... | collective-permute-start | bytes 331784 | tf_op jit(solution)/shard_map/ppermute | solution.py:604
  38.9 5.4 %collective-permute-start.14 = (bf16[144,384]{1,0:T(8,128)(2,1)S(1)}, bf16[144,384]{1,0:T(8,128)(2,1)S(1)}, u32[]{:S(2)}, u32[]{:S(2)}) collective-permute-start(bf16[144,384]{1,0:T(8,128)(2,1)S(1)} %get-tuple-element.64), channel_id=1, source_target_pairs={{0,8},{8,0},{16,24},{24,16},{1,9},{9,1},{17,25},{25,17},{2,10},{10... | collective-permute-start | bytes 331784 | tf_op jit(solution)/shard_map/ppermute | solution.py:604
  44.6 5.8 %collective-permute-start.15 = (bf16[48,384]{1,0:T(8,128)(2,1)S(1)}, bf16[48,384]{1,0:T(8,128)(2,1)S(1)}, u32[]{:S(2)}, u32[]{:S(2)}) collective-permute-start(bf16[48,384]{1,0:T(8,128)(2,1)S(1)} %get-tuple-element.66), channel_id=1, source_target_pairs={{0,6},{2,4},{4,2},{6,0},{1,7},{3,5},{5,3},{7,1},{8,14},{10,12},{12... | collective-permute-start | bytes 110600 | tf_op jit(solution)/shard_map/ppermute | solution.py:604
  46.9 4.9 %collective-permute-start.16 = (bf16[48,384]{1,0:T(8,128)(2,1)S(1)}, bf16[48,384]{1,0:T(8,128)(2,1)S(1)}, u32[]{:S(2)}, u32[]{:S(2)}) collective-permute-start(bf16[48,384]{1,0:T(8,128)(2,1)S(1)} %get-tuple-element.67), channel_id=1, source_target_pairs={{0,4},{2,6},{4,0},{6,2},{1,5},{3,7},{5,1},{7,3},{8,12},{10,14},{12... | collective-permute-start | bytes 110600 | tf_op jit(solution)/shard_map/ppermute | solution.py:604
  46.9 4.9 %collective-permute-start.17 = (bf16[48,384]{1,0:T(8,128)(2,1)S(1)}, bf16[48,384]{1,0:T(8,128)(2,1)S(1)}, u32[]{:S(2)}, u32[]{:S(2)}) collective-permute-start(bf16[48,384]{1,0:T(8,128)(2,1)S(1)} %get-tuple-element.68), channel_id=1, source_target_pairs={{0,2},{2,0},{4,6},{6,4},{1,3},{3,1},{5,7},{7,5},{8,10},{10,8},{12,... | collective-permute-start | bytes 110600 | tf_op jit(solution)/shard_map/ppermute | solution.py:604

commit v6 on v5

--- a/solution.py
+++ b/solution.py
@@ -642,7 +642,7 @@
     own, *sends = dispatch(pick, gathered, count)
     xs = [own] + swaps(sends, "dp")
     hidden = w_gate.shape[3]
-    split_at = max(128, hidden // 384 * 256)
+    split_at = (hidden + 128) // 256 * 128
     part, lhs = first_units(split_at, norm_gain.reshape(1, -1), w_gate, w_up, xs)
     other_part = other_units(split_at, lhs, w_gate, w_up)
     sums, scale = down_first(width, split_at, part, swap(part, "side", 1), weights)

time: 52.6 us -> 52.6 us (level)
  no operation moved by 1% of the time
where the time goes in v6:
time: 52.6 us; the launch traced here: 52.4 us
  starting transfers between devices  22.6 us (43%)
  Pallas kernels  15.1 us (29%)
  waiting for transfers between devices  13.9 us (26%)
  between operations  0.82 us (2%)
    ppermute x15, starting transfers between devices, swap(): return lax.ppermute(x, axis, [(i, i ^ k) for i in range(size)])  17.2 us
    ppermute x15, waiting for transfers between devices, swap(): return lax.ppermute(x, axis, [(i, i ^ k) for i in range(size)])  12.6 us
    ppermute x3, starting transfers between devices, cross_swaps(): lax.ppermute(x, ('heads', 'side'), [(2 * i + s, 2 * (i ^ k) + 1 - s) for...  5.39 us
    pallas_call x1, Pallas kernels, attention(): pl.pallas_call(attention_kernel, in_specs=hbm_specs(7), out_specs=whole_v...  4.16 us
    pallas_call x1, Pallas kernels, new_state(): pl.pallas_call(state_kernel, in_specs=[pl.BlockSpec(memory_space=pltpu.SM...  2.88 us
    pallas_call x1, Pallas kernels, regroup(): pl.pallas_call(regroup_kernel, in_specs=[*hbm_specs(1), pl.BlockSpec(memo...  2.37 us
    ppermute x3, waiting for transfers between devices, cross_swaps(): lax.ppermute(x, ('heads', 'side'), [(2 * i + s, 2 * (i ^ k) + 1 - s) for...  1.27 us
  transfers between devices with their start and end apart: 18, of which 12 were waited for; matrix products, arithmetic and copies ran while one was open for 0% of the time, Pallas kernels for 15%

profile of v6, /device:TPU:0, one launch (start us, length us, event | category | flops | bytes accessed | tf_op | source)
XLA Modules:
  0.0 52.4 jit_solution(12595799556771481455)
XLA Ops:
  0.6 4.2 %attention.1 = (bf16[4,48,384]{2,1,0:T(8,128)(2,1)S(1)}, bf16[48,512]{1,0:T(8,128)(2,1)S(1)}, bf16[24,4,128,128]{3,2,1,0:T(8,128)(2,1)S(1)}, bf16[4,512,384]{2,1,0:T(8,128)(2,1)S(1)}) custom-call(f32[4]{0:T(128)} %slope_ref.1, bf16[24,2,512]{2,1,0:T(2,128)(2,1)} %q_hbm.1, bf16[24,2,512]{2,1,0:T(2,128)(2,1)} %k_ref.1, bf16[24,2,512]{2,1,0:T(2,128)(2,1)} %v_ref.1, ...), custom_call_target="tpu_custom_call" | custom-call | tf_op jit(solution)/shard_map/attention/pallas_call | solution.py:158
  4.8 0.5 collective-permute-start
  5.7 0.7 %collective-permute-done.recv_ref = bf16[4,48,384]{2,1,0:T(8,128)(2,1)S(1)} collective-permute-done((bf16[4,48,384]{2,1,0:T(8,128)(2,1)S(1)}, bf16[4,48,384]{2,1,0:T(8,128)(2,1)S(1)}, u32[]{:S(2)}, u32[]{:S(2)}) %collective-permute-start) | collective-permute-done | bytes 147488 | tf_op jit(solution)/shard_map/ppermute | solution.py:604
  6.4 4.8 %collective-permute-start.1 = (bf16[48,384]{1,0:T(8,128)(2,1)S(1)}, bf16[48,384]{1,0:T(8,128)(2,1)S(1)}, u32[]{:S(2)}, u32[]{:S(2)}) collective-permute-start(bf16[48,384]{1,0:T(8,128)(2,1)S(1)} %get-tuple-element.41), channel_id=1, source_target_pairs={{0,7},{1,6},{2,5},{3,4},{4,3},{5,2},{6,1},{7,0},{8,15},{9,14},{10,... | collective-permute-start | bytes 110600 | tf_op jit(solution)/shard_map/ppermute | solution.py:614
  11.1 0.6 %collective-permute-start.3 = (bf16[48,384]{1,0:T(8,128)(2,1)S(1)}, bf16[48,384]{1,0:T(8,128)(2,1)S(1)}, u32[]{:S(2)}, u32[]{:S(2)}) collective-permute-start(bf16[48,384]{1,0:T(8,128)(2,1)S(1)} %get-tuple-element.43), channel_id=1, source_target_pairs={{0,3},{1,2},{2,1},{3,0},{4,7},{5,6},{6,5},{7,4},{8,11},{9,10},{10,... | collective-permute-start | bytes 110600 | tf_op jit(solution)/shard_map/ppermute | solution.py:614
  11.8 2.4 %regroup_down.1.after_ref.w_ref = bf16[4,1152,384]{2,1,0:T(8,128)(2,1)S(1)} custom-call(bf16[1,1152,4,384]{3,2,1,0:T(4,128)(2,1)} %w_hbm.3, f32[48,384]{1,0:T(8,128)S(1)} %get-tuple-element.40.after_ref.own_ref), custom_call_target="tpu_custom_call" | custom-call | flops 100000000 | bytes 7000000 | tf_op jit(solution)/shard_map/regroup_down/pallas_call | solution.py:486
  14.2 1.3 %collective-permute-done.2.refs_1_ = bf16[48,384]{1,0:T(8,128)(2,1)S(1)} collective-permute-done((bf16[48,384]{1,0:T(8,128)(2,1)S(1)}, bf16[48,384]{1,0:T(8,128)(2,1)S(1)}, u32[]{:S(2)}, u32[]{:S(2)}) %collective-permute-start.2) | collective-permute-done | bytes 36896 | tf_op jit(solution)/shard_map/ppermute | solution.py:614
  15.5 2.3 %collective-permute-start.4 = (bf16[48,384]{1,0:T(8,128)(2,1)S(1)}, bf16[48,384]{1,0:T(8,128)(2,1)S(1)}, u32[]{:S(2)}, u32[]{:S(2)}) collective-permute-start(bf16[48,384]{1,0:T(8,128)(2,1)S(1)} %get-tuple-element.46), channel_id=1, source_target_pairs={{0,6},{2,4},{4,2},{6,0},{1,7},{3,5},{5,3},{7,1},{8,14},{10,12},{12... | collective-permute-start | bytes 110600 | tf_op jit(solution)/shard_map/ppermute | solution.py:604
  18.0 2.0 %collective-permute-start.6 = (bf16[48,384]{1,0:T(8,128)(2,1)S(1)}, bf16[48,384]{1,0:T(8,128)(2,1)S(1)}, u32[]{:S(2)}, u32[]{:S(2)}) collective-permute-start(bf16[48,384]{1,0:T(8,128)(2,1)S(1)} %get-tuple-element.48), channel_id=1, source_target_pairs={{0,2},{2,0},{4,6},{6,4},{1,3},{3,1},{5,7},{7,5},{8,10},{10,8},{12,... | collective-permute-start | bytes 110600 | tf_op jit(solution)/shard_map/ppermute | solution.py:604
  20.2 1.5 %collective-permute-done.4.refs_1_ = bf16[48,384]{1,0:T(8,128)(2,1)S(1)} collective-permute-done((bf16[48,384]{1,0:T(8,128)(2,1)S(1)}, bf16[48,384]{1,0:T(8,128)(2,1)S(1)}, u32[]{:S(2)}, u32[]{:S(2)}) %collective-permute-start.4) | collective-permute-done | bytes 36896 | tf_op jit(solution)/shard_map/ppermute | solution.py:604
  21.8 1.2 %collective-permute-done.5.refs_2_ = bf16[48,384]{1,0:T(8,128)(2,1)S(1)} collective-permute-done((bf16[48,384]{1,0:T(8,128)(2,1)S(1)}, bf16[48,384]{1,0:T(8,128)(2,1)S(1)}, u32[]{:S(2)}, u32[]{:S(2)}) %collective-permute-start.5) | collective-permute-done | bytes 36896 | tf_op jit(solution)/shard_map/ppermute | solution.py:604
  23.3 2.5 %collective-permute-start.7 = (bf16[144,384]{1,0:T(8,128)(2,1)S(1)}, bf16[144,384]{1,0:T(8,128)(2,1)S(1)}, u32[]{:S(2)}, u32[]{:S(2)}) collective-permute-start(bf16[144,384]{1,0:T(8,128)(2,1)S(1)} %get-tuple-element.50), channel_id=1, source_target_pairs={{0,24},{8,16},{16,8},{24,0},{1,25},{9,17},{17,9},{25,1},{2,26},{10... | collective-permute-start | bytes 331784 | tf_op jit(solution)/shard_map/ppermute | solution.py:604
  25.8 0.5 collective-permute-start.8
  26.3 0.5 %collective-permute-start.9 = (bf16[144,384]{1,0:T(8,128)(2,1)S(1)}, bf16[144,384]{1,0:T(8,128)(2,1)S(1)}, u32[]{:S(2)}, u32[]{:S(2)}) collective-permute-start(bf16[144,384]{1,0:T(8,128)(2,1)S(1)} %get-tuple-element.52), channel_id=1, source_target_pairs={{0,8},{8,0},{16,24},{24,16},{1,9},{9,1},{17,25},{25,17},{2,10},{10... | collective-permute-start | bytes 331784 | tf_op jit(solution)/shard_map/ppermute | solution.py:604
  26.8 2.4 %collective-permute-done.7.refs_1_ = bf16[144,384]{1,0:T(8,128)(2,1)S(1)} collective-permute-done((bf16[144,384]{1,0:T(8,128)(2,1)S(1)}, bf16[144,384]{1,0:T(8,128)(2,1)S(1)}, u32[]{:S(2)}, u32[]{:S(2)}) %collective-permute-start.7) | collective-permute-done | bytes 110624 | tf_op jit(solution)/shard_map/ppermute | solution.py:604
  29.3 2.1 %collective-permute-done.8.refs_2_ = bf16[144,384]{1,0:T(8,128)(2,1)S(1)} collective-permute-done((bf16[144,384]{1,0:T(8,128)(2,1)S(1)}, bf16[144,384]{1,0:T(8,128)(2,1)S(1)}, u32[]{:S(2)}, u32[]{:S(2)}) %collective-permute-start.8) | collective-permute-done | bytes 110624 | tf_op jit(solution)/shard_map/ppermute | solution.py:604
  31.4 1.0 %first_units.1 = (bf16[144,1408]{1,0:T(8,128)(2,1)S(1)}, bf16[144,1536]{1,0:T(8,128)(2,1)S(1)}) custom-call(f32[1,3072]{1,0:T(1,128)S(1)} %bitcast.4, bf16[1,4,384,1152]{3,2,1,0:T(8,128)(2,1)S(1)} %copy-done, bf16[1,4,384,1152]{3,2,1,0:T(8,128)(2,1)S(1)} %copy-done.1, bf16[144,384]{1,0:T(8,128)(2,1)S(1)} %get-tuple-element.49.refs_0_, ...), custom_call_target="tpu_custom_call" | custom-call | tf_op jit(solution)/shard_map/first_units/pallas_call | solution.py:428
  32.5 0.6 %other_units.1.part_ref = bf16[144,1024]{1,0:T(8,128)(2,1)S(1)} custom-call(bf16[144,1536]{1,0:T(8,128)(2,1)S(1)} %get-tuple-element.53.lhs_ref, bf16[1,4,384,1152]{3,2,1,0:T(8,128)(2,1)S(1)} %copy-done, bf16[1,4,384,1152]{3,2,1,0:T(8,128)(2,1)S(1)} %copy-done.1), custom_call_target="tpu_custom_call" | custom-call | flops 1000000000 | bytes 4000000 | tf_op jit(solution)/shard_map/other_units/pallas_call | solution.py:447
  33.1 0.6 %collective-permute-start.10 = (bf16[144,1024]{1,0:T(8,128)(2,1)S(1)}, bf16[144,1024]{1,0:T(8,128)(2,1)S(1)}, u32[]{:S(2)}, u32[]{:S(2)}) collective-permute-start(bf16[144,1024]{1,0:T(8,128)(2,1)S(1)} %other_units.1.part_ref), channel_id=1, source_target_pairs={{0,1},{1,0},{2,3},{3,2},{4,5},{5,4},{6,7},{7,6},{8,9},{9,8},{10,11... | collective-permute-start | bytes 884744 | tf_op jit(solution)/shard_map/ppermute | solution.py:604
  33.7 0.5 %collective-permute-done.11.recv_ref = bf16[144,1408]{1,0:T(8,128)(2,1)S(1)} collective-permute-done((bf16[144,1408]{1,0:T(8,128)(2,1)S(1)}, bf16[144,1408]{1,0:T(8,128)(2,1)S(1)}, u32[]{:S(2)}, u32[]{:S(2)}) %collective-permute-start.11) | collective-permute-done | bytes 405536 | tf_op jit(solution)/shard_map/ppermute | solution.py:604
  34.2 0.9 %down_first.1 = (f32[4,144,384]{2,1,0:T(8,128)S(1)}, f32[144,128]{1,0:T(8,128)S(1)}) custom-call(bf16[144,1408]{1,0:T(8,128)(2,1)S(1)} %get-tuple-element.54.part_ref, bf16[144,1408]{1,0:T(8,128)(2,1)S(1)} %collective-permute-done.11.recv_ref, bf16[4,1152,384]{2,1,0:T(8,128)(2,1)S(1)} %regroup_down.1.after_ref.w_ref), custom_call_target="tpu_custom_call" | custom-call | flops 1000000000 | bytes 4000000 | tf_op jit(solution)/shard_map/down_first/pallas_call | solution.py:522
  35.1 0.6 %down.1 = (bf16[144,384]{1,0:T(8,128)(2,1)S(1)}, bf16[144,384]{1,0:T(8,128)(2,1)S(1)}, bf16[144,384]{1,0:T(8,128)(2,1)S(1)}, bf16[144,384]{1,0:T(8,128)(2,1)S(1)}) custom-call(bf16[144,1024]{1,0:T(8,128)(2,1)S(1)} %other_units.1.part_ref, bf16[144,1024]{1,0:T(8,128)(2,1)S(1)} %collective-permute-done.10.recv_ref, ...), custom_call_target="tpu_custom_call" | custom-call | tf_op jit(solution)/shard_map/down/pallas_call | solution.py:546
  35.8 1.8 %collective-permute-start.12 = (bf16[144,384]{1,0:T(8,128)(2,1)S(1)}, bf16[144,384]{1,0:T(8,128)(2,1)S(1)}, u32[]{:S(2)}, u32[]{:S(2)}) collective-permute-start(bf16[144,384]{1,0:T(8,128)(2,1)S(1)} %get-tuple-element.62), channel_id=1, source_target_pairs={{0,24},{8,16},{16,8},{24,0},{1,25},{9,17},{17,9},{25,1},{2,26},{10... | collective-permute-start | bytes 331784 | tf_op jit(solution)/shard_map/ppermute | solution.py:604
  37.5 1.3 %collective-permute-start.13 = (bf16[144,384]{1,0:T(8,128)(2,1)S(1)}, bf16[144,384]{1,0:T(8,128)(2,1)S(1)}, u32[]{:S(2)}, u32[]{:S(2)}) collective-permute-start(bf16[144,384]{1,0:T(8,128)(2,1)S(1)} %get-tuple-element.63), channel_id=1, source_target_pairs={{0,16},{8,24},{16,0},{24,8},{1,17},{9,25},{17,1},{25,9},{2,18},{10... | collective-permute-start | bytes 331784 | tf_op jit(solution)/shard_map/ppermute | solution.py:604
  39.3 2.9 %new_state.1 = (bf16[24,4,128,128]{3,2,1,0:T(8,128)(2,1)}, f32[8,128]{1,0:T(8,128)S(1)}) custom-call(f32[4]{0:T(128)S(1)} %copy-done.8, bf16[24,2,512]{2,1,0:T(2,128)(2,1)S(1)} %copy-done.2, bf16[24,2,512]{2,1,0:T(2,128)(2,1)S(1)} %copy-done.3, bf16[24,4,128,128]{3,2,1,0:T(8,128)(2,1)S(1)} %get-tuple-element.36.s_ref, ...), custom_call_target="tpu_custom_call" | custom-call | flops 100000000 | bytes 8000000 | tf_op jit(solution)/shard_map/new_state/pallas_call | solution.py:237
  42.5 1.7 %collective-permute-done.13.refs_2_ = bf16[144,384]{1,0:T(8,128)(2,1)S(1)} collective-permute-done((bf16[144,384]{1,0:T(8,128)(2,1)S(1)}, bf16[144,384]{1,0:T(8,128)(2,1)S(1)}, u32[]{:S(2)}, u32[]{:S(2)}) %collective-permute-start.13) | collective-permute-done | bytes 110624 | tf_op jit(solution)/shard_map/ppermute | solution.py:604
  44.6 2.3 %collective-permute-start.15 = (bf16[48,384]{1,0:T(8,128)(2,1)S(1)}, bf16[48,384]{1,0:T(8,128)(2,1)S(1)}, u32[]{:S(2)}, u32[]{:S(2)}) collective-permute-start(bf16[48,384]{1,0:T(8,128)(2,1)S(1)} %get-tuple-element.66), channel_id=1, source_target_pairs={{0,6},{2,4},{4,2},{6,0},{1,7},{3,5},{5,3},{7,1},{8,14},{10,12},{12... | collective-permute-start | bytes 110600 | tf_op jit(solution)/shard_map/ppermute | solution.py:604
  46.9 2.1 %collective-permute-start.17 = (bf16[48,384]{1,0:T(8,128)(2,1)S(1)}, bf16[48,384]{1,0:T(8,128)(2,1)S(1)}, u32[]{:S(2)}, u32[]{:S(2)}) collective-permute-start(bf16[48,384]{1,0:T(8,128)(2,1)S(1)} %get-tuple-element.68), channel_id=1, source_target_pairs={{0,2},{2,0},{4,6},{6,4},{1,3},{3,1},{5,7},{7,5},{8,10},{10,8},{12,... | collective-permute-start | bytes 110600 | tf_op jit(solution)/shard_map/ppermute | solution.py:604
  49.0 0.6 %by_request.1 = bf16[24,2,384]{2,1,0:T(2,128)(2,1)} custom-call(bf16[48,384]{1,0:T(8,128)(2,1)S(1)} %get-tuple-element.44.after_ref.refs_0_.flat_ref), custom_call_target="tpu_custom_call" | custom-call | flops 100000 | bytes 1000000 | tf_op jit(solution)/shard_map/by_request/pallas_call | solution.py:303
  49.6 0.8 %collective-permute-done.15.refs_0_ = bf16[48,384]{1,0:T(8,128)(2,1)S(1)} collective-permute-done((bf16[48,384]{1,0:T(8,128)(2,1)S(1)}, bf16[48,384]{1,0:T(8,128)(2,1)S(1)}, u32[]{:S(2)}, u32[]{:S(2)}) %collective-permute-start.15) | collective-permute-done | bytes 36896 | tf_op jit(solution)/shard_map/ppermute | solution.py:604
  50.4 1.3 %collective-permute-done.16.refs_1_ = bf16[48,384]{1,0:T(8,128)(2,1)S(1)} collective-permute-done((bf16[48,384]{1,0:T(8,128)(2,1)S(1)}, bf16[48,384]{1,0:T(8,128)(2,1)S(1)}, u32[]{:S(2)}, u32[]{:S(2)}) %collective-permute-start.16) | collective-permute-done | bytes 36896 | tf_op jit(solution)/shard_map/ppermute | solution.py:604
  51.8 0.7 %finish.1 = bf16[24,2,384]{2,1,0:T(2,128)(2,1)} custom-call(f32[48,384]{1,0:T(8,128)S(1)} %get-tuple-element.65.own_ref, bf16[48,384]{1,0:T(8,128)(2,1)S(1)} %collective-permute-done.15.refs_0_, bf16[48,384]{1,0:T(8,128)(2,1)S(1)} %collective-permute-done.16.refs_1_, bf16[48,384]{1,0:T(8,128)(2,1)S(1)} %collective-permute-done.17.refs_2_), custom_call_target="tpu_custom_call" | custom-call | tf_op jit(solution)/shard_map/finish/pallas_call | solution.py:592
  (37 shorter events, 2.5 us)
Async XLA Ops:
  4.8 1.5 %collective-permute-start = (bf16[4,48,384]{2,1,0:T(8,128)(2,1)S(1)}, bf16[4,48,384]{2,1,0:T(8,128)(2,1)S(1)}, u32[]{:S(2)}, u32[]{:S(2)}) collective-permute-start(bf16[4,48,384]{2,1,0:T(8,128)(2,1)S(1)} %get-tuple-element.39), channel_id=1, source_target_pairs={{0,1},{1,0},{2,3},{3,2},{4,5},{5,4},{6,7},{7,6},{8,9},{9,8},{10,11... | collective-permute-start | bytes 442376 | tf_op jit(solution)/shard_map/ppermute | solution.py:604
  6.4 7.8 %collective-permute-start.1 = (bf16[48,384]{1,0:T(8,128)(2,1)S(1)}, bf16[48,384]{1,0:T(8,128)(2,1)S(1)}, u32[]{:S(2)}, u32[]{:S(2)}) collective-permute-start(bf16[48,384]{1,0:T(8,128)(2,1)S(1)} %get-tuple-element.41), channel_id=1, source_target_pairs={{0,7},{1,6},{2,5},{3,4},{4,3},{5,2},{6,1},{7,0},{8,15},{9,14},{10,... | collective-permute-start | bytes 110600 | tf_op jit(solution)/shard_map/ppermute | solution.py:614
  11.1 4.3 %collective-permute-start.2 = (bf16[48,384]{1,0:T(8,128)(2,1)S(1)}, bf16[48,384]{1,0:T(8,128)(2,1)S(1)}, u32[]{:S(2)}, u32[]{:S(2)}) collective-permute-start(bf16[48,384]{1,0:T(8,128)(2,1)S(1)} %get-tuple-element.42), channel_id=1, source_target_pairs={{0,5},{1,4},{2,7},{3,6},{4,1},{5,0},{6,3},{7,2},{8,13},{9,12},{10,... | collective-permute-start | bytes 110600 | tf_op jit(solution)/shard_map/ppermute | solution.py:614
  11.1 4.3 %collective-permute-start.3 = (bf16[48,384]{1,0:T(8,128)(2,1)S(1)}, bf16[48,384]{1,0:T(8,128)(2,1)S(1)}, u32[]{:S(2)}, u32[]{:S(2)}) collective-permute-start(bf16[48,384]{1,0:T(8,128)(2,1)S(1)} %get-tuple-element.43), channel_id=1, source_target_pairs={{0,3},{1,2},{2,1},{3,0},{4,7},{5,6},{6,5},{7,4},{8,11},{9,10},{10,... | collective-permute-start | bytes 110600 | tf_op jit(solution)/shard_map/ppermute | solution.py:614
  11.8 3.7 %copy-start.4 = (bf16[24,2,384]{2,1,0:T(2,128)(2,1)S(1)}, bf16[24,2,384]{2,1,0:T(2,128)(2,1)}, u32[]{:S(2)}) copy-start(bf16[24,2,384]{2,1,0:T(2,128)(2,1)} %residual_ref.1) | copy-start | bytes 110596
  11.8 19.7 %copy-start.1 = (bf16[1,4,384,1152]{3,2,1,0:T(8,128)(2,1)S(1)}, bf16[1,4,384,1152]{3,2,1,0:T(8,128)(2,1)}, u32[]{:S(2)}) copy-start(bf16[1,4,384,1152]{3,2,1,0:T(8,128)(2,1)} %wu_ref.3) | copy-start | bytes 10616836
  14.1 5.8 %copy-start.6 = (s32[24,2,2]{0,2,1:T(2,128)S(1)}, s32[24,2,2]{0,2,1:T(2,128)}, u32[]{:S(2)}) copy-start(s32[24,2,2]{0,2,1:T(2,128)} %param.23) | copy-start | bytes 1156
  14.1 5.8 %copy-start.7 = (f32[24,2,2]{0,2,1:T(2,128)S(1)}, f32[24,2,2]{0,2,1:T(2,128)}, u32[]{:S(2)}) copy-start(f32[24,2,2]{0,2,1:T(2,128)} %param.24) | copy-start | bytes 1156
  14.2 17.3 %copy-start = (bf16[1,4,384,1152]{3,2,1,0:T(8,128)(2,1)S(1)}, bf16[1,4,384,1152]{3,2,1,0:T(8,128)(2,1)}, u32[]{:S(2)}) copy-start(bf16[1,4,384,1152]{3,2,1,0:T(8,128)(2,1)} %wg_ref.3) | copy-start | bytes 10616836
  14.2 17.3 %copy-start.5 = (f32[3072]{0:T(1024)S(1)}, f32[3072]{0:T(1024)}, u32[]{:S(2)}) copy-start(f32[3072]{0:T(1024)} %param.22) | copy-start | bytes 36868
  15.5 6.2 %collective-permute-start.4 = (bf16[48,384]{1,0:T(8,128)(2,1)S(1)}, bf16[48,384]{1,0:T(8,128)(2,1)S(1)}, u32[]{:S(2)}, u32[]{:S(2)}) collective-permute-start(bf16[48,384]{1,0:T(8,128)(2,1)S(1)} %get-tuple-element.46), channel_id=1, source_target_pairs={{0,6},{2,4},{4,2},{6,0},{1,7},{3,5},{5,3},{7,1},{8,14},{10,12},{12... | collective-permute-start | bytes 110600 | tf_op jit(solution)/shard_map/ppermute | solution.py:604
  17.9 5.1 %collective-permute-start.5 = (bf16[48,384]{1,0:T(8,128)(2,1)S(1)}, bf16[48,384]{1,0:T(8,128)(2,1)S(1)}, u32[]{:S(2)}, u32[]{:S(2)}) collective-permute-start(bf16[48,384]{1,0:T(8,128)(2,1)S(1)} %get-tuple-element.47), channel_id=1, source_target_pairs={{0,4},{2,6},{4,0},{6,2},{1,5},{3,7},{5,1},{7,3},{8,12},{10,14},{12... | collective-permute-start | bytes 110600 | tf_op jit(solution)/shard_map/ppermute | solution.py:604
  18.0 4.9 %collective-permute-start.6 = (bf16[48,384]{1,0:T(8,128)(2,1)S(1)}, bf16[48,384]{1,0:T(8,128)(2,1)S(1)}, u32[]{:S(2)}, u32[]{:S(2)}) collective-permute-start(bf16[48,384]{1,0:T(8,128)(2,1)S(1)} %get-tuple-element.48), channel_id=1, source_target_pairs={{0,2},{2,0},{4,6},{6,4},{1,3},{3,1},{5,7},{7,5},{8,10},{10,8},{12,... | collective-permute-start | bytes 110600 | tf_op jit(solution)/shard_map/ppermute | solution.py:604
  23.3 6.0 %collective-permute-start.7 = (bf16[144,384]{1,0:T(8,128)(2,1)S(1)}, bf16[144,384]{1,0:T(8,128)(2,1)S(1)}, u32[]{:S(2)}, u32[]{:S(2)}) collective-permute-start(bf16[144,384]{1,0:T(8,128)(2,1)S(1)} %get-tuple-element.50), channel_id=1, source_target_pairs={{0,24},{8,16},{16,8},{24,0},{1,25},{9,17},{17,9},{25,1},{2,26},{10... | collective-permute-start | bytes 331784 | tf_op jit(solution)/shard_map/ppermute | solution.py:604
  25.8 5.6 %collective-permute-start.8 = (bf16[144,384]{1,0:T(8,128)(2,1)S(1)}, bf16[144,384]{1,0:T(8,128)(2,1)S(1)}, u32[]{:S(2)}, u32[]{:S(2)}) collective-permute-start(bf16[144,384]{1,0:T(8,128)(2,1)S(1)} %get-tuple-element.51), channel_id=1, source_target_pairs={{0,16},{8,24},{16,0},{24,8},{1,17},{9,25},{17,1},{25,9},{2,18},{10... | collective-permute-start | bytes 331784 | tf_op jit(solution)/shard_map/ppermute | solution.py:604
  26.3 5.1 %collective-permute-start.9 = (bf16[144,384]{1,0:T(8,128)(2,1)S(1)}, bf16[144,384]{1,0:T(8,128)(2,1)S(1)}, u32[]{:S(2)}, u32[]{:S(2)}) collective-permute-start(bf16[144,384]{1,0:T(8,128)(2,1)S(1)} %get-tuple-element.52), channel_id=1, source_target_pairs={{0,8},{8,0},{16,24},{24,16},{1,9},{9,1},{17,25},{25,17},{2,10},{10... | collective-permute-start | bytes 331784 | tf_op jit(solution)/shard_map/ppermute | solution.py:604
  32.4 1.8 %collective-permute-start.11 = (bf16[144,1408]{1,0:T(8,128)(2,1)S(1)}, bf16[144,1408]{1,0:T(8,128)(2,1)S(1)}, u32[]{:S(2)}, u32[]{:S(2)}) collective-permute-start(bf16[144,1408]{1,0:T(8,128)(2,1)S(1)} %get-tuple-element.54.part_ref), channel_id=1, source_target_pairs={{0,1},{1,0},{2,3},{3,2},{4,5},{5,4},{6,7},{7,6},{8,9},{9,8},{10,11... | collective-permute-start | bytes 1216520 | tf_op jit(solution)/shard_map/ppermute | solution.py:604
  33.1 2.0 %collective-permute-start.10 = (bf16[144,1024]{1,0:T(8,128)(2,1)S(1)}, bf16[144,1024]{1,0:T(8,128)(2,1)S(1)}, u32[]{:S(2)}, u32[]{:S(2)}) collective-permute-start(bf16[144,1024]{1,0:T(8,128)(2,1)S(1)} %other_units.1.part_ref), channel_id=1, source_target_pairs={{0,1},{1,0},{2,3},{3,2},{4,5},{5,4},{6,7},{7,6},{8,9},{9,8},{10,11... | collective-permute-start | bytes 884744 | tf_op jit(solution)/shard_map/ppermute | solution.py:604
  35.1 4.2 %copy-start.2 = (bf16[24,2,512]{2,1,0:T(2,128)(2,1)S(1)}, bf16[24,2,512]{2,1,0:T(2,128)(2,1)}, u32[]{:S(2)}) copy-start(bf16[24,2,512]{2,1,0:T(2,128)(2,1)} %k_ref.1) | copy-start | bytes 147460
  35.1 4.2 %copy-start.3 = (bf16[24,2,512]{2,1,0:T(2,128)(2,1)S(1)}, bf16[24,2,512]{2,1,0:T(2,128)(2,1)}, u32[]{:S(2)}) copy-start(bf16[24,2,512]{2,1,0:T(2,128)(2,1)} %v_ref.1) | copy-start | bytes 147460
  35.1 4.2 %copy-start.8 = (f32[4]{0:T(128)S(1)}, f32[4]{0:T(128)}, u32[]{:S(2)}) copy-start(f32[4]{0:T(128)} %slope_ref.1) | copy-start | bytes 52
  35.8 6.8 %collective-permute-start.12 = (bf16[144,384]{1,0:T(8,128)(2,1)S(1)}, bf16[144,384]{1,0:T(8,128)(2,1)S(1)}, u32[]{:S(2)}, u32[]{:S(2)}) collective-permute-start(bf16[144,384]{1,0:T(8,128)(2,1)S(1)} %get-tuple-element.62), channel_id=1, source_target_pairs={{0,24},{8,16},{16,8},{24,0},{1,25},{9,17},{17,9},{25,1},{2,26},{10... | collective-permute-start | bytes 331784 | tf_op jit(solution)/shard_map/ppermute | solution.py:604
  37.5 6.7 %collective-permute-start.13 = (bf16[144,384]{1,0:T(8,128)(2,1)S(1)}, bf16[144,384]{1,0:T(8,128)(2,1)S(1)}, u32[]{:S(2)}, u32[]{:S(2)}) collective-permute-start(bf16[144,384]{1,0:T(8,128)(2,1)S(1)} %get-tuple-element.63), channel_id=1, source_target_pairs={{0,16},{8,24},{16,0},{24,8},{1,17},{9,25},{17,1},{25,9},{2,18},{10... | collective-permute-start | bytes 331784 | tf_op jit(solution)/shard_map/ppermute | solution.py:604
  38.8 5.4 %collective-permute-start.14 = (bf16[144,384]{1,0:T(8,128)(2,1)S(1)}, bf16[144,384]{1,0:T(8,128)(2,1)S(1)}, u32[]{:S(2)}, u32[]{:S(2)}) collective-permute-start(bf16[144,384]{1,0:T(8,128)(2,1)S(1)} %get-tuple-element.64), channel_id=1, source_target_pairs={{0,8},{8,0},{16,24},{24,16},{1,9},{9,1},{17,25},{25,17},{2,10},{10... | collective-permute-start | bytes 331784 | tf_op jit(solution)/shard_map/ppermute | solution.py:604
  44.6 5.8 %collective-permute-start.15 = (bf16[48,384]{1,0:T(8,128)(2,1)S(1)}, bf16[48,384]{1,0:T(8,128)(2,1)S(1)}, u32[]{:S(2)}, u32[]{:S(2)}) collective-permute-start(bf16[48,384]{1,0:T(8,128)(2,1)S(1)} %get-tuple-element.66), channel_id=1, source_target_pairs={{0,6},{2,4},{4,2},{6,0},{1,7},{3,5},{5,3},{7,1},{8,14},{10,12},{12... | collective-permute-start | bytes 110600 | tf_op jit(solution)/shard_map/ppermute | solution.py:604
  46.9 4.9 %collective-permute-start.16 = (bf16[48,384]{1,0:T(8,128)(2,1)S(1)}, bf16[48,384]{1,0:T(8,128)(2,1)S(1)}, u32[]{:S(2)}, u32[]{:S(2)}) collective-permute-start(bf16[48,384]{1,0:T(8,128)(2,1)S(1)} %get-tuple-element.67), channel_id=1, source_target_pairs={{0,4},{2,6},{4,0},{6,2},{1,5},{3,7},{5,1},{7,3},{8,12},{10,14},{12... | collective-permute-start | bytes 110600 | tf_op jit(solution)/shard_map/ppermute | solution.py:604
  46.9 4.9 %collective-permute-start.17 = (bf16[48,384]{1,0:T(8,128)(2,1)S(1)}, bf16[48,384]{1,0:T(8,128)(2,1)S(1)}, u32[]{:S(2)}, u32[]{:S(2)}) collective-permute-start(bf16[48,384]{1,0:T(8,128)(2,1)S(1)} %get-tuple-element.68), channel_id=1, source_target_pairs={{0,2},{2,0},{4,6},{6,4},{1,3},{3,1},{5,7},{7,5},{8,10},{10,8},{12,... | collective-permute-start | bytes 110600 | tf_op jit(solution)/shard_map/ppermute | solution.py:604

commit v7 on v6

--- a/solution.py
+++ b/solution.py
@@ -50,17 +50,17 @@
     return jnp.where((lax.axis_index("heads") == a) == mine, side, 1 - side)
 
 
-def load_columns(w_hbm, weight, sems, mine):
+def load_columns(w_hbm, weight, sems, mine, first=0):
     groups, _, piece = weight.shape
-    if groups == 1:
+    if piece == w_hbm.shape[1]:
         return [pltpu.make_async_copy(w_hbm, weight.at[0], sems.at[0])]
     return [
         pltpu.make_async_copy(
             w_hbm.at[:, pl.ds(pl.multiple_of((2 * a + side_of(a, mine)) * piece, 128), piece)],
-            weight.at[a],
+            weight.at[a - first],
             sems.at[a],
         )
-        for a in range(groups)
+        for a in range(first, first + groups)
     ]
 
 
@@ -68,6 +68,10 @@
     rows, width = out_weight.shape
     piece = width // (2 * groups)
     return (groups, rows, piece) if piece % 128 == 0 else (1, rows, width)
+
+
+def early_part(shape):
+    return (shape[0] - shape[0] // 4, *shape[1:])
 
 
 def project_columns(loads, weight, normed, mine, out_ref):
@@ -163,7 +167,7 @@
             in_vmem((groups, rows, piece), BF),
             in_vmem((rows, width), BF),
             in_vmem(head_states.shape, BF),
-            in_vmem(columns_shape(out_weight, groups), BF),
+            in_vmem(early_part(columns_shape(out_weight, groups)), BF),
         ],
         scratch_shapes=[
             pltpu.SMEM(slopes.shape, F32), vec, vec, vec,
@@ -179,20 +183,40 @@
     )(*[from_hbm(x) if x.size > 1 else x for x in operands])
 
 
-def project_kernel(normed_ref, weight, mine_ref):
-    project_columns([], weight, normed_ref[...], True, mine_ref)
-
-
-def project(normed, weight, shape):
+def project_kernel(w_hbm, normed_ref, weight, mine_ref, later=None, sems=None):
+    normed = normed_ref[...]
+    if later is None:
+        project_columns([], weight, normed, True, mine_ref)
+        return
+    held = weight.shape[0]
+    loads = load_columns(w_hbm, later, sems, True, held)
+    for copy in loads:
+        copy.start()
+    for a in range(held):
+        mine_ref[a] = dot(normed, weight[a])
+    for i, copy in enumerate(loads):
+        copy.wait()
+        mine_ref[held + i] = dot(normed, later[i])
+
+
+def project(out_weight, normed, weight, shape):
+    groups, held = shape[0], weight.shape[0]
+    scratch = []
+    if weight.shape[2] == shape[2] and held < groups:
+        scratch = [
+            pltpu.VMEM((groups - held, *weight.shape[1:]), BF),
+            pltpu.SemaphoreType.DMA((groups,)),
+        ]
     return pl.pallas_call(
         project_kernel,
-        in_specs=whole_vmem(2),
+        in_specs=hbm_specs(1) + whole_vmem(2),
         out_specs=whole_vmem(1)[0],
         out_shape=in_vmem(shape, F32),
+        scratch_shapes=scratch,
         compiler_params=params(),
         cost_estimate=cost(10**8, 2 * 10**6),
         name="project",
-    )(normed, weight)
+    )(from_hbm(out_weight), normed, weight)
 
 
 def state_kernel(slope_ref, k_ref, v_ref, s_ref, after_ref, so_hbm, done_ref, out, sems):
@@ -628,7 +652,7 @@
         slopes, queries, new_keys, new_values, head_states,
         head_gain.reshape(1, -1), out_weight, groups,
     )
-    mine = project(normed, weight, other.shape)
+    mine = project(out_weight, normed, weight, other.shape)
     own, *sends = split(mine, swap(other, "side", 1))
     weights = regroup(w_down, own)
     flat, *sends = add_residual(residual, weights, own, cross_swaps(sends))

time: 52.6 us -> 52.5 us (level)
  Pallas kernels: 15.1 us -> 16 us
  waiting for transfers between devices: 13.9 us -> 13.3 us
    ppermute x15, waiting for transfers between devices: 12.6 us -> 11.5 us  [swap(): return lax.ppermute(x, axis, [(i, i ^ k) for i in range(size)])]
    pallas_call x1, Pallas kernels: 0.34 us -> 1.37 us  [project(): pl.pallas_call(project_kernel, in_specs=hbm_specs(1) + whole_vmem(2), out...]
  transfers between devices with their start and end apart: 18 -> 18, of which waited for: 12 -> 11; matrix products, arithmetic and copies ran while one was open for 0% -> 0% of each run, Pallas kernels for 15% -> 17%
where the time goes in v7:
time: 52.5 us; the launch traced here: 52.4 us
  starting transfers between devices  22.2 us (42%)
  Pallas kernels  16 us (30%)
  waiting for transfers between devices  13.3 us (25%)
  between operations  0.82 us (2%)
    ppermute x15, starting transfers between devices, swap(): return lax.ppermute(x, axis, [(i, i ^ k) for i in range(size)])  17.2 us
    ppermute x15, waiting for transfers between devices, swap(): return lax.ppermute(x, axis, [(i, i ^ k) for i in range(size)])  11.5 us
    ppermute x3, starting transfers between devices, cross_swaps(): lax.ppermute(x, ('heads', 'side'), [(2 * i + s, 2 * (i ^ k) + 1 - s) for...  5.04 us
    pallas_call x1, Pallas kernels, attention(): pl.pallas_call(attention_kernel, in_specs=hbm_specs(7), out_specs=whole_v...  4.04 us
    pallas_call x1, Pallas kernels, new_state(): pl.pallas_call(state_kernel, in_specs=[pl.BlockSpec(memory_space=pltpu.SM...  2.88 us
    pallas_call x1, Pallas kernels, regroup(): pl.pallas_call(regroup_kernel, in_specs=[*hbm_specs(1), pl.BlockSpec(memo...  2.37 us
    ppermute x3, waiting for transfers between devices, cross_swaps(): lax.ppermute(x, ('heads', 'side'), [(2 * i + s, 2 * (i ^ k) + 1 - s) for...  1.78 us
    pallas_call x1, Pallas kernels, project(): pl.pallas_call(project_kernel, in_specs=hbm_specs(1) + whole_vmem(2), out...  1.37 us
  transfers between devices with their start and end apart: 18, of which 11 were waited for; matrix products, arithmetic and copies ran while one was open for 0% of the time, Pallas kernels for 17%

profile of v7, /device:TPU:0, one launch (start us, length us, event | category | flops | bytes accessed | tf_op | source)
XLA Modules:
  0.0 52.4 jit_solution(589101331612739506)
XLA Ops:
  0.6 4.0 %attention.1 = (bf16[4,48,384]{2,1,0:T(8,128)(2,1)S(1)}, bf16[48,512]{1,0:T(8,128)(2,1)S(1)}, bf16[24,4,128,128]{3,2,1,0:T(8,128)(2,1)S(1)}, bf16[3,512,384]{2,1,0:T(8,128)(2,1)S(1)}) custom-call(f32[4]{0:T(128)} %slope_ref.1, bf16[24,2,512]{2,1,0:T(2,128)(2,1)} %q_hbm.1, bf16[24,2,512]{2,1,0:T(2,128)(2,1)} %k_ref.1, bf16[24,2,512]{2,1,0:T(2,128)(2,1)} %v_ref.1, ...), custom_call_target="tpu_custom_call" | custom-call | tf_op jit(solution)/shard_map/attention/pallas_call | solution.py:162
  4.7 0.5 collective-permute-start
  5.2 1.4 %project.1.mine_ref = f32[4,48,384]{2,1,0:T(8,128)S(1)} custom-call(bf16[512,3072]{1,0:T(8,128)(2,1)} %w_hbm.4, bf16[48,512]{1,0:T(8,128)(2,1)S(1)} %get-tuple-element.37.normed_ref, bf16[3,512,384]{2,1,0:T(8,128)(2,1)S(1)} %get-tuple-element.38.weight), custom_call_target="tpu_custom_call" | custom-call | flops 100000000 | bytes 2000000 | tf_op jit(solution)/shard_map/project/pallas_call | solution.py:210
  6.6 4.8 %collective-permute-start.1 = (bf16[48,384]{1,0:T(8,128)(2,1)S(1)}, bf16[48,384]{1,0:T(8,128)(2,1)S(1)}, u32[]{:S(2)}, u32[]{:S(2)}) collective-permute-start(bf16[48,384]{1,0:T(8,128)(2,1)S(1)} %get-tuple-element.41), channel_id=1, source_target_pairs={{0,7},{1,6},{2,5},{3,4},{4,3},{5,2},{6,1},{7,0},{8,15},{9,14},{10,... | collective-permute-start | bytes 110600 | tf_op jit(solution)/shard_map/ppermute | solution.py:638
  11.7 2.4 %regroup_down.1.after_ref.w_ref = bf16[4,1152,384]{2,1,0:T(8,128)(2,1)S(1)} custom-call(bf16[1,1152,4,384]{3,2,1,0:T(4,128)(2,1)} %w_hbm.5, f32[48,384]{1,0:T(8,128)S(1)} %get-tuple-element.40.after_ref.own_ref), custom_call_target="tpu_custom_call" | custom-call | flops 100000000 | bytes 7000000 | tf_op jit(solution)/shard_map/regroup_down/pallas_call | solution.py:510
  14.1 1.8 %collective-permute-done.2.refs_1_ = bf16[48,384]{1,0:T(8,128)(2,1)S(1)} collective-permute-done((bf16[48,384]{1,0:T(8,128)(2,1)S(1)}, bf16[48,384]{1,0:T(8,128)(2,1)S(1)}, u32[]{:S(2)}, u32[]{:S(2)}) %collective-permute-start.2) | collective-permute-done | bytes 36896 | tf_op jit(solution)/shard_map/ppermute | solution.py:638
  15.9 2.2 %collective-permute-start.4 = (bf16[48,384]{1,0:T(8,128)(2,1)S(1)}, bf16[48,384]{1,0:T(8,128)(2,1)S(1)}, u32[]{:S(2)}, u32[]{:S(2)}) collective-permute-start(bf16[48,384]{1,0:T(8,128)(2,1)S(1)} %get-tuple-element.46), channel_id=1, source_target_pairs={{0,6},{2,4},{4,2},{6,0},{1,7},{3,5},{5,3},{7,1},{8,14},{10,12},{12... | collective-permute-start | bytes 110600 | tf_op jit(solution)/shard_map/ppermute | solution.py:628
  18.1 2.3 %collective-permute-start.6 = (bf16[48,384]{1,0:T(8,128)(2,1)S(1)}, bf16[48,384]{1,0:T(8,128)(2,1)S(1)}, u32[]{:S(2)}, u32[]{:S(2)}) collective-permute-start(bf16[48,384]{1,0:T(8,128)(2,1)S(1)} %get-tuple-element.48), channel_id=1, source_target_pairs={{0,2},{2,0},{4,6},{6,4},{1,3},{3,1},{5,7},{7,5},{8,10},{10,8},{12,... | collective-permute-start | bytes 110600 | tf_op jit(solution)/shard_map/ppermute | solution.py:628
  20.6 1.4 %collective-permute-done.4.refs_1_ = bf16[48,384]{1,0:T(8,128)(2,1)S(1)} collective-permute-done((bf16[48,384]{1,0:T(8,128)(2,1)S(1)}, bf16[48,384]{1,0:T(8,128)(2,1)S(1)}, u32[]{:S(2)}, u32[]{:S(2)}) %collective-permute-start.4) | collective-permute-done | bytes 36896 | tf_op jit(solution)/shard_map/ppermute | solution.py:628
  22.0 1.1 %collective-permute-done.5.refs_2_ = bf16[48,384]{1,0:T(8,128)(2,1)S(1)} collective-permute-done((bf16[48,384]{1,0:T(8,128)(2,1)S(1)}, bf16[48,384]{1,0:T(8,128)(2,1)S(1)}, u32[]{:S(2)}, u32[]{:S(2)}) %collective-permute-start.5) | collective-permute-done | bytes 36896 | tf_op jit(solution)/shard_map/ppermute | solution.py:628
  23.5 2.5 %collective-permute-start.7 = (bf16[144,384]{1,0:T(8,128)(2,1)S(1)}, bf16[144,384]{1,0:T(8,128)(2,1)S(1)}, u32[]{:S(2)}, u32[]{:S(2)}) collective-permute-start(bf16[144,384]{1,0:T(8,128)(2,1)S(1)} %get-tuple-element.50), channel_id=1, source_target_pairs={{0,24},{8,16},{16,8},{24,0},{1,25},{9,17},{17,9},{25,1},{2,26},{10... | collective-permute-start | bytes 331784 | tf_op jit(solution)/shard_map/ppermute | solution.py:628
  26.0 0.5 collective-permute-start.8
  26.5 0.5 %collective-permute-start.9 = (bf16[144,384]{1,0:T(8,128)(2,1)S(1)}, bf16[144,384]{1,0:T(8,128)(2,1)S(1)}, u32[]{:S(2)}, u32[]{:S(2)}) collective-permute-start(bf16[144,384]{1,0:T(8,128)(2,1)S(1)} %get-tuple-element.52), channel_id=1, source_target_pairs={{0,8},{8,0},{16,24},{24,16},{1,9},{9,1},{17,25},{25,17},{2,10},{10... | collective-permute-start | bytes 331784 | tf_op jit(solution)/shard_map/ppermute | solution.py:628
  27.0 2.4 %collective-permute-done.7.refs_1_ = bf16[144,384]{1,0:T(8,128)(2,1)S(1)} collective-permute-done((bf16[144,384]{1,0:T(8,128)(2,1)S(1)}, bf16[144,384]{1,0:T(8,128)(2,1)S(1)}, u32[]{:S(2)}, u32[]{:S(2)}) %collective-permute-start.7) | collective-permute-done | bytes 110624 | tf_op jit(solution)/shard_map/ppermute | solution.py:628
  29.4 2.2 %collective-permute-done.8.refs_2_ = bf16[144,384]{1,0:T(8,128)(2,1)S(1)} collective-permute-done((bf16[144,384]{1,0:T(8,128)(2,1)S(1)}, bf16[144,384]{1,0:T(8,128)(2,1)S(1)}, u32[]{:S(2)}, u32[]{:S(2)}) %collective-permute-start.8) | collective-permute-done | bytes 110624 | tf_op jit(solution)/shard_map/ppermute | solution.py:628
  31.7 1.0 %first_units.1 = (bf16[144,1408]{1,0:T(8,128)(2,1)S(1)}, bf16[144,1536]{1,0:T(8,128)(2,1)S(1)}) custom-call(f32[1,3072]{1,0:T(1,128)S(1)} %bitcast.4, bf16[1,4,384,1152]{3,2,1,0:T(8,128)(2,1)S(1)} %copy-done, bf16[1,4,384,1152]{3,2,1,0:T(8,128)(2,1)S(1)} %copy-done.1, bf16[144,384]{1,0:T(8,128)(2,1)S(1)} %get-tuple-element.49.refs_0_, ...), custom_call_target="tpu_custom_call" | custom-call | tf_op jit(solution)/shard_map/first_units/pallas_call | solution.py:452
  32.8 0.6 %other_units.1.part_ref = bf16[144,1024]{1,0:T(8,128)(2,1)S(1)} custom-call(bf16[144,1536]{1,0:T(8,128)(2,1)S(1)} %get-tuple-element.53.lhs_ref, bf16[1,4,384,1152]{3,2,1,0:T(8,128)(2,1)S(1)} %copy-done, bf16[1,4,384,1152]{3,2,1,0:T(8,128)(2,1)S(1)} %copy-done.1), custom_call_target="tpu_custom_call" | custom-call | flops 1000000000 | bytes 4000000 | tf_op jit(solution)/shard_map/other_units/pallas_call | solution.py:471
  33.4 0.6 %collective-permute-start.10 = (bf16[144,1024]{1,0:T(8,128)(2,1)S(1)}, bf16[144,1024]{1,0:T(8,128)(2,1)S(1)}, u32[]{:S(2)}, u32[]{:S(2)}) collective-permute-start(bf16[144,1024]{1,0:T(8,128)(2,1)S(1)} %other_units.1.part_ref), channel_id=1, source_target_pairs={{0,1},{1,0},{2,3},{3,2},{4,5},{5,4},{6,7},{7,6},{8,9},{9,8},{10,11... | collective-permute-start | bytes 884744 | tf_op jit(solution)/shard_map/ppermute | solution.py:628
  34.0 0.5 %collective-permute-done.11.recv_ref = bf16[144,1408]{1,0:T(8,128)(2,1)S(1)} collective-permute-done((bf16[144,1408]{1,0:T(8,128)(2,1)S(1)}, bf16[144,1408]{1,0:T(8,128)(2,1)S(1)}, u32[]{:S(2)}, u32[]{:S(2)}) %collective-permute-start.11) | collective-permute-done | bytes 405536 | tf_op jit(solution)/shard_map/ppermute | solution.py:628
  34.5 0.9 %down_first.1 = (f32[4,144,384]{2,1,0:T(8,128)S(1)}, f32[144,128]{1,0:T(8,128)S(1)}) custom-call(bf16[144,1408]{1,0:T(8,128)(2,1)S(1)} %get-tuple-element.54.part_ref, bf16[144,1408]{1,0:T(8,128)(2,1)S(1)} %collective-permute-done.11.recv_ref, bf16[4,1152,384]{2,1,0:T(8,128)(2,1)S(1)} %regroup_down.1.after_ref.w_ref), custom_call_target="tpu_custom_call" | custom-call | flops 1000000000 | bytes 4000000 | tf_op jit(solution)/shard_map/down_first/pallas_call | solution.py:546
  35.5 0.6 %down.1 = (bf16[144,384]{1,0:T(8,128)(2,1)S(1)}, bf16[144,384]{1,0:T(8,128)(2,1)S(1)}, bf16[144,384]{1,0:T(8,128)(2,1)S(1)}, bf16[144,384]{1,0:T(8,128)(2,1)S(1)}) custom-call(bf16[144,1024]{1,0:T(8,128)(2,1)S(1)} %other_units.1.part_ref, bf16[144,1024]{1,0:T(8,128)(2,1)S(1)} %collective-permute-done.10.recv_ref, ...), custom_call_target="tpu_custom_call" | custom-call | tf_op jit(solution)/shard_map/down/pallas_call | solution.py:570
  36.1 1.8 %collective-permute-start.12 = (bf16[144,384]{1,0:T(8,128)(2,1)S(1)}, bf16[144,384]{1,0:T(8,128)(2,1)S(1)}, u32[]{:S(2)}, u32[]{:S(2)}) collective-permute-start(bf16[144,384]{1,0:T(8,128)(2,1)S(1)} %get-tuple-element.62), channel_id=1, source_target_pairs={{0,24},{8,16},{16,8},{24,0},{1,25},{9,17},{17,9},{25,1},{2,26},{10... | collective-permute-start | bytes 331784 | tf_op jit(solution)/shard_map/ppermute | solution.py:628
  37.8 1.3 %collective-permute-start.13 = (bf16[144,384]{1,0:T(8,128)(2,1)S(1)}, bf16[144,384]{1,0:T(8,128)(2,1)S(1)}, u32[]{:S(2)}, u32[]{:S(2)}) collective-permute-start(bf16[144,384]{1,0:T(8,128)(2,1)S(1)} %get-tuple-element.63), channel_id=1, source_target_pairs={{0,16},{8,24},{16,0},{24,8},{1,17},{9,25},{17,1},{25,9},{2,18},{10... | collective-permute-start | bytes 331784 | tf_op jit(solution)/shard_map/ppermute | solution.py:628
  39.1 0.5 collective-permute-start.14
  39.6 2.9 %new_state.1 = (bf16[24,4,128,128]{3,2,1,0:T(8,128)(2,1)}, f32[8,128]{1,0:T(8,128)S(1)}) custom-call(f32[4]{0:T(128)S(1)} %copy-done.8, bf16[24,2,512]{2,1,0:T(2,128)(2,1)S(1)} %copy-done.2, bf16[24,2,512]{2,1,0:T(2,128)(2,1)S(1)} %copy-done.3, bf16[24,4,128,128]{3,2,1,0:T(8,128)(2,1)S(1)} %get-tuple-element.36.s_ref, ...), custom_call_target="tpu_custom_call" | custom-call | flops 100000000 | bytes 8000000 | tf_op jit(solution)/shard_map/new_state/pallas_call | solution.py:261
  42.8 1.7 %collective-permute-done.13.refs_2_ = bf16[144,384]{1,0:T(8,128)(2,1)S(1)} collective-permute-done((bf16[144,384]{1,0:T(8,128)(2,1)S(1)}, bf16[144,384]{1,0:T(8,128)(2,1)S(1)}, u32[]{:S(2)}, u32[]{:S(2)}) %collective-permute-start.13) | collective-permute-done | bytes 110624 | tf_op jit(solution)/shard_map/ppermute | solution.py:628
  44.9 1.9 %collective-permute-start.15 = (bf16[48,384]{1,0:T(8,128)(2,1)S(1)}, bf16[48,384]{1,0:T(8,128)(2,1)S(1)}, u32[]{:S(2)}, u32[]{:S(2)}) collective-permute-start(bf16[48,384]{1,0:T(8,128)(2,1)S(1)} %get-tuple-element.66), channel_id=1, source_target_pairs={{0,6},{2,4},{4,2},{6,0},{1,7},{3,5},{5,3},{7,1},{8,14},{10,12},{12... | collective-permute-start | bytes 110600 | tf_op jit(solution)/shard_map/ppermute | solution.py:628
  47.2 2.1 %collective-permute-start.17 = (bf16[48,384]{1,0:T(8,128)(2,1)S(1)}, bf16[48,384]{1,0:T(8,128)(2,1)S(1)}, u32[]{:S(2)}, u32[]{:S(2)}) collective-permute-start(bf16[48,384]{1,0:T(8,128)(2,1)S(1)} %get-tuple-element.68), channel_id=1, source_target_pairs={{0,2},{2,0},{4,6},{6,4},{1,3},{3,1},{5,7},{7,5},{8,10},{10,8},{12,... | collective-permute-start | bytes 110600 | tf_op jit(solution)/shard_map/ppermute | solution.py:628
  49.3 0.6 %by_request.1 = bf16[24,2,384]{2,1,0:T(2,128)(2,1)} custom-call(bf16[48,384]{1,0:T(8,128)(2,1)S(1)} %get-tuple-element.44.after_ref.refs_0_.flat_ref), custom_call_target="tpu_custom_call" | custom-call | flops 100000 | bytes 1000000 | tf_op jit(solution)/shard_map/by_request/pallas_call | solution.py:327
  49.9 0.7 %collective-permute-done.15.refs_0_ = bf16[48,384]{1,0:T(8,128)(2,1)S(1)} collective-permute-done((bf16[48,384]{1,0:T(8,128)(2,1)S(1)}, bf16[48,384]{1,0:T(8,128)(2,1)S(1)}, u32[]{:S(2)}, u32[]{:S(2)}) %collective-permute-start.15) | collective-permute-done | bytes 36896 | tf_op jit(solution)/shard_map/ppermute | solution.py:628
  50.7 1.0 %collective-permute-done.16.refs_1_ = bf16[48,384]{1,0:T(8,128)(2,1)S(1)} collective-permute-done((bf16[48,384]{1,0:T(8,128)(2,1)S(1)}, bf16[48,384]{1,0:T(8,128)(2,1)S(1)}, u32[]{:S(2)}, u32[]{:S(2)}) %collective-permute-start.16) | collective-permute-done | bytes 36896 | tf_op jit(solution)/shard_map/ppermute | solution.py:628
  51.7 0.7 %finish.1 = bf16[24,2,384]{2,1,0:T(2,128)(2,1)} custom-call(f32[48,384]{1,0:T(8,128)S(1)} %get-tuple-element.65.own_ref, bf16[48,384]{1,0:T(8,128)(2,1)S(1)} %collective-permute-done.15.refs_0_, bf16[48,384]{1,0:T(8,128)(2,1)S(1)} %collective-permute-done.16.refs_1_, bf16[48,384]{1,0:T(8,128)(2,1)S(1)} %collective-permute-done.17.refs_2_), custom_call_target="tpu_custom_call" | custom-call | tf_op jit(solution)/shard_map/finish/pallas_call | solution.py:616
  (37 shorter events, 2.3 us)
Async XLA Ops:
  4.7 1.9 %collective-permute-start = (bf16[4,48,384]{2,1,0:T(8,128)(2,1)S(1)}, bf16[4,48,384]{2,1,0:T(8,128)(2,1)S(1)}, u32[]{:S(2)}, u32[]{:S(2)}) collective-permute-start(bf16[4,48,384]{2,1,0:T(8,128)(2,1)S(1)} %get-tuple-element.39), channel_id=1, source_target_pairs={{0,1},{1,0},{2,3},{3,2},{4,5},{5,4},{6,7},{7,6},{8,9},{9,8},{10,11... | collective-permute-start | bytes 442376 | tf_op jit(solution)/shard_map/ppermute | solution.py:628
  6.6 7.5 %collective-permute-start.1 = (bf16[48,384]{1,0:T(8,128)(2,1)S(1)}, bf16[48,384]{1,0:T(8,128)(2,1)S(1)}, u32[]{:S(2)}, u32[]{:S(2)}) collective-permute-start(bf16[48,384]{1,0:T(8,128)(2,1)S(1)} %get-tuple-element.41), channel_id=1, source_target_pairs={{0,7},{1,6},{2,5},{3,4},{4,3},{5,2},{6,1},{7,0},{8,15},{9,14},{10,... | collective-permute-start | bytes 110600 | tf_op jit(solution)/shard_map/ppermute | solution.py:638
  11.4 4.5 %collective-permute-start.2 = (bf16[48,384]{1,0:T(8,128)(2,1)S(1)}, bf16[48,384]{1,0:T(8,128)(2,1)S(1)}, u32[]{:S(2)}, u32[]{:S(2)}) collective-permute-start(bf16[48,384]{1,0:T(8,128)(2,1)S(1)} %get-tuple-element.42), channel_id=1, source_target_pairs={{0,5},{1,4},{2,7},{3,6},{4,1},{5,0},{6,3},{7,2},{8,13},{9,12},{10,... | collective-permute-start | bytes 110600 | tf_op jit(solution)/shard_map/ppermute | solution.py:638
  11.4 4.5 %collective-permute-start.3 = (bf16[48,384]{1,0:T(8,128)(2,1)S(1)}, bf16[48,384]{1,0:T(8,128)(2,1)S(1)}, u32[]{:S(2)}, u32[]{:S(2)}) collective-permute-start(bf16[48,384]{1,0:T(8,128)(2,1)S(1)} %get-tuple-element.43), channel_id=1, source_target_pairs={{0,3},{1,2},{2,1},{3,0},{4,7},{5,6},{6,5},{7,4},{8,11},{9,10},{10,... | collective-permute-start | bytes 110600 | tf_op jit(solution)/shard_map/ppermute | solution.py:638
  11.7 4.2 %copy-start.4 = (bf16[24,2,384]{2,1,0:T(2,128)(2,1)S(1)}, bf16[24,2,384]{2,1,0:T(2,128)(2,1)}, u32[]{:S(2)}) copy-start(bf16[24,2,384]{2,1,0:T(2,128)(2,1)} %residual_ref.1) | copy-start | bytes 110596
  11.7 20.1 %copy-start.1 = (bf16[1,4,384,1152]{3,2,1,0:T(8,128)(2,1)S(1)}, bf16[1,4,384,1152]{3,2,1,0:T(8,128)(2,1)}, u32[]{:S(2)}) copy-start(bf16[1,4,384,1152]{3,2,1,0:T(8,128)(2,1)} %wu_ref.3) | copy-start | bytes 10616836
  14.1 6.3 %copy-start.6 = (s32[24,2,2]{0,2,1:T(2,128)S(1)}, s32[24,2,2]{0,2,1:T(2,128)}, u32[]{:S(2)}) copy-start(s32[24,2,2]{0,2,1:T(2,128)} %param.23) | copy-start | bytes 1156
  14.1 6.3 %copy-start.7 = (f32[24,2,2]{0,2,1:T(2,128)S(1)}, f32[24,2,2]{0,2,1:T(2,128)}, u32[]{:S(2)}) copy-start(f32[24,2,2]{0,2,1:T(2,128)} %param.24) | copy-start | bytes 1156
  14.1 17.7 %copy-start = (bf16[1,4,384,1152]{3,2,1,0:T(8,128)(2,1)S(1)}, bf16[1,4,384,1152]{3,2,1,0:T(8,128)(2,1)}, u32[]{:S(2)}) copy-start(bf16[1,4,384,1152]{3,2,1,0:T(8,128)(2,1)} %wg_ref.3) | copy-start | bytes 10616836
  14.1 17.6 %copy-start.5 = (f32[3072]{0:T(1024)S(1)}, f32[3072]{0:T(1024)}, u32[]{:S(2)}) copy-start(f32[3072]{0:T(1024)} %param.22) | copy-start | bytes 36868
  15.9 6.1 %collective-permute-start.4 = (bf16[48,384]{1,0:T(8,128)(2,1)S(1)}, bf16[48,384]{1,0:T(8,128)(2,1)S(1)}, u32[]{:S(2)}, u32[]{:S(2)}) collective-permute-start(bf16[48,384]{1,0:T(8,128)(2,1)S(1)} %get-tuple-element.46), channel_id=1, source_target_pairs={{0,6},{2,4},{4,2},{6,0},{1,7},{3,5},{5,3},{7,1},{8,14},{10,12},{12... | collective-permute-start | bytes 110600 | tf_op jit(solution)/shard_map/ppermute | solution.py:628
  18.1 5.0 %collective-permute-start.5 = (bf16[48,384]{1,0:T(8,128)(2,1)S(1)}, bf16[48,384]{1,0:T(8,128)(2,1)S(1)}, u32[]{:S(2)}, u32[]{:S(2)}) collective-permute-start(bf16[48,384]{1,0:T(8,128)(2,1)S(1)} %get-tuple-element.47), channel_id=1, source_target_pairs={{0,4},{2,6},{4,0},{6,2},{1,5},{3,7},{5,1},{7,3},{8,12},{10,14},{12... | collective-permute-start | bytes 110600 | tf_op jit(solution)/shard_map/ppermute | solution.py:628
  18.1 5.0 %collective-permute-start.6 = (bf16[48,384]{1,0:T(8,128)(2,1)S(1)}, bf16[48,384]{1,0:T(8,128)(2,1)S(1)}, u32[]{:S(2)}, u32[]{:S(2)}) collective-permute-start(bf16[48,384]{1,0:T(8,128)(2,1)S(1)} %get-tuple-element.48), channel_id=1, source_target_pairs={{0,2},{2,0},{4,6},{6,4},{1,3},{3,1},{5,7},{7,5},{8,10},{10,8},{12,... | collective-permute-start | bytes 110600 | tf_op jit(solution)/shard_map/ppermute | solution.py:628
  23.5 6.0 %collective-permute-start.7 = (bf16[144,384]{1,0:T(8,128)(2,1)S(1)}, bf16[144,384]{1,0:T(8,128)(2,1)S(1)}, u32[]{:S(2)}, u32[]{:S(2)}) collective-permute-start(bf16[144,384]{1,0:T(8,128)(2,1)S(1)} %get-tuple-element.50), channel_id=1, source_target_pairs={{0,24},{8,16},{16,8},{24,0},{1,25},{9,17},{17,9},{25,1},{2,26},{10... | collective-permute-start | bytes 331784 | tf_op jit(solution)/shard_map/ppermute | solution.py:628
  26.0 5.7 %collective-permute-start.8 = (bf16[144,384]{1,0:T(8,128)(2,1)S(1)}, bf16[144,384]{1,0:T(8,128)(2,1)S(1)}, u32[]{:S(2)}, u32[]{:S(2)}) collective-permute-start(bf16[144,384]{1,0:T(8,128)(2,1)S(1)} %get-tuple-element.51), channel_id=1, source_target_pairs={{0,16},{8,24},{16,0},{24,8},{1,17},{9,25},{17,1},{25,9},{2,18},{10... | collective-permute-start | bytes 331784 | tf_op jit(solution)/shard_map/ppermute | solution.py:628
  26.5 5.2 %collective-permute-start.9 = (bf16[144,384]{1,0:T(8,128)(2,1)S(1)}, bf16[144,384]{1,0:T(8,128)(2,1)S(1)}, u32[]{:S(2)}, u32[]{:S(2)}) collective-permute-start(bf16[144,384]{1,0:T(8,128)(2,1)S(1)} %get-tuple-element.52), channel_id=1, source_target_pairs={{0,8},{8,0},{16,24},{24,16},{1,9},{9,1},{17,25},{25,17},{2,10},{10... | collective-permute-start | bytes 331784 | tf_op jit(solution)/shard_map/ppermute | solution.py:628
  32.7 1.8 %collective-permute-start.11 = (bf16[144,1408]{1,0:T(8,128)(2,1)S(1)}, bf16[144,1408]{1,0:T(8,128)(2,1)S(1)}, u32[]{:S(2)}, u32[]{:S(2)}) collective-permute-start(bf16[144,1408]{1,0:T(8,128)(2,1)S(1)} %get-tuple-element.54.part_ref), channel_id=1, source_target_pairs={{0,1},{1,0},{2,3},{3,2},{4,5},{5,4},{6,7},{7,6},{8,9},{9,8},{10,11... | collective-permute-start | bytes 1216520 | tf_op jit(solution)/shard_map/ppermute | solution.py:628
  33.4 2.0 %collective-permute-start.10 = (bf16[144,1024]{1,0:T(8,128)(2,1)S(1)}, bf16[144,1024]{1,0:T(8,128)(2,1)S(1)}, u32[]{:S(2)}, u32[]{:S(2)}) collective-permute-start(bf16[144,1024]{1,0:T(8,128)(2,1)S(1)} %other_units.1.part_ref), channel_id=1, source_target_pairs={{0,1},{1,0},{2,3},{3,2},{4,5},{5,4},{6,7},{7,6},{8,9},{9,8},{10,11... | collective-permute-start | bytes 884744 | tf_op jit(solution)/shard_map/ppermute | solution.py:628
  35.4 4.2 %copy-start.2 = (bf16[24,2,512]{2,1,0:T(2,128)(2,1)S(1)}, bf16[24,2,512]{2,1,0:T(2,128)(2,1)}, u32[]{:S(2)}) copy-start(bf16[24,2,512]{2,1,0:T(2,128)(2,1)} %k_ref.1) | copy-start | bytes 147460
  35.4 4.2 %copy-start.3 = (bf16[24,2,512]{2,1,0:T(2,128)(2,1)S(1)}, bf16[24,2,512]{2,1,0:T(2,128)(2,1)}, u32[]{:S(2)}) copy-start(bf16[24,2,512]{2,1,0:T(2,128)(2,1)} %v_ref.1) | copy-start | bytes 147460
  35.4 4.2 %copy-start.8 = (f32[4]{0:T(128)S(1)}, f32[4]{0:T(128)}, u32[]{:S(2)}) copy-start(f32[4]{0:T(128)} %slope_ref.1) | copy-start | bytes 52
  36.1 6.8 %collective-permute-start.12 = (bf16[144,384]{1,0:T(8,128)(2,1)S(1)}, bf16[144,384]{1,0:T(8,128)(2,1)S(1)}, u32[]{:S(2)}, u32[]{:S(2)}) collective-permute-start(bf16[144,384]{1,0:T(8,128)(2,1)S(1)} %get-tuple-element.62), channel_id=1, source_target_pairs={{0,24},{8,16},{16,8},{24,0},{1,25},{9,17},{17,9},{25,1},{2,26},{10... | collective-permute-start | bytes 331784 | tf_op jit(solution)/shard_map/ppermute | solution.py:628
  37.8 6.7 %collective-permute-start.13 = (bf16[144,384]{1,0:T(8,128)(2,1)S(1)}, bf16[144,384]{1,0:T(8,128)(2,1)S(1)}, u32[]{:S(2)}, u32[]{:S(2)}) collective-permute-start(bf16[144,384]{1,0:T(8,128)(2,1)S(1)} %get-tuple-element.63), channel_id=1, source_target_pairs={{0,16},{8,24},{16,0},{24,8},{1,17},{9,25},{17,1},{25,9},{2,18},{10... | collective-permute-start | bytes 331784 | tf_op jit(solution)/shard_map/ppermute | solution.py:628
  39.1 5.4 %collective-permute-start.14 = (bf16[144,384]{1,0:T(8,128)(2,1)S(1)}, bf16[144,384]{1,0:T(8,128)(2,1)S(1)}, u32[]{:S(2)}, u32[]{:S(2)}) collective-permute-start(bf16[144,384]{1,0:T(8,128)(2,1)S(1)} %get-tuple-element.64), channel_id=1, source_target_pairs={{0,8},{8,0},{16,24},{24,16},{1,9},{9,1},{17,25},{25,17},{2,10},{10... | collective-permute-start | bytes 331784 | tf_op jit(solution)/shard_map/ppermute | solution.py:628
  44.9 5.8 %collective-permute-start.15 = (bf16[48,384]{1,0:T(8,128)(2,1)S(1)}, bf16[48,384]{1,0:T(8,128)(2,1)S(1)}, u32[]{:S(2)}, u32[]{:S(2)}) collective-permute-start(bf16[48,384]{1,0:T(8,128)(2,1)S(1)} %get-tuple-element.66), channel_id=1, source_target_pairs={{0,6},{2,4},{4,2},{6,0},{1,7},{3,5},{5,3},{7,1},{8,14},{10,12},{12... | collective-permute-start | bytes 110600 | tf_op jit(solution)/shard_map/ppermute | solution.py:628
  46.7 5.0 %collective-permute-start.16 = (bf16[48,384]{1,0:T(8,128)(2,1)S(1)}, bf16[48,384]{1,0:T(8,128)(2,1)S(1)}, u32[]{:S(2)}, u32[]{:S(2)}) collective-permute-start(bf16[48,384]{1,0:T(8,128)(2,1)S(1)} %get-tuple-element.67), channel_id=1, source_target_pairs={{0,4},{2,6},{4,0},{6,2},{1,5},{3,7},{5,1},{7,3},{8,12},{10,14},{12... | collective-permute-start | bytes 110600 | tf_op jit(solution)/shard_map/ppermute | solution.py:628
  47.2 4.5 %collective-permute-start.17 = (bf16[48,384]{1,0:T(8,128)(2,1)S(1)}, bf16[48,384]{1,0:T(8,128)(2,1)S(1)}, u32[]{:S(2)}, u32[]{:S(2)}) collective-permute-start(bf16[48,384]{1,0:T(8,128)(2,1)S(1)} %get-tuple-element.68), channel_id=1, source_target_pairs={{0,2},{2,0},{4,6},{6,4},{1,3},{3,1},{5,7},{7,5},{8,10},{10,8},{12,... | collective-permute-start | bytes 110600 | tf_op jit(solution)/shard_map/ppermute | solution.py:628
